TPU v7x, 32 devices: a whole 2x2x4 slice. The times are simulated.
32 devices in a mesh: dp: 4 (over x, core), expert: 8 (over z, y).
Axes of the slice: x: 2, y: 2, z: 4, core: 2. Of those that a mesh axis runs over, the one named last changes fastest.
Arguments:
- tokens: bfloat16 [4096, 1024], P(('dp', 'expert')), may hold values from -6 to 6
- context: bfloat16 [4096, 1024], P(('dp', 'expert')), may hold values from -6 to 6
- w_out: bfloat16 [1024, 1024], replicated, may hold values from -0.1875 to 0.1875
- w_router: bfloat16 [1024, 8], replicated, may hold values from -0.1875 to 0.1875
- expert_ids: int32 [4096, 2], P(('dp', 'expert')), may hold values from 0 to 7, as said below
- w_in: bfloat16 [8, 1024, 4096], P('expert', None, 'dp'), may hold values from -0.1875 to 0.1875
- w_down: bfloat16 [8, 4096, 1024], P('expert', 'dp'), may hold values from -0.09375 to 0.09375
- cotangent: bfloat16 [4096, 1024], P(('dp', 'expert')), may hold values from -6 to 6
Outputs:
- output: bfloat16 [4096, 1024], P(('dp', 'expert'))
- grad_tokens: bfloat16 [4096, 1024], P(('dp', 'expert'))
- grad_context: bfloat16 [4096, 1024], P(('dp', 'expert'))
- grad_w_out: float32 [1024, 1024], P('expert')
- grad_w_router: float32 [1024, 8], P(None, 'expert')
- grad_w_in: bfloat16 [8, 1024, 4096], P('expert', None, 'dp')
- grad_w_down: bfloat16 [8, 4096, 1024], P('expert', 'dp')
Inputs may be any that keep to these rules, and one draw needn't show every extreme that they name: `expert_ids`: the two experts of a row differ; among the 128 rows of one device every expert is named exactly 32 times.
All inputs are finite; a program needn't handle non-finite values.
Results may differ from a plain program's by a relative error of at most 0.02.
Values may be sent and summed in bfloat16 or wider, within the bound.
No kernel may reach another device: no remote copies, remote signals or barrier semaphores. Data moves between devices by JAX's collectives and lax.ppermute only.
A program may use at most 128 MiB of HBM per device.

v0:
```python
import jax
import jax.numpy as jnp
from jax import lax
from jax.sharding import PartitionSpec as P

GELU_C = 0.7978845608028654
GELU_A = 0.044715
EPSILON = 1e-06


def gelu_pair(preact):
    cubed_in = preact * preact * preact
    tangent = jnp.tanh(GELU_C * (preact + GELU_A * cubed_in))
    gelu_value = 0.5 * preact * (1.0 + tangent)
    derivative = 0.5 * (1.0 + tangent) + 0.5 * preact * (1.0 - tangent * tangent) * GELU_C * (
        1.0 + 3.0 * GELU_A * preact * preact
    )
    return (gelu_value, derivative)


def on_device(tokens, context, w_out, w_router, expert_ids, w_in, w_down, cotangent):
    tok_count, model_width = tokens.shape
    expert_count = lax.axis_size("expert")
    capacity = 2 * tok_count // expert_count
    attn_out = jnp.dot(context, w_out, preferred_element_type=jnp.float32)
    residual = (tokens.astype(jnp.float32) + attn_out).astype(jnp.bfloat16)
    resid_f = residual.astype(jnp.float32)
    inv_rms = lax.rsqrt(jnp.mean(resid_f * resid_f, axis=1, keepdims=True) + EPSILON)
    normed = (resid_f * inv_rms).astype(jnp.bfloat16)
    logits = jnp.dot(normed, w_router, preferred_element_type=jnp.float32)
    picked = jnp.take_along_axis(logits, expert_ids, axis=1)
    gates = jax.nn.sigmoid(picked)
    cot_f = cotangent.astype(jnp.float32)
    flat_ids = expert_ids.reshape(-1)
    onehot_flat = (flat_ids[:, None] == jnp.arange(expert_count, dtype=jnp.int32)[None, :]).astype(
        jnp.int32
    )
    earlier = jnp.cumsum(onehot_flat, axis=0) - onehot_flat
    placed = flat_ids * capacity + jnp.sum(earlier * onehot_flat, axis=1)
    sources = (
        jnp.zeros((2 * tok_count,), jnp.int32)
        .at[placed]
        .set(jnp.arange(2 * tok_count, dtype=jnp.int32))
    )
    source_rows = sources // 2
    send_in = normed[source_rows].reshape(expert_count, capacity, model_width)
    send_grad = (gates.reshape(-1)[sources][:, None] * cot_f[source_rows]).astype(jnp.bfloat16)
    send_grad = send_grad.reshape(expert_count, capacity, model_width)
    weight_in = w_in[0]
    weight_down = w_down[0]
    got_in = lax.all_to_all(send_in, "expert", split_axis=0, concat_axis=0, tiled=True)
    group_in = lax.all_gather(got_in, "dp", axis=0, tiled=True)
    rows_in = group_in.reshape(-1, model_width)
    preact = jnp.dot(rows_in, weight_in, preferred_element_type=jnp.float32)
    gelu_value, derivative = gelu_pair(preact)
    activated = gelu_value.astype(jnp.bfloat16)
    expert_sum = lax.psum_scatter(
        jnp.dot(activated, weight_down, preferred_element_type=jnp.float32),
        "dp",
        scatter_dimension=0,
        tiled=True,
    )
    back_out = lax.all_to_all(
        expert_sum.astype(jnp.bfloat16).reshape(expert_count, capacity, model_width),
        "expert",
        split_axis=0,
        concat_axis=0,
        tiled=True,
    )
    slot_out = back_out.reshape(2 * tok_count, model_width)[placed].reshape(
        tok_count, 2, model_width
    )
    slot_out_f = slot_out.astype(jnp.float32)
    output = (resid_f + jnp.sum(gates[:, :, None] * slot_out_f, axis=1)).astype(jnp.bfloat16)
    got_grad = lax.all_to_all(send_grad, "expert", split_axis=0, concat_axis=0, tiled=True)
    group_grad = lax.all_gather(got_grad, "dp", axis=0, tiled=True)
    rows_grad = group_grad.reshape(-1, model_width)
    act_grad = jnp.dot(rows_grad, weight_down.T, preferred_element_type=jnp.float32)
    pre_grad = (act_grad * derivative).astype(jnp.bfloat16)
    grad_w_down = jnp.dot(activated.T, rows_grad, preferred_element_type=jnp.float32).astype(
        jnp.bfloat16
    )
    grad_w_in = jnp.dot(rows_in.T, pre_grad, preferred_element_type=jnp.float32).astype(
        jnp.bfloat16
    )
    input_sum = lax.psum_scatter(
        jnp.dot(pre_grad, weight_in.T, preferred_element_type=jnp.float32).astype(jnp.bfloat16),
        "dp",
        scatter_dimension=0,
        tiled=True,
    )
    back_grad = lax.all_to_all(
        input_sum.reshape(expert_count, capacity, model_width),
        "expert",
        split_axis=0,
        concat_axis=0,
        tiled=True,
    )
    slot_in_grad = back_grad.reshape(2 * tok_count, model_width)[placed].reshape(
        tok_count, 2, model_width
    )
    gate_grad = jnp.sum(cot_f[:, None, :] * slot_out_f, axis=2)
    logit_grad = gate_grad * gates * (1.0 - gates)
    onehot_ids = (
        expert_ids[:, :, None] == jnp.arange(expert_count, dtype=jnp.int32)[None, None, :]
    ).astype(jnp.float32)
    logit_table = jnp.sum(onehot_ids * logit_grad[:, :, None], axis=1).astype(jnp.bfloat16)
    normed_grad = jnp.sum(slot_in_grad.astype(jnp.float32), axis=1) + jnp.dot(
        logit_table, w_router.T, preferred_element_type=jnp.float32
    )
    mean_term = jnp.mean(normed_grad * resid_f, axis=1, keepdims=True)
    resid_grad = inv_rms * normed_grad - inv_rms * inv_rms * inv_rms * resid_f * mean_term
    grad_tokens = (cot_f + resid_grad).astype(jnp.bfloat16)
    grad_context = jnp.dot(grad_tokens, w_out.T, preferred_element_type=jnp.float32).astype(
        jnp.bfloat16
    )
    local_out = jnp.dot(context.T, grad_tokens, preferred_element_type=jnp.float32)
    local_router = jnp.dot(normed.T, logit_table, preferred_element_type=jnp.float32)
    share_out, share_router = (
        lax.psum_scatter(local_out, "expert", scatter_dimension=0, tiled=True),
        lax.psum_scatter(local_router, "expert", scatter_dimension=1, tiled=True),
    )
    grad_w_out, grad_w_router = (
        lax.psum(share_out.astype(jnp.bfloat16), "dp").astype(jnp.float32),
        lax.psum(share_router.astype(jnp.bfloat16), "dp").astype(jnp.float32),
    )
    return (
        output,
        grad_tokens,
        grad_context,
        grad_w_out,
        grad_w_router,
        grad_w_in.reshape(1, model_width, -1),
        grad_w_down.reshape(1, -1, model_width),
    )


def solution(mesh):
    placed = (
        P(("dp", "expert"), None),
        P(("dp", "expert"), None),
        P(),
        P(),
        P(("dp", "expert"), None),
        P("expert", None, "dp"),
        P("expert", "dp", None),
        P(("dp", "expert"), None),
    )
    return jax.shard_map(
        on_device,
        mesh=mesh,
        in_specs=placed,
        out_specs=(
            P(("dp", "expert"), None),
            P(("dp", "expert"), None),
            P(("dp", "expert"), None),
            P("expert", None),
            P(None, "expert"),
            P("expert", None, "dp"),
            P("expert", "dp", None),
        ),
        check_vma=False,
    )
```

profile of v0, /device:TPU:0, one launch (start us, length us, event | category | flops | bytes accessed | tf_op | source)
XLA Modules:
  0.0 357.1 jit_solution(7279997219072086787)
XLA Ops:
  11.8 2.2 multiply_reduce_fusion.3
  16.0 21.7 %all_to_all.20 = bf16[8,32,1024]{2,1,0:T(8,128)(2,1)} all-to-all(bf16[8,32,1024]{2,1,0:T(8,128)(2,1)S(1)} %bitcast.63), channel_id=1, replica_groups=mesh['dp'=4,'expert'=8] {'expert'}, dimensions={0} | all-to-all | bytes 1048576 | tf_op jit(solution)/shard_map/all_to_all | solution.py:51
  46.0 17.6 %all_to_all.21 = bf16[8,32,1024]{2,1,0:T(8,128)(2,1)} all-to-all(bf16[8,32,1024]{2,1,0:T(8,128)(2,1)S(1)} %multiply_convert_fusion.1), channel_id=1, replica_groups=mesh['dp'=4,'expert'=8] {'expert'}, dimensions={0} | all-to-all | bytes 1048576 | tf_op jit(solution)/shard_map/all_to_all | solution.py:75
  63.9 5.8 %fusion.14 = f32[1024,1024]{1,0:T(8,128)} fusion(bf16[1024,1024]{1,0:T(8,128)(2,1)} %bitcast.68, bf16[1,1024,1024]{2,1,0:T(8,128)(2,1)S(1)} %copy-done), kind=kOutput, calls=%fused_computation.25 | convolution fusion | flops 2147483648 | bytes 8388608 | tf_op jit(solution)/shard_map/dot_general | solution.py:54
  69.8 15.7 %all-gather.5.cloned.1.call-done = bf16[32,32,1024]{2,1,0:T(8,128)(2,1)} async-done(((bf16[8,32,1024]{2,1,0:T(8,128)(2,1)}), bf16[32,32,1024]{2,1,0:T(8,128)(2,1)}) %all-gather.5.cloned.1.call-update) | async-done | bytes 2097168 | tf_op jit(solution)/shard_map/all_gather | solution.py:76
  85.4 7.7 %fusion.8 = bf16[1024,1024]{1,0:T(8,128)(2,1)S(1)} fusion(f32[1024,1024]{1,0:T(8,128)} %fusion.14, bf16[1024,1024]{1,0:T(8,128)(2,1)} %bitcast.70, bf16[1,1024,1024]{2,1,0:T(8,128)(2,1)} %param.14), kind=kOutput, calls=%fused_computation.17 | convolution fusion | flops 2167406592 | bytes 10485760 | tf_op jit(solution)/shard_map/dot_general | solution.py:78
  94.5 3.7 %fusion.16 = bf16[1024,1024]{1,0:T(8,128)(2,1)} fusion(bf16[1024,1024]{1,0:T(8,128)(2,1)S(1)} %fusion.8, bf16[1,1024,1024]{2,1,0:T(8,128)(2,1)S(1)} %copy-done), kind=kOutput, calls=%fused_computation.29 | convolution fusion | flops 2148532224 | bytes 6291456 | tf_op jit(solution)/shard_map/dot_general | solution.py:87
  98.3 7.4 %fusion.10 = f32[1024,1024]{1,0:T(8,128)} fusion(bf16[1,1024,1024]{2,1,0:T(8,128)(2,1)} %param.14, f32[1024,1024]{1,0:T(8,128)} %fusion.14), kind=kOutput, calls=%fused_computation.21 | convolution fusion | flops 2156920832 | bytes 10485760 | tf_op jit(solution)/shard_map/dot_general | solution.py:58
  105.8 24.1 %reduce-scatter.6.cloned.1.call-done = bf16[256,1024]{1,0:T(8,128)(2,1)} async-done(((bf16[1024,1024]{1,0:T(8,128)(2,1)}), bf16[256,1024]{1,0:T(8,128)(2,1)}) %reduce-scatter.6.cloned.1.call-update) | async-done | bytes 524304 | tf_op jit(solution)/shard_map/reduce_scatter | solution.py:86
  129.8 5.5 %all-to-all-start.3 = ((bf16[8,32,1024]{2,1,0:T(8,128)(2,1)}), bf16[8,32,1024]{2,1,0:T(8,128)(2,1)S(1)}, u32[]{:S(2)}, u32[]{:S(2)}) async-start(bf16[8,32,1024]{2,1,0:T(8,128)(2,1)} %bitcast.64), calls=%async_computation.5 | async-start | bytes 1048576 | tf_op jit(solution)/shard_map/all_to_all | solution.py:92
  135.3 41.6 %reduce-scatter.4.cloned.1.call-done = f32[256,1024]{1,0:T(8,128)} async-done(((f32[1024,1024]{1,0:T(8,128)}), f32[256,1024]{1,0:T(8,128)}) %reduce-scatter.4.cloned.1.call-update) | async-done | bytes 1048592 | tf_op jit(solution)/shard_map/reduce_scatter | solution.py:57
  179.0 5.5 %all-to-all-start.1 = ((bf16[8,32,1024]{2,1,0:T(8,128)(2,1)}), bf16[8,32,1024]{2,1,0:T(8,128)(2,1)}, u32[]{:S(2)}, u32[]{:S(2)}) async-start(bf16[8,32,1024]{2,1,0:T(8,128)(2,1)} %bitcast.62), calls=%async_computation.2 | async-start | bytes 1048576 | tf_op jit(solution)/shard_map/all_to_all | solution.py:63
  186.7 2.7 reshape.178
  189.4 3.3 reduce_sum.69
  192.7 6.4 %all-to-all-done.1 = bf16[8,32,1024]{2,1,0:T(8,128)(2,1)} async-done(((bf16[8,32,1024]{2,1,0:T(8,128)(2,1)}), bf16[8,32,1024]{2,1,0:T(8,128)(2,1)}, u32[]{:S(2)}, u32[]{:S(2)}) %all-to-all-start.1) | async-done | bytes 524320 | tf_op jit(solution)/shard_map/all_to_all | solution.py:63
  199.1 3.5 gather_fusion.1
  202.6 2.7 reshape.175
  205.3 3.9 %multiply_reduce_fusion = (f32[128,2]{1,0:T(8,128)S(1)}, f32[128,1024]{1,0:T(8,128)}) fusion(f32[128,2,1024]{2,1,0:T(2,128)} %reshape.175, f32[128,1024]{1,0:T(8,128)S(1)} %convert_element_type.96, f32[128,2]{1,0:T(8,128)S(1)} %copy.59), kind=kLoop, calls=%fused_computation.35 | loop fusion | flops 917248 | bytes 2099200 | tf_op jit(solution)/shard_map/reduce_sum | solution.py:102
  214.1 2.7 convolution_bitcast_fusion
  217.7 6.1 %convert_bitcast_fusion.1 = bf16[1,1024,1024]{2,1,0:T(8,128)(2,1)} fusion(bf16[1024,1024]{1,0:T(8,128)(2,1)} %bitcast.69, bf16[1024,1024]{1,0:T(8,128)(2,1)} %copy-done.14), kind=kOutput, calls=%fused_computation.28 | convolution fusion | flops 2148532224 | bytes 6291456 | tf_op jit(solution)/shard_map/dot_general | solution.py:83
  223.8 4.1 %convert_bitcast_fusion = bf16[1,1024,1024]{2,1,0:T(8,128)(2,1)} fusion(bf16[1024,1024]{1,0:T(8,128)(2,1)S(1)} %bitcast.71, f32[1024,1024]{1,0:T(8,128)S(1)} %copy-done.13), kind=kOutput, calls=%fused_computation.27 | convolution fusion | flops 2157969408 | bytes 8388608 | tf_op jit(solution)/shard_map/dot_general | solution.py:80
  229.4 74.1 %reduce-scatter.8.cloned.1.call-done = f32[128,1024]{0,1:T(8,128)} async-done(((f32[1024,1024]{0,1:T(8,128)}), f32[128,1024]{0,1:T(8,128)}) %reduce-scatter.8.cloned.1.call-update) | async-done | bytes 524304 | tf_op jit(solution)/shard_map/reduce_scatter | solution.py:120
  305.5 35.9 %all-reduce = bf16[1024,8]{0,1:T(8,128)(2,1)S(1)} all-reduce(f32[1024,8]{0,1:T(8,128)S(1)} %fusion.31), channel_id=5, replica_groups=mesh['dp'=4,'expert'=8] {'expert'}, use_global_device_ids=true, to_apply=%region_14.15.clone | all-reduce | flops 8192 | bytes 49152
  342.1 5.7 %psum.15 = bf16[1024,1]{0,1:T(2,128)(2,1)S(1)} all-reduce(bf16[1024,1]{0,1:T(2,128)(2,1)S(1)} %dynamic-slice_convert_fusion), channel_id=1, replica_groups=mesh['dp'=4,'expert'=8] {'dp'}, use_global_device_ids=true, to_apply=%region_15.16 | all-reduce | flops 1024 | bytes 4096 | tf_op jit(solution)/shard_map/psum | solution.py:125
  (96 shorter events, 33.2 us)
Async XLA Ops:
  7.2 56.7 %copy-start = (bf16[1,1024,1024]{2,1,0:T(8,128)(2,1)S(1)}, bf16[1,1024,1024]{2,1,0:T(8,128)(2,1)}, u32[]{:S(2)}) copy-start(bf16[1,1024,1024]{2,1,0:T(8,128)(2,1)} %param.13) | copy-start | bytes 6291460
  7.2 56.7 %all-gather.3.cloned.1.call-start = ((), (), s32[]{:S(2)}) async-start(), calls=%async_computation.7 | async-start | bytes 2621440 | tf_op jit(solution)/shard_map/all_gather | solution.py:52
  14.0 0.8 copy-start.2
  14.0 23.9 %copy-start.8 = (s32[128,2]{0,1:T(2,128)S(1)}, s32[128,2]{0,1:T(2,128)}, u32[]{:S(2)}) copy-start(s32[128,2]{0,1:T(2,128)} %param.12) | copy-start | bytes 3076
  14.0 24.1 %copy-start.5 = (bf16[128,1024]{1,0:T(8,128)(2,1)S(1)}, bf16[128,1024]{1,0:T(8,128)(2,1)}, u32[]{:S(2)}) copy-start(bf16[128,1024]{1,0:T(8,128)(2,1)} %param.15) | copy-start | bytes 786436
  14.0 24.2 %copy-start.7 = (bf16[1024,8]{0,1:T(8,128)(2,1)S(1)}, bf16[1024,8]{0,1:T(8,128)(2,1)}, u32[]{:S(2)}) copy-start(bf16[1024,8]{0,1:T(8,128)(2,1)} %param.11) | copy-start | bytes 49156
  14.5 25.2 %copy-start.10 = (f32[128]{0:T(128)}, f32[128]{0:T(128)S(1)}, u32[]{:S(2)}) copy-start(f32[128]{0:T(128)S(1)} %get-tuple-element.56) | copy-start | bytes 1540
  37.8 47.7 %all-gather.5.cloned.1.call-start = ((), (), s32[]{:S(2)}) async-start(), calls=%async_computation.9 | async-start | bytes 2621440 | tf_op jit(solution)/shard_map/all_gather | solution.py:76
  40.0 0.6 copy-start.9
  63.6 66.2 %reduce-scatter.6.cloned.1.call-start = ((), (), s32[]{:S(2)}) async-start(), calls=%async_computation.10 | async-start | bytes 2621440 | tf_op jit(solution)/shard_map/reduce_scatter | solution.py:86
  93.2 1.4 copy-start.14
  98.2 78.6 %reduce-scatter.4.cloned.1.call-start = ((), (), s32[]{:S(2)}) async-start(), calls=%async_computation.8 | async-start | bytes 5242880 | tf_op jit(solution)/shard_map/reduce_scatter | solution.py:57
  129.8 49.2 %all-to-all-start.3 = ((bf16[8,32,1024]{2,1,0:T(8,128)(2,1)}), bf16[8,32,1024]{2,1,0:T(8,128)(2,1)S(1)}, u32[]{:S(2)}, u32[]{:S(2)}) async-start(bf16[8,32,1024]{2,1,0:T(8,128)(2,1)} %bitcast.64), calls=%async_computation.5 | async-start | bytes 1048576 | tf_op jit(solution)/shard_map/all_to_all | solution.py:92
  179.0 20.1 %all-to-all-start.1 = ((bf16[8,32,1024]{2,1,0:T(8,128)(2,1)}), bf16[8,32,1024]{2,1,0:T(8,128)(2,1)}, u32[]{:S(2)}, u32[]{:S(2)}) async-start(bf16[8,32,1024]{2,1,0:T(8,128)(2,1)} %bitcast.62), calls=%async_computation.2 | async-start | bytes 1048576 | tf_op jit(solution)/shard_map/all_to_all | solution.py:63
  184.5 119.0 %reduce-scatter.8.cloned.1.call-start = ((), (), s32[]{:S(2)}) async-start(), calls=%async_computation.11 | async-start | bytes 4718592 | tf_op jit(solution)/shard_map/reduce_scatter | solution.py:120
  199.1 11.5 %copy-start.3 = (f32[128,1024]{1,0:T(8,128)S(1)}, f32[128,1024]{1,0:T(8,128)}, u32[]{:S(2)}) copy-start(f32[128,1024]{1,0:T(8,128)} %copy-done.2) | copy-start | bytes 1572868
  209.1 4.9 %copy-start.6 = (bf16[128,1024]{1,0:T(8,128)(2,1)S(1)}, bf16[128,1024]{1,0:T(8,128)(2,1)}, u32[]{:S(2)}) copy-start(bf16[128,1024]{1,0:T(8,128)(2,1)} %param.9) | copy-start | bytes 786436
  214.0 13.8 %copy-start.4 = (bf16[128,1024]{1,0:T(8,128)(2,1)}, bf16[128,1024]{1,0:T(8,128)(2,1)S(1)}, u32[]{:S(2)}) copy-start(bf16[128,1024]{1,0:T(8,128)(2,1)S(1)} %get-tuple-element.51) | copy-start | bytes 786436
  214.1 3.1 copy-start.12
  216.8 131.6 %all-reduce.3.cloned.1.call-start = ((), (), s32[]{:S(2)}) async-start(), calls=%async_computation.12 | async-start | bytes 524288 | tf_op jit(solution)/shard_map/psum | solution.py:124
  217.7 6.1 %copy-start.11 = (bf16[32,32,1024]{2,1,0:T(8,128)(2,1)S(1)}, bf16[32,32,1024]{2,1,0:T(8,128)(2,1)}, u32[]{:S(2)}) copy-start(bf16[32,32,1024]{2,1,0:T(8,128)(2,1)} %all-gather.5.cloned.1.call-done) | copy-start | bytes 6291460
  217.7 6.1 %copy-start.13 = (f32[1024,1024]{1,0:T(8,128)S(1)}, f32[1024,1024]{1,0:T(8,128)}, u32[]{:S(2)}) copy-start(f32[1024,1024]{1,0:T(8,128)} %fusion.14) | copy-start | bytes 12582916
  223.8 4.1 %copy-start.1 = (bf16[1024,1024]{1,0:T(8,128)(2,1)S(1)}, bf16[1024,1024]{1,0:T(8,128)(2,1)}, u32[]{:S(2)}) copy-start(bf16[1024,1024]{1,0:T(8,128)(2,1)} %param.10) | copy-start | bytes 6291460
Sparse Core Ops, SparseCore 0:
  37.9 21.5 all-gather.2
  63.8 21.6 all-gather.4
  98.4 31.4 reduce-scatter.5
  132.4 44.4 reduce-scatter.3
  216.9 86.5 reduce-scatter.7
  306.4 31.7 all-reduce.2
where the time goes:
time: 358 us; the launch traced here: 357 us
  waiting for transfers between devices  162 us (45%)
  blocking collectives  80.9 us (23%)
  matrix products  43 us (12%)
  local copies, waits for them, and re-layouts  26.2 us (7%)
  other arithmetic  18.7 us (5%)
  between operations  14.4 us (4%)
  starting transfers between devices  11.9 us (3%)
    reduce_scatter x1, waiting for transfers between devices, on_device(): lax.psum_scatter(local_out, 'expert', scatter_dimension=0, tiled=True)  74.1 us
    reduce_scatter x1, waiting for transfers between devices, on_device(): lax.psum_scatter(jnp.dot(activated, weight_down, preferred_element_type=j...  41.6 us
    unnamed x1, blocking collectives  35.9 us
    reduce_scatter x1, waiting for transfers between devices, on_device(): lax.psum_scatter(jnp.dot(pre_grad, weight_in.T, preferred_element_type=jn...  24.1 us
    all_to_all x1, blocking collectives, on_device(): lax.all_to_all(send_in, 'expert', split_axis=0, concat_axis=0, tiled=True)  21.7 us
    all_to_all x1, blocking collectives, on_device(): lax.all_to_all(send_grad, 'expert', split_axis=0, concat_axis=0, tiled=True)  17.6 us
    all_gather x1, waiting for transfers between devices, on_device(): group_grad = lax.all_gather(got_grad, 'dp', axis=0, tiled=True)  15.7 us
    dot_general x1, matrix products, on_device(): jnp.dot(rows_grad, weight_down.T, preferred_element_type=jnp.float32)  7.71 us
  transfers between devices with their start and end apart: 8, of which 5 were waited for; matrix products, arithmetic and copies ran while one was open for 13% of the time, Pallas kernels for 0%

commit v1 on v0

v1 whole, which is shorter than its diff:
```python
import functools

import jax
import jax.numpy as jnp
from jax import lax
from jax.experimental import pallas as pl
from jax.experimental.pallas import tpu as pltpu
from jax.sharding import PartitionSpec as P

GELU_C = 0.7978845608028654
GELU_A = 0.044715
EPSILON = 1e-06
BF = jnp.bfloat16
F32 = jnp.float32
LANES = 128
VMEM_BYTES = 40 * 1024 * 1024

NN = (((1,), (0,)), ((), ()))
NT = (((1,), (1,)), ((), ()))
TN = (((0,), (0,)), ((), ()))


def mm(a, b, dims=NN):
    return lax.dot_general(a, b, dims, preferred_element_type=F32)


def gelu_pair(preact):
    square = preact * preact
    tangent = jnp.tanh(GELU_C * (preact + GELU_A * (square * preact)))
    half = 0.5 * (1.0 + tangent)
    derivative = half + (0.5 * GELU_C) * preact * (1.0 - tangent * tangent) * (
        1.0 + 3.0 * GELU_A * square
    )
    return preact * half, derivative


def call(body, outs, args, specs=None, out_specs=None, grid=(), scratch=(), flops=0, moved=0, name=None):
    whole = pl.BlockSpec(memory_space=pltpu.VMEM)
    return pl.pallas_call(
        body,
        out_shape=outs,
        grid=grid,
        in_specs=specs if specs is not None else [whole] * len(args),
        out_specs=out_specs if out_specs is not None else [whole] * len(outs),
        scratch_shapes=scratch,
        compiler_params=pltpu.CompilerParams(vmem_limit_bytes=VMEM_BYTES),
        cost_estimate=pl.CostEstimate(flops=flops, bytes_accessed=moved, transcendentals=0),
        name=name,
    )(*args)


def shape(dims, dtype=BF):
    return jax.ShapeDtypeStruct(dims, dtype)


def onehot(column, width):
    lanes = lax.broadcasted_iota(jnp.int32, (column.shape[0], width), 1)
    return (lanes == column).astype(F32)


def place_body(me_ref, ids_ref, cot_ref, placed_ref, send_ref, *, capacity):
    tok = ids_ref.shape[0]
    rows = lax.broadcasted_iota(jnp.int32, (tok, tok), 0)
    cols = lax.broadcasted_iota(jnp.int32, (tok, tok), 1)
    lower = (cols < rows).astype(BF)
    rel = [ids_ref[:, k : k + 1] ^ me_ref[0] for k in range(2)]
    hot = [onehot(r, LANES) for r in rel]
    before = [mm(lower, h.astype(BF)) for h in hot]
    rank_0 = jnp.sum(before[0] * hot[0], axis=1, keepdims=True)
    first = jnp.sum(hot[0], axis=0, keepdims=True)
    rank_1 = jnp.sum((before[1] + first) * hot[1], axis=1, keepdims=True)
    spot = [r * capacity + q.astype(jnp.int32) for r, q in zip(rel, (rank_0, rank_1))]
    for k in range(2):
        placed_ref[:, k : k + 1] = spot[k]
    where = onehot(spot[0], 2 * tok) + onehot(spot[1], 2 * tok)
    send_ref[...] = mm(where.astype(BF), cot_ref[...], TN).astype(BF)


def head_body(me_ref, tok_ref, ctx_ref, w_out_ref, router_ref, ids_ref, placed_ref,
              resid_ref, inv_ref, normed_ref, gates_ref, send_ref):
    tok = ids_ref.shape[0]
    resid = (tok_ref[...].astype(F32) + mm(ctx_ref[...], w_out_ref[...])).astype(BF)
    resid_ref[...] = resid
    resid_f = resid.astype(F32)
    inv = lax.rsqrt(jnp.mean(resid_f * resid_f, axis=1, keepdims=True) + EPSILON)
    inv_ref[...] = inv
    normed = (resid_f * inv).astype(BF)
    normed_ref[...] = normed
    where = onehot(placed_ref[:, 0:1], 2 * tok) + onehot(placed_ref[:, 1:2], 2 * tok)
    send_ref[...] = mm(where.astype(BF), normed, TN).astype(BF)
    logits = mm(normed, router_ref[...])
    for k in range(2):
        picked = jnp.sum(logits * onehot(ids_ref[:, k : k + 1], LANES), axis=1, keepdims=True)
        gates_ref[:, k : k + 1] = jax.nn.sigmoid(picked)


def forward_body(me_ref, *refs, pieces):
    parts, (router_ref, w_in_ref, w_down_ref, rows_ref, act_ref, der_ref, gate_ref, keep_ref, send_ref, total) = (
        refs[:pieces], refs[pieces:])
    step = pl.program_id(0)
    size = parts[0].shape[0]

    @pl.when(step == 0)
    def _():
        for i, part in enumerate(parts):
            rows_ref[pl.ds(i * size, size), :] = part[...]
        logits = mm(rows_ref[...], router_ref[...])
        lanes = lax.broadcasted_iota(jnp.int32, logits.shape, 1)
        picked = jnp.sum(jnp.where(lanes == me_ref[0], logits, 0.0), axis=1, keepdims=True)
        gate_ref[...] = jax.nn.sigmoid(picked)

    value, derivative = gelu_pair(mm(rows_ref[...], w_in_ref[...]))
    act = value.astype(BF)
    act_ref[...] = act
    der_ref[...] = derivative.astype(BF)
    term = mm(act, w_down_ref[...])

    @pl.when(step == 0)
    def _():
        total[...] = term

    @pl.when(step > 0)
    def _():
        total[...] += term

    @pl.when(step == pl.num_programs(0) - 1)
    def _():
        half = keep_ref.shape[0]
        keep_ref[...] = total[:half, :].astype(BF)
        send_ref[...] = total[half:, :].astype(BF)


def backward_body(*refs, pieces):
    parts, (gate_ref, der_ref, w_in_ref, w_down_ref, grads_ref, pre_ref, keep_ref, send_ref, total) = (
        refs[:pieces], refs[pieces:])
    step = pl.program_id(0)
    size = parts[0].shape[0]

    @pl.when(step == 0)
    def _():
        for i, part in enumerate(parts):
            at = pl.ds(i * size, size)
            grads_ref[at, :] = (gate_ref[at, :] * part[...].astype(F32)).astype(BF)

    act_grad = mm(grads_ref[...], w_down_ref[...], NT)
    pre = (act_grad * der_ref[...].astype(F32)).astype(BF)
    pre_ref[...] = pre
    term = mm(pre, w_in_ref[...], NT)

    @pl.when(step == 0)
    def _():
        total[...] = term

    @pl.when(step > 0)
    def _():
        total[...] += term

    @pl.when(step == pl.num_programs(0) - 1)
    def _():
        half = keep_ref.shape[0]
        keep_ref[...] = total[:half, :].astype(BF)
        send_ref[...] = total[half:, :].astype(BF)


def weight_body(left_a, left_b, right_a, right_b, out_ref):
    out_ref[...] = (mm(left_a[...], right_a[...], TN) + mm(left_b[...], right_b[...], TN)).astype(BF)


def combine_body(me_ref, *refs, pieces):
    backs, (ids_ref, placed_ref, gates_ref, resid_ref, cot_ref, normed_ref, out_ref, table_ref, router_ref, slots) = (
        refs[:pieces], refs[pieces:])
    size = backs[0].shape[0]
    for i, back in enumerate(backs):
        slots[pl.ds(i * size, size), :] = back[...]
    held = slots[...]
    cot_f = cot_ref[...].astype(F32)
    total = resid_ref[...].astype(F32)
    table = jnp.zeros((cot_f.shape[0], LANES), F32)
    table_rel = jnp.zeros((cot_f.shape[0], LANES), F32)
    for k in range(2):
        gate = gates_ref[:, k : k + 1]
        mine = mm(onehot(placed_ref[:, k : k + 1], held.shape[0]).astype(BF), held)
        total = total + gate * mine
        logit = jnp.sum(cot_f * mine, axis=1, keepdims=True) * gate * (1.0 - gate)
        ids = ids_ref[:, k : k + 1]
        table = table + onehot(ids, LANES) * logit
        table_rel = table_rel + onehot(ids ^ me_ref[0], LANES) * logit
    out_ref[...] = total.astype(BF)
    table_ref[...] = table.astype(BF)
    router_ref[...] = mm(table_rel.astype(BF), normed_ref[...], TN)


def tail_body(cols_ref, *refs, pieces):
    backs, (placed_ref, table_ref, router_t_ref, resid_ref, inv_ref, cot_ref, w_out_ref, ctx_t_ref,
            grad_ref, grad_ctx_ref, keep_ref, send_ref, slots) = (refs[:pieces], refs[pieces:])
    size = backs[0].shape[0]
    for i, back in enumerate(backs):
        slots[pl.ds(i * size, size), :] = back[...]
    total = slots.shape[0]
    where = onehot(placed_ref[:, 0:1], total) + onehot(placed_ref[:, 1:2], total)
    normed_grad = mm(where.astype(BF), slots[...]) + mm(table_ref[...], router_t_ref[...])
    resid_f = resid_ref[...].astype(F32)
    inv = inv_ref[...]
    mean_term = jnp.mean(normed_grad * resid_f, axis=1, keepdims=True)
    grad = (cot_ref[...].astype(F32) + inv * normed_grad - (inv * inv * inv * mean_term) * resid_f).astype(BF)
    grad_ref[...] = grad
    width = keep_ref.shape[2]
    for m in range(2 * keep_ref.shape[0]):
        part = grad_ref[:, pl.ds(pl.multiple_of(cols_ref[m] * width, LANES), width)]
        held = (send_ref if m % 2 else keep_ref).at[m // 2]
        held[...] = mm(ctx_t_ref[...], part).astype(BF)
    grad_ctx_ref[...] = mm(grad, w_out_ref[...], NT).astype(BF)


def swap(x, axis, mask):
    count = lax.axis_size(axis)
    return lax.ppermute(x, axis, [(i, i ^ mask) for i in range(count)])


def added(*terms):
    return functools.reduce(jnp.add, [t.astype(F32) for t in terms])


class Expert:
    def __init__(self, count, capacity):
        self.high = 4 if count % 4 == 0 else 1
        self.low = count // self.high
        self.capacity = capacity
        self.chunks = [list(range(self.high))[: self.high // 2], list(range(self.high))[self.high // 2 :]]
        self.chunks = [c for c in self.chunks if c]

    def out(self, send):
        size, cap = self.low * self.capacity, self.capacity
        held = [send[k * size : (k + 1) * size] for k in range(self.high)]
        held = [held[0]] + [swap(held[k], "expert", k * self.low) for k in range(1, self.high)]
        groups = []
        for ks in self.chunks:
            rows = [jnp.concatenate([held[k][:cap] for k in ks])]
            for m in range(1, self.low):
                rows.append(swap(jnp.concatenate([held[k][m * cap : (m + 1) * cap] for k in ks]), "expert", m))
            groups.append(jnp.concatenate(rows))
        return groups

    def back(self, groups):
        cap = self.capacity
        blocks = {}
        for ks, rows in zip(self.chunks, groups):
            size = len(ks) * cap
            parts = [rows[:size]] + [swap(rows[m * size : (m + 1) * size], "expert", m) for m in range(1, self.low)]
            for i, k in enumerate(ks):
                block = jnp.concatenate([part[i * cap : (i + 1) * cap] for part in parts])
                blocks[k] = swap(block, "expert", k * self.low) if k else block
        return [blocks[k] for k in range(self.high)]


def on_device(tokens, context, w_out, w_router, expert_ids, w_in, w_down, cotangent):
    tok, width = tokens.shape
    experts = lax.axis_size("expert")
    dp = lax.axis_size("dp")
    far = dp // 2
    capacity = 2 * tok // experts
    slots = 2 * tok
    me = lax.axis_index("expert").astype(jnp.int32)
    mine = lax.axis_index("dp").astype(jnp.int32)
    me_1 = me.reshape(1)
    cols = mine ^ jnp.arange(dp, dtype=jnp.int32)
    weight_in, weight_down = w_in[0], w_down[0]
    hidden = weight_in.shape[1]
    router = jnp.pad(w_router, ((0, 0), (0, LANES - experts)))
    router_t = router.T
    per = width // experts
    ctx_t = jnp.take(context.T.reshape(experts, per, tok), me ^ jnp.arange(experts, dtype=jnp.int32), axis=0)
    ctx_t = ctx_t.reshape(width, tok)
    net = Expert(experts, capacity)
    smem = pl.BlockSpec(memory_space=pltpu.SMEM)
    vmem = pl.BlockSpec(memory_space=pltpu.VMEM)

    placed, cot_send = call(
        functools.partial(place_body, capacity=capacity),
        [shape((tok, 2), jnp.int32), shape((slots, width))],
        (me_1, expert_ids, cotangent), specs=[smem, vmem, vmem], moved=1 << 20, name="place")
    resid, inv, normed, gates, normed_send = call(
        head_body,
        [shape((tok, width)), shape((tok, 1), F32), shape((tok, width)), shape((tok, 2), F32), shape((slots, width))],
        (me_1, tokens, context, w_out, router, expert_ids, placed), specs=[smem] + [vmem] * 6,
        flops=2 * tok * width * width, moved=4 << 20, name="head")

    def spread(send):
        own = net.out(send)
        across = [swap(g, "dp", far) for g in own]
        return own + [swap(g, "dp", 1) for g in own], across + [swap(g, "dp", 1) for g in across]

    rows = spread(normed_send)
    grads = spread(cot_send)
    half = 2 * slots
    block = 256 if hidden % 256 == 0 else hidden
    steps = hidden // block

    def held(dims):
        return pl.BlockSpec(dims, lambda j: (0,) * len(dims))

    in_spec = pl.BlockSpec((width, block), lambda j: (0, j))
    down_spec = pl.BlockSpec((block, width), lambda j: (j, 0))
    hid_spec = pl.BlockSpec((half, block), lambda j: (0, j))

    def forward(parts):
        size = parts[0].shape[0]
        return call(
            functools.partial(forward_body, pieces=len(parts)),
            [shape((half, width)), shape((half, hidden)), shape((half, hidden)), shape((half, 1), F32),
             shape((slots, width)), shape((slots, width))],
            (me_1, *parts, router, weight_in, weight_down),
            specs=[smem] + [held((size, width))] * len(parts) + [held((width, LANES)), in_spec, down_spec],
            out_specs=[held((half, width)), hid_spec, hid_spec, held((half, 1)), held((slots, width)), held((slots, width))],
            grid=(steps,), scratch=[pltpu.VMEM((half, width), F32)],
            flops=4 * half * width * hidden, moved=8 << 20, name="forward")

    def backward(parts, gate, der):
        size = parts[0].shape[0]
        return call(
            functools.partial(backward_body, pieces=len(parts)),
            [shape((half, width)), shape((half, hidden)), shape((slots, width)), shape((slots, width))],
            (*parts, gate, der, weight_in, weight_down),
            specs=[held((size, width))] * len(parts) + [held((half, 1)), hid_spec, in_spec, down_spec],
            out_specs=[held((half, width)), hid_spec, held((slots, width)), held((slots, width))],
            grid=(steps,), scratch=[pltpu.VMEM((half, width), F32)],
            flops=4 * half * width * hidden, moved=8 << 20, name="backward")

    def gather_back(near, away):
        pick = [slice(i * slots // len(net.chunks), (i + 1) * slots // len(net.chunks)) for i in range(len(net.chunks))]
        away_in = swap(away[1], "dp", 1)
        near_in = swap(near[1], "dp", 1)
        crossing = [swap(added(away[0][p], away_in[p]).astype(BF), "dp", far) for p in pick]
        sums = [added(near[0][p], near_in[p], c).astype(BF) for p, c in zip(pick, crossing)]
        return net.back(sums)

    rows_a, act_a, der_a, gate_a, keep_a, send_a = forward(rows[0])
    rows_b, act_b, der_b, gate_b, keep_b, send_b = forward(rows[1])
    back_out = gather_back((keep_a, send_a), (keep_b, send_b))
    grads_a, pre_a, ikeep_a, isend_a = backward(grads[0], gate_a, der_a)
    grads_b, pre_b, ikeep_b, isend_b = backward(grads[1], gate_b, der_b)
    back_in = gather_back((ikeep_a, isend_a), (ikeep_b, isend_b))

    def weight_grad(left_a, left_b, right_a, right_b):
        left, right = left_a.shape[1], right_a.shape[1]
        tile = 256 if left % 256 == 0 else left
        left_spec = pl.BlockSpec((half, tile), lambda i: (0, i))
        return call(
            weight_body, [shape((left, right))], (left_a, left_b, right_a, right_b),
            specs=[left_spec, left_spec, held((half, right)), held((half, right))],
            out_specs=[pl.BlockSpec((tile, right), lambda i: (i, 0))], grid=(left // tile,),
            flops=4 * half * left * right, moved=6 << 20, name="weights")[0]

    grad_w_down = weight_grad(act_a, act_b, grads_a, grads_b)
    grad_w_in = weight_grad(rows_a, rows_b, pre_a, pre_b)

    output, table, local_router = call(
        functools.partial(combine_body, pieces=net.high),
        [shape((tok, width)), shape((tok, LANES)), shape((LANES, width), F32)],
        (me_1, *back_out, expert_ids, placed, gates, resid, cotangent, normed),
        specs=[smem] + [vmem] * (net.high + 6), scratch=[pltpu.VMEM((slots, width), BF)],
        flops=8 * tok * slots * width, moved=2 << 20, name="combine")

    part = width // dp
    grad_tokens, grad_context, keep, send = call(
        functools.partial(tail_body, pieces=net.high),
        [shape((tok, width)), shape((tok, width)), shape((dp // 2, width, part)), shape((dp // 2, width, part))],
        (cols, *back_in, placed, table, router_t, resid, inv, cotangent, w_out, ctx_t),
        specs=[smem] + [vmem] * (net.high + 8), scratch=[pltpu.VMEM((slots, width), BF)],
        flops=6 * tok * width * width, moved=6 << 20, name="tail")

    high, low = net.high, net.low
    summed = added(keep, swap(send, "dp", 1)).astype(BF).reshape(dp // 2, high, low, per, part)
    first, second = summed[:, : high // 2], summed[:, high // 2 :]
    first = added(first[0], swap(first[1], "dp", far)).astype(BF)
    first = added(first[:, 0], *[swap(first[:, m], "expert", m) for m in range(1, low)]).astype(BF)
    second = added(second[:, :, 0], *[swap(second[:, :, m], "expert", m) for m in range(1, low)]).astype(BF)
    second = added(second[0], swap(second[1], "dp", far)).astype(BF)
    blocks = [first[k] for k in range(high // 2)] + [second[k] for k in range(high - high // 2)]
    own = added(blocks[0], *[swap(blocks[k], "expert", k * low) for k in range(1, high)]).astype(BF)
    pair = jnp.stack([own, swap(own, "dp", far)])
    other = swap(pair, "dp", 1)
    quarters = jnp.stack([pair, other], axis=1).reshape(dp, per, part)
    grad_w_out = jnp.take(quarters, cols, axis=0).transpose(1, 0, 2).reshape(per, width).astype(F32)

    table_sum = local_router[:experts]
    table_sum = table_sum + swap(table_sum, "dp", 1)
    table_sum = table_sum + swap(table_sum, "dp", far)
    table_sum = table_sum.reshape(high, low, width)
    table_sum = added(table_sum[:, 0], *[swap(table_sum[:, m], "expert", m) for m in range(1, low)])
    table_sum = added(table_sum[0], *[swap(table_sum[k], "expert", k * low) for k in range(1, high)])
    grad_w_router = table_sum.reshape(width, 1)

    return (
        output,
        grad_tokens,
        grad_context,
        grad_w_out,
        grad_w_router,
        grad_w_in.reshape(1, width, hidden),
        grad_w_down.reshape(1, hidden, width),
    )


def solution(mesh):
    split = P(("dp", "expert"), None)
    return jax.shard_map(
        on_device,
        mesh=mesh,
        in_specs=(split, split, P(), P(), split, P("expert", None, "dp"), P("expert", "dp", None), split),
        out_specs=(split, split, split, P("expert", None), P(None, "expert"), P("expert", None, "dp"),
                   P("expert", "dp", None)),
        check_vma=False,
    )
```

time: 358 us -> 203 us (0.57)
  waiting for transfers between devices: 162 us -> 72.2 us
  blocking collectives: 80.9 us -> 0 us
  Pallas kernels: 0 us -> 46.1 us
  starting transfers between devices: 11.9 us -> 55.9 us
  matrix products: 43 us -> 0 us
  other arithmetic: 18.7 us -> 4.89 us
  between operations: 14.4 us -> 1.34 us
  local copies, waits for them, and re-layouts: 26.2 us -> 22.4 us
    reduce_scatter x3 -> x0, waiting for transfers between devices: 140 us -> none  [the longest x1 74.1 us: on_device(): lax.psum_scatter(local_out, 'expert', scatter_dimension=0, tiled=True)]
    ppermute x0 -> x56, waiting for transfers between devices: none -> 72.2 us  [swap(): return lax.ppermute(x, axis, [(i, i ^ mask) for i in range(count)])]
    ppermute x0 -> x56, starting transfers between devices: none -> 55.9 us  [swap(): return lax.ppermute(x, axis, [(i, i ^ mask) for i in range(count)])]
    pallas_call x0 -> x10, Pallas kernels: none -> 46.1 us  [call(): pl.pallas_call(body, out_shape=outs, grid=grid, in_specs=specs if specs i...]
    dot_general x12 -> x0, matrix products: 43 us -> none  [the longest x1 7.71 us: on_device(): jnp.dot(rows_grad, weight_down.T, preferred_element_type=jnp.float32)]
    all_to_all x2 -> x0, blocking collectives: 39.3 us -> none  [the longest x1 21.7 us: on_device(): lax.all_to_all(send_in, 'expert', split_axis=0, concat_axis=0, tiled=True)]
    unnamed x1 -> x0, blocking collectives: 35.9 us -> none
    all_gather x2 -> x0, waiting for transfers between devices: 15.7 us -> none  [the longest x1 15.7 us: on_device(): group_grad = lax.all_gather(got_grad, 'dp', axis=0, tiled=True)]
  transfers between devices with their start and end apart: 8 -> 56, of which waited for: 5 -> 20; matrix products, arithmetic and copies ran while one was open for 13% -> 2% of each run, Pallas kernels for 0% -> 20%
where the time goes in v1:
time: 203 us
  waiting for transfers between devices  72.2 us (36%)
  starting transfers between devices  55.9 us (28%)
  Pallas kernels  46.1 us (23%)
  local copies, waits for them, and re-layouts  22.4 us (11%)
  other arithmetic  4.89 us (2%)
    ppermute x56, waiting for transfers between devices, swap(): return lax.ppermute(x, axis, [(i, i ^ mask) for i in range(count)])  72.2 us
    ppermute x56, starting transfers between devices, swap(): return lax.ppermute(x, axis, [(i, i ^ mask) for i in range(count)])  55.9 us
    pallas_call x10, Pallas kernels, call(): pl.pallas_call(body, out_shape=outs, grid=grid, in_specs=specs if specs i...  46.1 us
    unnamed x51, local copies, waits for them, and re-layouts  20.3 us
  transfers between devices with their start and end apart: 56, of which 20 were waited for; matrix products, arithmetic and copies ran while one was open for 2% of the time, Pallas kernels for 20%

profile of v1, /device:TPU:0, one launch (start us, length us, event | category | flops | bytes accessed | tf_op | source)
XLA Modules:
  0.0 202.8 jit_solution(4806978095331118705)
XLA Ops:
  8.6 3.1 %collective-permute-start = (bf16[64,1024]{1,0:T(8,128)(2,1)S(1)}, bf16[64,1024]{1,0:T(8,128)(2,1)S(1)}, u32[]{:S(2)}, u32[]{:S(2)}) collective-permute-start(bf16[64,1024]{1,0:T(8,128)(2,1)S(1)} %get-tuple-element.99), channel_id=1, source_target_pairs={{0,2},{1,3},{2,0},{3,1},{4,6},{5,7},{6,4},{7,5},{8,10},{9,11},{10,... | collective-permute-start | bytes 393224 | tf_op jit(solution)/shard_map/ppermute | solution.py:217
  11.7 2.5 %collective-permute-start.3 = (bf16[64,1024]{1,0:T(8,128)(2,1)S(1)}, bf16[64,1024]{1,0:T(8,128)(2,1)S(1)}, u32[]{:S(2)}, u32[]{:S(2)}) collective-permute-start(bf16[64,1024]{1,0:T(8,128)(2,1)S(1)} %get-tuple-element.98), channel_id=1, source_target_pairs={{0,6},{1,7},{2,4},{3,5},{4,2},{5,3},{6,0},{7,1},{8,14},{9,15},{10,... | collective-permute-start | bytes 393224 | tf_op jit(solution)/shard_map/ppermute | solution.py:217
  23.0 9.5 %collective-permute-done.2 = bf16[64,1024]{1,0:T(8,128)(2,1)S(1)} collective-permute-done((bf16[64,1024]{1,0:T(8,128)(2,1)S(1)}, bf16[64,1024]{1,0:T(8,128)(2,1)S(1)}, u32[]{:S(2)}, u32[]{:S(2)}) %collective-permute-start.2) | collective-permute-done | bytes 131104 | tf_op jit(solution)/shard_map/ppermute | solution.py:217
  34.7 2.5 %collective-permute-done.22 = bf16[64,1024]{1,0:T(8,128)(2,1)S(1)} collective-permute-done((bf16[64,1024]{1,0:T(8,128)(2,1)S(1)}, bf16[64,1024]{1,0:T(8,128)(2,1)S(1)}, u32[]{:S(2)}, u32[]{:S(2)}) %collective-permute-start.22) | collective-permute-done | bytes 131104 | tf_op jit(solution)/shard_map/ppermute | solution.py:217
  43.8 4.3 %collective-permute-done.8.refs_0_ = bf16[128,1024]{1,0:T(8,128)(2,1)S(1)} collective-permute-done((bf16[128,1024]{1,0:T(8,128)(2,1)S(1)}, bf16[128,1024]{1,0:T(8,128)(2,1)S(1)}, u32[]{:S(2)}, u32[]{:S(2)}) %collective-permute-start.8) | collective-permute-done | bytes 262176 | tf_op jit(solution)/shard_map/ppermute | solution.py:217
  48.1 5.6 %collective-permute-done.9.refs_1_ = bf16[128,1024]{1,0:T(8,128)(2,1)S(1)} collective-permute-done((bf16[128,1024]{1,0:T(8,128)(2,1)S(1)}, bf16[128,1024]{1,0:T(8,128)(2,1)S(1)}, u32[]{:S(2)}, u32[]{:S(2)}) %collective-permute-start.9) | collective-permute-done | bytes 262176 | tf_op jit(solution)/shard_map/ppermute | solution.py:217
  54.7 4.6 %collective-permute-done.28.refs_0_ = bf16[128,1024]{1,0:T(8,128)(2,1)S(1)} collective-permute-done((bf16[128,1024]{1,0:T(8,128)(2,1)S(1)}, bf16[128,1024]{1,0:T(8,128)(2,1)S(1)}, u32[]{:S(2)}, u32[]{:S(2)}) %collective-permute-start.28) | collective-permute-done | bytes 262176 | tf_op jit(solution)/shard_map/ppermute | solution.py:217
  59.3 3.6 %collective-permute-done.29.refs_1_ = bf16[128,1024]{1,0:T(8,128)(2,1)} collective-permute-done((bf16[128,1024]{1,0:T(8,128)(2,1)S(1)}, bf16[128,1024]{1,0:T(8,128)(2,1)}, u32[]{:S(2)}, u32[]{:S(2)}) %collective-permute-start.29) | collective-permute-done | bytes 262176 | tf_op jit(solution)/shard_map/ppermute | solution.py:217
  67.1 9.4 %forward.3 = (bf16[512,1024]{1,0:T(8,128)(2,1)S(1)}, bf16[512,1024]{1,0:T(8,128)(2,1)S(1)}, bf16[512,1024]{1,0:T(8,128)(2,1)S(1)}, f32[512,1]{1,0:T(8,128)S(1)},...) custom-call(s32[1]{0:T(128)} %bitcast.me_ref, bf16[128,1024]{1,0:T(8,128)(2,1)S(1)} %collective-permute-done.8.refs_0_, ...), custom_call_target="tpu_custom_call" | custom-call | flops 2147483648 | bytes 8388608 | tf_op jit(solution)/shard_map/forward/pallas_call | solution.py:39
  87.1 7.8 %backward.3 = (bf16[512,1024]{1,0:T(8,128)(2,1)S(1)}, bf16[512,1024]{1,0:T(8,128)(2,1)S(1)}, bf16[256,1024]{1,0:T(8,128)(2,1)S(1)}, bf16[256,1024]{1,0:T(8,128)(2,1)S(1)}) custom-call(bf16[128,1024]{1,0:T(8,128)(2,1)S(1)} %collective-permute-done.28.refs_0_, bf16[128,1024]{1,0:T(8,128)(2,1)} %collective-permute-done.29.refs_1_, ...), custom_call_target="tpu_custom_call" | custom-call | flops 2147483648 | bytes 8388608 | tf_op jit(solution)/shard_map/backward/pallas_call | solution.py:39
  95.1 7.6 %forward.2 = (bf16[512,1024]{1,0:T(8,128)(2,1)S(1)}, bf16[512,1024]{1,0:T(8,128)(2,1)S(1)}, bf16[512,1024]{1,0:T(8,128)(2,1)S(1)}, f32[512,1]{1,0:T(8,128)S(1)},...) custom-call(s32[1]{0:T(128)} %bitcast.me_ref, bf16[128,1024]{1,0:T(8,128)(2,1)S(1)} %pad_maximum_fusion.refs_0_, ...), custom_call_target="tpu_custom_call" | custom-call | flops 2147483648 | bytes 8388608 | tf_op jit(solution)/shard_map/forward/pallas_call | solution.py:39
  106.5 6.9 %backward.2 = (bf16[512,1024]{1,0:T(8,128)(2,1)S(1)}, bf16[512,1024]{1,0:T(8,128)(2,1)S(1)}, bf16[256,1024]{1,0:T(8,128)(2,1)S(1)}, bf16[256,1024]{1,0:T(8,128)(2,1)S(1)}) custom-call(bf16[128,1024]{1,0:T(8,128)(2,1)S(1)} %pad_maximum_fusion.2.refs_0_, bf16[128,1024]{1,0:T(8,128)(2,1)S(1)} %pad_maximum_fusion.3.refs_1_, ...), custom_call_target="tpu_custom_call" | custom-call | flops 2147483648 | bytes 8388608 | tf_op jit(solution)/shard_map/backward/pallas_call | solution.py:39
  115.8 3.5 %collective-permute-done.13 = bf16[128,1024]{1,0:T(8,128)(2,1)S(1)} collective-permute-done((bf16[128,1024]{1,0:T(8,128)(2,1)S(1)}, bf16[128,1024]{1,0:T(8,128)(2,1)S(1)}, u32[]{:S(2)}, u32[]{:S(2)}) %collective-permute-start.13) | collective-permute-done | bytes 262176 | tf_op jit(solution)/shard_map/ppermute | solution.py:217
  121.8 3.1 %collective-permute-done.36 = bf16[128,1024]{1,0:T(8,128)(2,1)S(1)} collective-permute-done((bf16[128,1024]{1,0:T(8,128)(2,1)S(1)}, bf16[128,1024]{1,0:T(8,128)(2,1)S(1)}, u32[]{:S(2)}, u32[]{:S(2)}) %collective-permute-start.36) | collective-permute-done | bytes 262176 | tf_op jit(solution)/shard_map/ppermute | solution.py:217
  124.9 4.8 %collective-permute-done.33 = bf16[128,1024]{1,0:T(8,128)(2,1)S(1)} collective-permute-done((bf16[128,1024]{1,0:T(8,128)(2,1)S(1)}, bf16[128,1024]{1,0:T(8,128)(2,1)S(1)}, u32[]{:S(2)}, u32[]{:S(2)}) %collective-permute-start.33) | collective-permute-done | bytes 262176 | tf_op jit(solution)/shard_map/ppermute | solution.py:217
  132.4 3.0 %collective-permute-start.18 = (bf16[64,1024]{1,0:T(8,128)(2,1)S(1)}, bf16[64,1024]{1,0:T(8,128)(2,1)S(1)}, u32[]{:S(2)}, u32[]{:S(2)}) collective-permute-start(bf16[64,1024]{1,0:T(8,128)(2,1)S(1)} %pad_maximum_fusion.9), channel_id=1, source_target_pairs={{0,4},{1,5},{2,6},{3,7},{4,0},{5,1},{6,2},{7,3},{8,12},{9,13},{10,... | collective-permute-start | bytes 393224 | tf_op jit(solution)/shard_map/ppermute | solution.py:217
  141.6 3.9 %collective-permute-done.18.refs_2_ = bf16[64,1024]{1,0:T(8,128)(2,1)S(1)} collective-permute-done((bf16[64,1024]{1,0:T(8,128)(2,1)S(1)}, bf16[64,1024]{1,0:T(8,128)(2,1)S(1)}, u32[]{:S(2)}, u32[]{:S(2)}) %collective-permute-start.18) | collective-permute-done | bytes 131104 | tf_op jit(solution)/shard_map/ppermute | solution.py:217
  146.9 8.8 %collective-permute-done.38.refs_2_ = bf16[64,1024]{1,0:T(8,128)(2,1)S(1)} collective-permute-done((bf16[64,1024]{1,0:T(8,128)(2,1)S(1)}, bf16[64,1024]{1,0:T(8,128)(2,1)S(1)}, u32[]{:S(2)}, u32[]{:S(2)}) %collective-permute-start.38) | collective-permute-done | bytes 131104 | tf_op jit(solution)/shard_map/ppermute | solution.py:217
  155.7 3.1 %tail.1 = (bf16[128,1024]{1,0:T(8,128)(2,1)}, bf16[128,1024]{1,0:T(8,128)(2,1)}, bf16[2,1024,256]{2,1,0:T(8,128)(2,1)S(1)}, bf16[2,1024,256]{2,1,0:T(8,128)(2,1)S(1)}) custom-call(s32[4]{0:T(128)S(1)} %iota_xor_fusion.cols_ref, bf16[64,1024]{1,0:T(8,128)(2,1)S(1)} %pad_maximum_fusion.13.refs_0_, bf16[64,1024]{1,0:T(8,128)(2,1)S(1)} %collective-permute-done.35.refs_1_, ...), custom_call_target="tpu_custom_call" | custom-call | flops 805306368 | bytes 6291456 | tf_op jit(solution)/shard_map/tail/pallas_call | solution.py:39
  159.4 4.1 %weights.2 = bf16[1024,1024]{1,0:T(8,128)(2,1)} custom-call(bf16[512,1024]{1,0:T(8,128)(2,1)S(1)} %get-tuple-element.67.left_a, bf16[512,1024]{1,0:T(8,128)(2,1)S(1)} %copy-done.19, bf16[512,1024]{1,0:T(8,128)(2,1)S(1)} %get-tuple-element.69.right_a, bf16[512,1024]{1,0:T(8,128)(2,1)S(1)} %get-tuple-element.70.right_b), custom_call_target="tpu_custom_call" | custom-call | flops 2147483648 | bytes 6291456 | tf_op jit(solution)/shard_map/weights/pallas_call | solution.py:39
  165.1 4.1 %weights.3 = bf16[1024,1024]{1,0:T(8,128)(2,1)} custom-call(bf16[512,1024]{1,0:T(8,128)(2,1)S(1)} %get-tuple-element.71.left_a, bf16[512,1024]{1,0:T(8,128)(2,1)S(1)} %copy-done.17, bf16[512,1024]{1,0:T(8,128)(2,1)S(1)} %get-tuple-element.73.right_a, bf16[512,1024]{1,0:T(8,128)(2,1)S(1)} %get-tuple-element.74.right_b), custom_call_target="tpu_custom_call" | custom-call | flops 2147483648 | bytes 6291456 | tf_op jit(solution)/shard_map/weights/pallas_call | solution.py:39
  173.6 5.3 %collective-permute-done.44 = bf16[2,2,128,256]{3,2,1,0:T(8,128)(2,1)S(1)} collective-permute-done((bf16[2,2,128,256]{3,2,1,0:T(8,128)(2,1)S(1)}, bf16[2,2,128,256]{3,2,1,0:T(8,128)(2,1)S(1)}, u32[]{:S(2)}, u32[]{:S(2)}) %collective-permute-start.44) | collective-permute-done | bytes 262176 | tf_op jit(solution)/shard_map/ppermute | solution.py:217
  181.2 2.9 %collective-permute-done.45 = bf16[2,128,256]{2,1,0:T(8,128)(2,1)S(1)} collective-permute-done((bf16[2,128,256]{2,1,0:T(8,128)(2,1)S(1)}, bf16[2,128,256]{2,1,0:T(8,128)(2,1)S(1)}, u32[]{:S(2)}, u32[]{:S(2)}) %collective-permute-start.45) | collective-permute-done | bytes 131104 | tf_op jit(solution)/shard_map/ppermute | solution.py:217
  193.1 2.6 %collective-permute-start.55 = (f32[1024]{0:T(1024)S(1)}, f32[1024]{0:T(1024)S(1)}, u32[]{:S(2)}, u32[]{:S(2)}) collective-permute-start(f32[1024]{0:T(1024)S(1)} %bitcast.109), channel_id=1, source_target_pairs={{0,6},{1,7},{2,4},{3,5},{4,2},{5,3},{6,0},{7,1},{8,14},{9,15},{10,... | collective-permute-start | bytes 12296 | tf_op jit(solution)/shard_map/ppermute | solution.py:217
  (227 shorter events, 85.0 us)
Async XLA Ops:
  14.2 18.3 %collective-permute-start.2 = (bf16[64,1024]{1,0:T(8,128)(2,1)S(1)}, bf16[64,1024]{1,0:T(8,128)(2,1)S(1)}, u32[]{:S(2)}, u32[]{:S(2)}) collective-permute-start(bf16[64,1024]{1,0:T(8,128)(2,1)S(1)} %get-tuple-element.97), channel_id=1, source_target_pairs={{0,4},{1,5},{2,6},{3,7},{4,0},{5,1},{6,2},{7,3},{8,12},{9,13},{10,... | collective-permute-start | bytes 393224 | tf_op jit(solution)/shard_map/ppermute | solution.py:217
  14.3 19.7 %collective-permute-start.20 = (bf16[64,1024]{1,0:T(8,128)(2,1)S(1)}, bf16[64,1024]{1,0:T(8,128)(2,1)S(1)}, u32[]{:S(2)}, u32[]{:S(2)}) collective-permute-start(bf16[64,1024]{1,0:T(8,128)(2,1)S(1)} %get-tuple-element.94), channel_id=1, source_target_pairs={{0,2},{1,3},{2,0},{3,1},{4,6},{5,7},{6,4},{7,5},{8,10},{9,11},{10,... | collective-permute-start | bytes 393224 | tf_op jit(solution)/shard_map/ppermute | solution.py:217
  16.2 18.5 %collective-permute-start.23 = (bf16[64,1024]{1,0:T(8,128)(2,1)S(1)}, bf16[64,1024]{1,0:T(8,128)(2,1)S(1)}, u32[]{:S(2)}, u32[]{:S(2)}) collective-permute-start(bf16[64,1024]{1,0:T(8,128)(2,1)S(1)} %get-tuple-element.93), channel_id=1, source_target_pairs={{0,6},{1,7},{2,4},{3,5},{4,2},{5,3},{6,0},{7,1},{8,14},{9,15},{10,... | collective-permute-start | bytes 393224 | tf_op jit(solution)/shard_map/ppermute | solution.py:217
  18.8 18.4 %collective-permute-start.22 = (bf16[64,1024]{1,0:T(8,128)(2,1)S(1)}, bf16[64,1024]{1,0:T(8,128)(2,1)S(1)}, u32[]{:S(2)}, u32[]{:S(2)}) collective-permute-start(bf16[64,1024]{1,0:T(8,128)(2,1)S(1)} %get-tuple-element.92), channel_id=1, source_target_pairs={{0,4},{1,5},{2,6},{3,7},{4,0},{5,1},{6,2},{7,3},{8,12},{9,13},{10,... | collective-permute-start | bytes 393224 | tf_op jit(solution)/shard_map/ppermute | solution.py:217
  21.4 17.3 %collective-permute-start.1 = (bf16[64,1024]{1,0:T(8,128)(2,1)S(1)}, bf16[64,1024]{1,0:T(8,128)(2,1)S(1)}, u32[]{:S(2)}, u32[]{:S(2)}) collective-permute-start(bf16[64,1024]{1,0:T(8,128)(2,1)S(1)} %pad_maximum_fusion.5), channel_id=1, source_target_pairs={{0,1},{1,0},{2,3},{3,2},{4,5},{5,4},{6,7},{7,6},{8,9},{9,8},{10,11... | collective-permute-start | bytes 393224 | tf_op jit(solution)/shard_map/ppermute | solution.py:217
  40.4 13.3 %collective-permute-start.9 = (bf16[128,1024]{1,0:T(8,128)(2,1)S(1)}, bf16[128,1024]{1,0:T(8,128)(2,1)S(1)}, u32[]{:S(2)}, u32[]{:S(2)}) collective-permute-start(bf16[128,1024]{1,0:T(8,128)(2,1)S(1)} %pad_maximum_fusion.1.refs_1_), channel_id=1, source_target_pairs={{0,16},{8,24},{16,0},{24,8},{1,17},{9,25},{17,1},{25,9},{2,18},{10... | collective-permute-start | bytes 786440 | tf_op jit(solution)/shard_map/ppermute | solution.py:217
  41.0 18.3 %collective-permute-start.28 = (bf16[128,1024]{1,0:T(8,128)(2,1)S(1)}, bf16[128,1024]{1,0:T(8,128)(2,1)S(1)}, u32[]{:S(2)}, u32[]{:S(2)}) collective-permute-start(bf16[128,1024]{1,0:T(8,128)(2,1)S(1)} %pad_maximum_fusion.2.refs_0_), channel_id=1, source_target_pairs={{0,16},{8,24},{16,0},{24,8},{1,17},{9,25},{17,1},{25,9},{2,18},{10... | collective-permute-start | bytes 786440 | tf_op jit(solution)/shard_map/ppermute | solution.py:217
  42.6 20.4 %collective-permute-start.29 = (bf16[128,1024]{1,0:T(8,128)(2,1)S(1)}, bf16[128,1024]{1,0:T(8,128)(2,1)}, u32[]{:S(2)}, u32[]{:S(2)}) collective-permute-start(bf16[128,1024]{1,0:T(8,128)(2,1)S(1)} %pad_maximum_fusion.3.refs_1_), channel_id=1, source_target_pairs={{0,16},{8,24},{16,0},{24,8},{1,17},{9,25},{17,1},{25,9},{2,18},{10... | collective-permute-start | bytes 786440 | tf_op jit(solution)/shard_map/ppermute | solution.py:217
  48.1 14.9 %collective-permute-start.10 = (bf16[128,1024]{1,0:T(8,128)(2,1)S(1)}, bf16[128,1024]{1,0:T(8,128)(2,1)}, u32[]{:S(2)}, u32[]{:S(2)}) collective-permute-start(bf16[128,1024]{1,0:T(8,128)(2,1)S(1)} %collective-permute-done.8.refs_0_), channel_id=1, source_target_pairs={{0,8},{8,0},{16,24},{24,16},{1,9},{9,1},{17,25},{25,17},{2,10},{10... | collective-permute-start | bytes 786440 | tf_op jit(solution)/shard_map/ppermute | solution.py:217
  59.3 21.9 %collective-permute-start.30 = (bf16[128,1024]{1,0:T(8,128)(2,1)S(1)}, bf16[128,1024]{1,0:T(8,128)(2,1)}, u32[]{:S(2)}, u32[]{:S(2)}) collective-permute-start(bf16[128,1024]{1,0:T(8,128)(2,1)S(1)} %collective-permute-done.28.refs_0_), channel_id=1, source_target_pairs={{0,8},{8,0},{16,24},{24,16},{1,9},{9,1},{17,25},{25,17},{2,10},{10... | collective-permute-start | bytes 786440 | tf_op jit(solution)/shard_map/ppermute | solution.py:217
  63.0 18.4 %collective-permute-start.31 = (bf16[128,1024]{1,0:T(8,128)(2,1)}, bf16[128,1024]{1,0:T(8,128)(2,1)}, u32[]{:S(2)}, u32[]{:S(2)}) collective-permute-start(bf16[128,1024]{1,0:T(8,128)(2,1)} %collective-permute-done.29.refs_1_), channel_id=1, source_target_pairs={{0,8},{8,0},{16,24},{24,16},{1,9},{9,1},{17,25},{25,17},{2,10},{10... | collective-permute-start | bytes 786440 | tf_op jit(solution)/shard_map/ppermute | solution.py:217
  80.1 23.1 %collective-permute-start.12 = (bf16[256,1024]{1,0:T(8,128)(2,1)}, bf16[256,1024]{1,0:T(8,128)(2,1)}, u32[]{:S(2)}, u32[]{:S(2)}) collective-permute-start(bf16[256,1024]{1,0:T(8,128)(2,1)} %get-tuple-element.46), channel_id=1, source_target_pairs={{0,8},{8,0},{16,24},{24,16},{1,9},{9,1},{17,25},{25,17},{2,10},{10... | collective-permute-start | bytes 1572872 | tf_op jit(solution)/shard_map/ppermute | solution.py:217
  80.6 14.3 %collective-permute-start.5 = (bf16[128,1024]{1,0:T(8,128)(2,1)S(1)}, bf16[128,1024]{1,0:T(8,128)(2,1)S(1)}, u32[]{:S(2)}, u32[]{:S(2)}) collective-permute-start(bf16[128,1024]{1,0:T(8,128)(2,1)S(1)} %pad_maximum_fusion.refs_0_), channel_id=1, source_target_pairs={{0,8},{8,0},{16,24},{24,16},{1,9},{9,1},{17,25},{25,17},{2,10},{10... | collective-permute-start | bytes 786440 | tf_op jit(solution)/shard_map/ppermute | solution.py:217
  80.7 14.4 %collective-permute-start.6 = (bf16[128,1024]{1,0:T(8,128)(2,1)S(1)}, bf16[128,1024]{1,0:T(8,128)(2,1)S(1)}, u32[]{:S(2)}, u32[]{:S(2)}) collective-permute-start(bf16[128,1024]{1,0:T(8,128)(2,1)S(1)} %pad_maximum_fusion.1.refs_1_), channel_id=1, source_target_pairs={{0,8},{8,0},{16,24},{24,16},{1,9},{9,1},{17,25},{25,17},{2,10},{10... | collective-permute-start | bytes 786440 | tf_op jit(solution)/shard_map/ppermute | solution.py:217
  81.2 24.8 %collective-permute-start.25 = (bf16[128,1024]{1,0:T(8,128)(2,1)S(1)}, bf16[128,1024]{1,0:T(8,128)(2,1)S(1)}, u32[]{:S(2)}, u32[]{:S(2)}) collective-permute-start(bf16[128,1024]{1,0:T(8,128)(2,1)S(1)} %pad_maximum_fusion.2.refs_0_), channel_id=1, source_target_pairs={{0,8},{8,0},{16,24},{24,16},{1,9},{9,1},{17,25},{25,17},{2,10},{10... | collective-permute-start | bytes 786440 | tf_op jit(solution)/shard_map/ppermute | solution.py:217
  81.3 25.2 %collective-permute-start.26 = (bf16[128,1024]{1,0:T(8,128)(2,1)S(1)}, bf16[128,1024]{1,0:T(8,128)(2,1)S(1)}, u32[]{:S(2)}, u32[]{:S(2)}) collective-permute-start(bf16[128,1024]{1,0:T(8,128)(2,1)S(1)} %pad_maximum_fusion.3.refs_1_), channel_id=1, source_target_pairs={{0,8},{8,0},{16,24},{24,16},{1,9},{9,1},{17,25},{25,17},{2,10},{10... | collective-permute-start | bytes 786440 | tf_op jit(solution)/shard_map/ppermute | solution.py:217
  95.0 18.5 %collective-permute-start.32 = (bf16[256,1024]{1,0:T(8,128)(2,1)S(1)}, bf16[256,1024]{1,0:T(8,128)(2,1)S(1)}, u32[]{:S(2)}, u32[]{:S(2)}) collective-permute-start(bf16[256,1024]{1,0:T(8,128)(2,1)S(1)} %get-tuple-element.59), channel_id=1, source_target_pairs={{0,8},{8,0},{16,24},{24,16},{1,9},{9,1},{17,25},{25,17},{2,10},{10... | collective-permute-start | bytes 1572872 | tf_op jit(solution)/shard_map/ppermute | solution.py:217
  106.0 13.3 %collective-permute-start.13 = (bf16[128,1024]{1,0:T(8,128)(2,1)S(1)}, bf16[128,1024]{1,0:T(8,128)(2,1)S(1)}, u32[]{:S(2)}, u32[]{:S(2)}) collective-permute-start(bf16[128,1024]{1,0:T(8,128)(2,1)S(1)} %get-tuple-element.91), channel_id=1, source_target_pairs={{0,16},{8,24},{16,0},{24,8},{1,17},{9,25},{17,1},{25,9},{2,18},{10... | collective-permute-start | bytes 786440 | tf_op jit(solution)/shard_map/ppermute | solution.py:217
  115.3 14.4 %collective-permute-start.33 = (bf16[128,1024]{1,0:T(8,128)(2,1)S(1)}, bf16[128,1024]{1,0:T(8,128)(2,1)S(1)}, u32[]{:S(2)}, u32[]{:S(2)}) collective-permute-start(bf16[128,1024]{1,0:T(8,128)(2,1)S(1)} %get-tuple-element.87), channel_id=1, source_target_pairs={{0,16},{8,24},{16,0},{24,8},{1,17},{9,25},{17,1},{25,9},{2,18},{10... | collective-permute-start | bytes 786440 | tf_op jit(solution)/shard_map/ppermute | solution.py:217
  119.6 12.6 %collective-permute-start.14 = (bf16[64,1024]{1,0:T(8,128)(2,1)S(1)}, bf16[64,1024]{1,0:T(8,128)(2,1)S(1)}, u32[]{:S(2)}, u32[]{:S(2)}) collective-permute-start(bf16[64,1024]{1,0:T(8,128)(2,1)S(1)} %slice.345), channel_id=1, source_target_pairs={{0,1},{1,0},{2,3},{3,2},{4,5},{5,4},{6,7},{7,6},{8,9},{9,8},{10,11... | collective-permute-start | bytes 393224 | tf_op jit(solution)/shard_map/ppermute | solution.py:217
  132.4 13.1 %collective-permute-start.18 = (bf16[64,1024]{1,0:T(8,128)(2,1)S(1)}, bf16[64,1024]{1,0:T(8,128)(2,1)S(1)}, u32[]{:S(2)}, u32[]{:S(2)}) collective-permute-start(bf16[64,1024]{1,0:T(8,128)(2,1)S(1)} %pad_maximum_fusion.9), channel_id=1, source_target_pairs={{0,4},{1,5},{2,6},{3,7},{4,0},{5,1},{6,2},{7,3},{8,12},{9,13},{10,... | collective-permute-start | bytes 393224 | tf_op jit(solution)/shard_map/ppermute | solution.py:217
  137.5 18.2 %collective-permute-start.38 = (bf16[64,1024]{1,0:T(8,128)(2,1)S(1)}, bf16[64,1024]{1,0:T(8,128)(2,1)S(1)}, u32[]{:S(2)}, u32[]{:S(2)}) collective-permute-start(bf16[64,1024]{1,0:T(8,128)(2,1)S(1)} %pad_maximum_fusion.15), channel_id=1, source_target_pairs={{0,4},{1,5},{2,6},{3,7},{4,0},{5,1},{6,2},{7,3},{8,12},{9,13},{10,... | collective-permute-start | bytes 393224 | tf_op jit(solution)/shard_map/ppermute | solution.py:217
  140.0 15.7 %collective-permute-start.39 = (bf16[64,1024]{1,0:T(8,128)(2,1)S(1)}, bf16[64,1024]{1,0:T(8,128)(2,1)S(1)}, u32[]{:S(2)}, u32[]{:S(2)}) collective-permute-start(bf16[64,1024]{1,0:T(8,128)(2,1)S(1)} %pad_maximum_fusion.16), channel_id=1, source_target_pairs={{0,6},{1,7},{2,4},{3,5},{4,2},{5,3},{6,0},{7,1},{8,14},{9,15},{10,... | collective-permute-start | bytes 393224 | tf_op jit(solution)/shard_map/ppermute | solution.py:217
  171.3 17.4 %collective-permute-start.52 = (f32[4,1024]{1,0:T(4,128)S(1)}, f32[4,1024]{1,0:T(4,128)S(1)}, u32[]{:S(2)}, u32[]{:S(2)}) collective-permute-start(f32[4,1024]{1,0:T(4,128)S(1)} %bitcast.104), channel_id=1, source_target_pairs={{0,1},{1,0},{2,3},{3,2},{4,5},{5,4},{6,7},{7,6},{8,9},{9,8},{10,11... | collective-permute-start | bytes 49160 | tf_op jit(solution)/shard_map/ppermute | solution.py:217
  (55 other events, 384.1 us)

commit v2 on v0

v2 whole, which is shorter than its diff:
```python
import functools

import jax
import jax.numpy as jnp
from jax import lax
from jax.experimental import pallas as pl
from jax.experimental.pallas import tpu as pltpu
from jax.sharding import PartitionSpec as P

GELU_C = 0.7978845608028654
GELU_A = 0.044715
EPSILON = 1e-06
BF = jnp.bfloat16
F32 = jnp.float32
LANES = 128
TILE = 16
MIB = 1024 * 1024

NN = (((1,), (0,)), ((), ()))
NT = (((1,), (1,)), ((), ()))
TN = (((0,), (0,)), ((), ()))

VMEM = pl.BlockSpec(memory_space=pltpu.VMEM)
SMEM = pl.BlockSpec(memory_space=pltpu.SMEM)
ANY = pl.BlockSpec(memory_space=pl.ANY)
HBM = pl.BlockSpec(memory_space=pltpu.HBM)
DMA = pltpu.SemaphoreType.DMA


def mm(a, b, dims=NN):
    return lax.dot_general(a, b, dims, preferred_element_type=F32)


def shape(dims, dtype=BF):
    return jax.ShapeDtypeStruct(dims, dtype)


def gelu_pair(preact):
    square = preact * preact
    tangent = jnp.tanh(GELU_C * (preact + GELU_A * (square * preact)))
    half = 0.5 * (1.0 + tangent)
    derivative = half + (0.5 * GELU_C) * preact * (1.0 - tangent * tangent) * (
        1.0 + 3.0 * GELU_A * square
    )
    return preact * half, derivative


class Line:
    def __init__(self):
        self.last = None

    def call(self, body, outs, args, specs=None, out_specs=None, scratch=(), flops=0, moved=MIB, vmem=8 * MIB, name=None):
        args, specs = list(args), list(specs) if specs is not None else [VMEM] * len(args)
        out_specs = list(out_specs) if out_specs is not None else [VMEM] * len(outs)
        count, given = len(args), len(outs)
        if self.last is not None:
            args.append(self.last)
            specs.append(ANY)

        def kernel(*refs):
            results = refs[len(args) :]
            results[given][...] = jnp.zeros((8, LANES), F32)
            body(*refs[:count], *results[:given], *results[given + 1 :])

        *results, self.last = pl.pallas_call(
            kernel,
            out_shape=[*outs, shape((8, LANES), F32)],
            in_specs=specs,
            out_specs=[*out_specs, VMEM],
            scratch_shapes=scratch,
            compiler_params=pltpu.CompilerParams(vmem_limit_bytes=vmem),
            cost_estimate=pl.CostEstimate(flops=flops, bytes_accessed=moved, transcendentals=0),
            name=name,
        )(*args)
        return results

    def move(self, *outputs, name="move"):
        arrays, places = [], {}
        aligned = True
        for pieces in outputs:
            for rows, terms in pieces:
                aligned = aligned and rows % TILE == 0
                for array, first in terms:
                    aligned = aligned and first % TILE == 0
                    if id(array) not in places:
                        places[id(array)] = len(arrays)
                        arrays.append(array)
        width = arrays[0].shape[1]
        if not aligned:
            return [
                jnp.concatenate([
                    added(*[a[f : f + rows] for a, f in terms]) if len(terms) > 1 else terms[0][0][terms[0][1] : terms[0][1] + rows]
                    for rows, terms in pieces
                ])
                for pieces in outputs
            ]

        def body(*refs):
            for pieces, out in zip(outputs, refs[len(arrays) :]):
                at = 0
                for rows, terms in pieces:
                    parts = [refs[places[id(a)]][f : f + rows, :] for a, f in terms]
                    if len(parts) > 1:
                        parts = [functools.reduce(jnp.add, [p.astype(F32) for p in parts]).astype(BF)]
                    out[at : at + rows, :] = parts[0]
                    at += rows

        outs = [shape((sum(rows for rows, _ in pieces), width)) for pieces in outputs]
        return self.call(body, outs, arrays, name=name)


def added(*terms):
    return functools.reduce(jnp.add, [t.astype(F32) for t in terms]).astype(BF)


def swap(x, axis, mask):
    return lax.ppermute(x, axis, [(i, i ^ mask) for i in range(lax.axis_size(axis))])


def hot_rows(ids_ref, rel_to, count):
    tok = ids_ref.shape[1]
    rows = lax.broadcasted_iota(jnp.int32, (count, tok), 0)
    return [(rows == (ids_ref[k : k + 1, :] ^ rel_to)).astype(F32) for k in range(2)]


def at_rows(places, total):
    tok = places[0].shape[1]
    rows = lax.broadcasted_iota(jnp.int32, (total, tok), 0)
    return functools.reduce(jnp.add, [(rows == p).astype(F32) for p in places]).astype(BF)


def onehot(column, width):
    lanes = lax.broadcasted_iota(jnp.int32, (column.shape[0], width), 1)
    return (lanes == column).astype(F32)


def on_device(tokens, context, w_out, w_router, expert_ids, w_in, w_down, cotangent):
    tok, width = tokens.shape
    experts = lax.axis_size("expert")
    dp = lax.axis_size("dp")
    far = dp // 2
    cap = 2 * tok // experts
    slots = 2 * tok
    hidden = w_in.shape[2]
    masks = [0, 2, 1, 3]
    low = experts // len(masks)
    shift = low.bit_length() - 1
    chunks = [[0, 1], [2, 3]]
    size = low * cap
    me = lax.axis_index("expert").astype(jnp.int32)
    mine = lax.axis_index("dp").astype(jnp.int32)
    info = jnp.concatenate([me.reshape(1), mine ^ jnp.arange(dp, dtype=jnp.int32)])
    ids_t = expert_ids.T
    router_t = w_router.T
    weight_in, weight_down = w_in[0], w_down[0]
    per = width // experts
    part = width // dp
    line = Line()

    def order(rel):
        high = rel >> shift
        return (high >> 1) | ((high & 1) << 1), rel & (low - 1)

    def head_body(info_ref, ids_hbm, cot_hbm, tok_hbm, ctx_hbm, router_hbm, w_out_hbm, *refs):
        outs, copies = refs[: low + 9], refs[low + 9 :]
        lows, (placed_ref, resid_ref, inv_ref, normed_ref, cols_ref), sends = outs[:low], outs[low : low + 5], outs[low + 5 :]
        held, sems = copies[:6], copies[6]
        loads = [pltpu.make_async_copy(src, dst, sems.at[i]) for i, (src, dst) in enumerate(
            zip((ids_hbm, ctx_hbm, w_out_hbm, tok_hbm, cot_hbm, router_hbm), held))]
        for load in loads:
            load.start()
        ids_ref, ctx_ref, w_out_ref, tok_ref, cot_ref, router_ref = held
        loads[0].wait()
        rows = lax.broadcasted_iota(jnp.int32, (tok, tok), 0)
        cols = lax.broadcasted_iota(jnp.int32, (tok, tok), 1)
        upper = (rows < cols).astype(BF)
        hot = hot_rows(ids_ref, info_ref[0], experts)
        before = [mm(h.astype(BF), upper) for h in hot]
        first = jnp.sum(hot[0], axis=1, keepdims=True)
        rank = [jnp.sum(before[0] * hot[0], axis=0, keepdims=True),
                jnp.sum((before[1] + first) * hot[1], axis=0, keepdims=True)]
        places, spots = [], []
        for k in range(2):
            block, lower = order(ids_ref[k : k + 1, :] ^ info_ref[0])
            places.append((block * low + lower) * cap + rank[k].astype(jnp.int32))
            placed_ref[k : k + 1, :] = places[k]
            spots.append((lower * len(masks) + block) * cap + rank[k].astype(jnp.int32))
        loads[1].wait()
        loads[2].wait()
        attn = mm(ctx_ref[...], w_out_ref[...])
        loads[3].wait()
        resid = (tok_ref[...].astype(F32) + attn).astype(BF)
        resid_ref[...] = resid
        resid_f = resid.astype(F32)
        inv = lax.rsqrt(jnp.mean(resid_f * resid_f, axis=1, keepdims=True) + EPSILON)
        inv_ref[...] = inv
        normed = (resid_f * inv).astype(BF)
        normed_ref[...] = normed
        moved = mm(at_rows(places, slots), normed).astype(BF)
        for c in range(len(masks)):
            sends[c][...] = moved[c * size : (c + 1) * size, :]
        loads[4].wait()
        moved = mm(at_rows(spots, slots), cot_ref[...]).astype(BF)
        each = slots // low
        for m in range(low):
            lows[m][...] = moved[m * each : (m + 1) * each, :]
        loads[5].wait()
        logits = mm(router_ref[...], normed, NT)
        hot = hot_rows(ids_ref, 0, experts)
        gates = [jax.nn.sigmoid(jnp.sum(logits * h, axis=0, keepdims=True)) for h in hot]
        ids_f = ids_ref[...].astype(F32)
        table = jnp.concatenate(gates + [ids_f, placed_ref[...].astype(F32), ids_f], axis=0)
        cols_ref[...] = table.T

    outs = line.call(
        head_body,
        [shape((slots // low, width))] * low + [shape((2, tok), jnp.int32)]
        + [shape((tok, width)), shape((tok, 1), F32), shape((tok, width)), shape((tok, 8), F32)] + [shape((size, width))] * 4,
        (info, ids_t, cotangent, tokens, context, router_t, w_out), specs=[SMEM] + [HBM] * 6,
        scratch=[pltpu.VMEM((2, tok), jnp.int32), pltpu.VMEM((tok, width), BF), pltpu.VMEM((width, width), BF),
                 pltpu.VMEM((tok, width), BF), pltpu.VMEM((tok, width), BF), pltpu.VMEM((experts, width), BF), DMA((6,))],
        flops=2 * tok * width * width, moved=4 * MIB, vmem=12 * MIB, name="head")
    cot_low, (placed, resid, inv, normed, cols), sends = outs[:low], outs[low : low + 5], outs[low + 5 :]
    cot_low = [cot_low[0]] + [swap(cot_low[m], "expert", m) for m in range(1, low)]
    norm_high = [sends[0]] + [swap(sends[c], "expert", masks[c] * low) for c in (1, 2, 3)]

    cot_high = line.move(*[[(cap, [(cot_low[m], c * cap)]) for m in range(low)] for c in range(4)], name="pack_cot_z")
    cot_high = [cot_high[0]] + [swap(cot_high[c], "expert", masks[c] * low) for c in (1, 2, 3)]

    def norm_chunk(chunk):
        lows = []
        if low > 1:
            lows = line.move(*[[(cap, [(norm_high[c], m * cap)]) for c in chunk] for m in range(1, low)], name="pack_norm_y")
            lows = [swap(x, "expert", m + 1) for m, x in enumerate(lows)]
        pieces = []
        for i, c in enumerate(chunk):
            pieces.append((cap, [(norm_high[c], 0)]))
            pieces += [(cap, [(x, i * cap)]) for x in lows]
        own = line.move(pieces, name="pack_norm_x")[0]
        across = swap(own, "dp", far)
        return own, swap(own, "dp", 1), across, swap(across, "dp", 1)

    def cot_chunk(chunk):
        own = line.move([(size, [(cot_high[c], 0)]) for c in chunk], name="pack_cot_x")[0]
        across = swap(own, "dp", far)
        return own, swap(own, "dp", 1), across, swap(across, "dp", 1)

    block = 256 if hidden % 256 == 0 else hidden

    def forward(parts):
        each = parts[0].shape[0]
        rows = each * len(parts)

        def body(info_ref, *refs):
            ins = refs[: len(parts)]
            (router_ref, in_ref, down_ref, rows_hbm, act_hbm, der_ref, gate_ref, keep_ref, send_ref,
             rows_ref, act_ref, total, sems) = refs[len(parts) :]
            for i, ref in enumerate(ins):
                rows_ref[i * each : (i + 1) * each, :] = ref[...]
            stores = [pltpu.make_async_copy(rows_ref, rows_hbm, sems.at[0]), pltpu.make_async_copy(act_ref, act_hbm, sems.at[1])]
            stores[0].start()
            for j in range(hidden // block):
                at = slice(j * block, (j + 1) * block)
                value, derivative = gelu_pair(mm(rows_ref[...], in_ref[:, at]))
                act = value.astype(BF)
                act_ref[:, at] = act
                der_ref[:, at] = derivative.astype(BF)
                term = mm(act, down_ref[at, :])
                total[...] = term if j == 0 else total[...] + term
            stores[1].start()
            keep_ref[...] = total[: rows // 2, :].astype(BF)
            send_ref[...] = total[rows // 2 :, :].astype(BF)
            logits = mm(rows_ref[...], router_ref[...], NT)
            lanes = lax.broadcasted_iota(jnp.int32, logits.shape, 1)
            picked = jnp.sum(jnp.where(lanes == info_ref[0], logits, 0.0), axis=1, keepdims=True)
            gate_ref[...] = jax.nn.sigmoid(picked)
            for store in stores:
                store.wait()

        return line.call(
            body,
            [shape((rows, width)), shape((rows, hidden)), shape((rows, hidden)), shape((rows, 1), F32),
             shape((rows // 2, width)), shape((rows // 2, width))],
            (info, *parts, router_t, weight_in, weight_down), specs=[SMEM] + [VMEM] * (len(parts) + 3),
            out_specs=[HBM] * 2 + [VMEM] * 4,
            scratch=[pltpu.VMEM((rows, width), BF), pltpu.VMEM((rows, hidden), BF), pltpu.VMEM((rows, width), F32), DMA((2,))],
            flops=4 * rows * width * hidden, moved=8 * MIB, vmem=20 * MIB, name="forward")

    def backward(parts, gate, der):
        each = parts[0].shape[0]
        rows = each * len(parts)

        def body(*refs):
            ins = refs[: len(parts)]
            (gate_ref, der_ref, in_ref, down_ref, grads_hbm, pre_hbm, keep_ref, send_ref,
             grads_ref, pre_ref, total, sems) = refs[len(parts) :]
            for i, ref in enumerate(ins):
                at = slice(i * each, (i + 1) * each)
                grads_ref[at, :] = (gate_ref[at, :] * ref[...].astype(F32)).astype(BF)
            stores = [pltpu.make_async_copy(grads_ref, grads_hbm, sems.at[0]), pltpu.make_async_copy(pre_ref, pre_hbm, sems.at[1])]
            stores[0].start()
            for j in range(hidden // block):
                at = slice(j * block, (j + 1) * block)
                act_grad = mm(grads_ref[...], down_ref[at, :], NT)
                pre = (act_grad * der_ref[:, at].astype(F32)).astype(BF)
                pre_ref[:, at] = pre
                term = mm(pre, in_ref[:, at], NT)
                total[...] = term if j == 0 else total[...] + term
            stores[1].start()
            keep_ref[...] = total[: rows // 2, :].astype(BF)
            send_ref[...] = total[rows // 2 :, :].astype(BF)
            for store in stores:
                store.wait()

        return line.call(
            body,
            [shape((rows, width)), shape((rows, hidden)), shape((rows // 2, width)), shape((rows // 2, width))],
            (*parts, gate, der, weight_in, weight_down), out_specs=[HBM] * 2 + [VMEM] * 2,
            scratch=[pltpu.VMEM((rows, width), BF), pltpu.VMEM((rows, hidden), BF), pltpu.VMEM((rows, width), F32), DMA((2,))],
            flops=4 * rows * width * hidden, moved=8 * MIB, vmem=20 * MIB, name="backward")

    half = slots // 2

    def cross(keep, send_in):
        both = line.move([(half, [(keep, 0), (send_in, 0)])], name="sum_core")[0]
        return swap(both, "dp", far)

    def gather(i, near_keep, near_in, crossing):
        terms = lambda at, rows: (rows, [(near_keep, i * half + at), (near_in, i * half + at), (crossing, at)])
        total, *lows = line.move(
            [terms(0, half)], *[[terms(j * size + m * cap, cap) for j in range(2)] for m in range(1, low)], name="sum_x")
        return total, [swap(x, "expert", m + 1) for m, x in enumerate(lows)]

    def send_back(i, total, lows):
        blocks = line.move(
            *[[(cap, [(total, j * size)])] + [(cap, [(x, j * cap)]) for x in lows] for j in range(2)], name="pack_back_z")
        return [swap(b, "expert", masks[c] * low) if masks[c] else b for c, b in zip(chunks[i], blocks)]

    norm_a = norm_chunk(chunks[0])
    norm_b = norm_chunk(chunks[1])
    cot_a = cot_chunk(chunks[0])
    rows_n, act_n, der_n, gate_n, keep_n, send_n = forward([norm_a[0], norm_b[0], norm_a[1], norm_b[1]])
    near_out = swap(send_n, "dp", 1)
    cot_b = cot_chunk(chunks[1])
    rows_a, act_a, der_a, gate_a, keep_a, send_a = forward([norm_a[2], norm_a[3]])
    core_a = swap(send_a, "dp", 1)
    rows_b, act_b, der_b, gate_b, keep_b, send_b = forward([norm_b[2], norm_b[3]])
    core_b = swap(send_b, "dp", 1)
    out_a = cross(keep_a, core_a)
    out_b = cross(keep_b, core_b)
    grads_n, pre_n, ikeep_n, isend_n = backward([cot_a[0], cot_b[0], cot_a[1], cot_b[1]], gate_n, der_n)
    near_in = swap(isend_n, "dp", 1)
    grads_a, pre_a, ikeep_a, isend_a = backward([cot_a[2], cot_a[3]], gate_a, der_a)
    icore_a = swap(isend_a, "dp", 1)
    grads_b, pre_b, ikeep_b, isend_b = backward([cot_b[2], cot_b[3]], gate_b, der_b)
    icore_b = swap(isend_b, "dp", 1)
    in_a = cross(ikeep_a, icore_a)
    in_b = cross(ikeep_b, icore_b)
    total_oa = gather(0, keep_n, near_out, out_a)
    total_ob = gather(1, keep_n, near_out, out_b)
    back_out = send_back(0, *total_oa)
    back_out += send_back(1, *total_ob)

    def weight_grad(lefts, rights):
        left, right = lefts[0].shape[1], rights[0].shape[1]
        tile = 256 if left % 256 == 0 else left

        def body(*refs):
            count = 2 * len(lefts)
            out_hbm, held, result, sems = refs[count], refs[count + 1 : 2 * count + 1], refs[2 * count + 1], refs[2 * count + 2]
            loads = [pltpu.make_async_copy(src, dst, sems.at[i]) for i, (src, dst) in enumerate(zip(refs[:count], held))]
            for load in loads:
                load.start()
            for load in loads:
                load.wait()
            stores = []
            for i in range(left // tile):
                at = slice(i * tile, (i + 1) * tile)
                result[at, :] = functools.reduce(
                    jnp.add, [mm(a[:, at], b[...], TN) for a, b in zip(held[: len(lefts)], held[len(lefts) :])]).astype(BF)
                stores.append(pltpu.make_async_copy(result.at[at, :], out_hbm.at[at, :], sems.at[count + i]))
                stores[-1].start()
            for store in stores:
                store.wait()

        return line.call(
            body, [shape((left, right))], (*lefts, *rights), specs=[HBM] * (2 * len(lefts)), out_specs=[HBM],
            scratch=[pltpu.VMEM(x.shape, BF) for x in (*lefts, *rights)]
            + [pltpu.VMEM((left, right), BF), DMA((2 * len(lefts) + left // tile,))],
            flops=4 * slots * 2 * left * right, moved=6 * MIB, vmem=20 * MIB, name="weights")[0]

    grad_w_down = weight_grad((act_n, act_a, act_b), (grads_n, grads_a, grads_b))
    total_ia = gather(0, ikeep_n, near_in, in_a)
    grad_w_in = weight_grad((rows_n, rows_a, rows_b), (pre_n, pre_a, pre_b))
    back_in = send_back(0, *total_ia)
    total_ib = gather(1, ikeep_n, near_in, in_b)
    back_in += send_back(1, *total_ib)

    spare = -(-experts // TILE) * TILE
    span = width + spare

    def combine_body(*refs):
        backs = refs[:4]
        placed_ref, cols_ref, resid_ref, cot_ref, normed_ref, out_ref, table_ref, router_ref = refs[4:]
        held = jnp.concatenate([b[...] for b in backs], axis=0)
        cot_f = cot_ref[...].astype(F32)
        total = resid_ref[...].astype(F32)
        table = jnp.zeros((tok, LANES), F32)
        for k in range(2):
            gate = cols_ref[:, k : k + 1]
            taken = mm(at_rows([placed_ref[k : k + 1, :]], slots), held, TN)
            total = total + gate * taken
            logit = jnp.sum(cot_f * taken, axis=1, keepdims=True) * gate * (1.0 - gate)
            table = table + onehot(cols_ref[:, 2 + k : 3 + k].astype(jnp.int32), LANES) * logit
        out_ref[...] = total.astype(BF)
        table = table.astype(BF)
        table_ref[...] = table
        router_ref[...] = mm(table, normed_ref[...], TN)[:spare, :].astype(BF)

    output, table, local_router = line.call(
        combine_body, [shape((tok, width)), shape((tok, LANES)), shape((spare, width))],
        (*back_out, placed, cols, resid, cotangent, normed),
        flops=8 * tok * slots * width, moved=2 * MIB, name="combine")

    def tail_body(info_ref, *refs):
        backs = refs[:4]
        (placed_ref, table_ref, router_ref, resid_ref, inv_ref, local_ref, cot_hbm, w_out_hbm, ctx_hbm,
         grad_ref, grad_ctx_ref, keep_ref, send_ref, cot_ref, w_out_ref, ctx_ref, turned, sems) = refs[4:]
        loads = [pltpu.make_async_copy(src, dst, sems.at[i]) for i, (src, dst) in enumerate(
            ((cot_hbm, cot_ref), (ctx_hbm, ctx_ref), (w_out_hbm, w_out_ref)))]
        for load in loads:
            load.start()
        held = jnp.concatenate([b[...] for b in backs], axis=0)
        where = at_rows([placed_ref[k : k + 1, :] for k in range(2)], slots)
        normed_grad = mm(where, held, TN) + mm(table_ref[:, :experts], router_ref[...])
        resid_f = resid_ref[...].astype(F32)
        inv_col = inv_ref[...]
        mean_term = jnp.mean(normed_grad * resid_f, axis=1, keepdims=True)
        loads[0].wait()
        grad = (cot_ref[...].astype(F32) + inv_col * normed_grad
                - (inv_col * inv_col * inv_col * mean_term) * resid_f).astype(BF)
        grad_ref[...] = grad
        outs = [(send_ref if m % 2 else keep_ref, (m // 2) * span) for m in range(dp)]
        for m, (out, base) in enumerate(outs):
            at = pl.ds(pl.multiple_of(info_ref[1 + m] * part, LANES), part)
            turned[:, m * part : (m + 1) * part] = grad_ref[:, at]
            out[base + width : base + span, :] = local_ref[:, at]
        loads[1].wait()
        tile = max(per, LANES)
        for i in range(width // tile):
            block = mm(ctx_ref[:, i * tile : (i + 1) * tile], turned[...], TN).astype(BF)
            for j in range(tile // per):
                spot, lower = order((i * (tile // per) + j) ^ info_ref[0])
                to = (spot * low + lower) * per
                for m, (out, base) in enumerate(outs):
                    out[pl.ds(pl.multiple_of(base + to, TILE), per), :] = (
                        block[j * per : (j + 1) * per, m * part : (m + 1) * part])
        loads[2].wait()
        grad_ctx_ref[...] = mm(grad, w_out_ref[...], NT).astype(BF)

    grad_tokens, grad_context, keep, send = line.call(
        tail_body,
        [shape((tok, width)), shape((tok, width)), shape((far * span, part)), shape((far * span, part))],
        (info, *back_in, placed, table, router_t, resid, inv, local_router, cotangent, w_out, context),
        specs=[SMEM] + [VMEM] * 10 + [HBM] * 3,
        scratch=[pltpu.VMEM((tok, width), BF), pltpu.VMEM((width, width), BF), pltpu.VMEM((tok, width), BF),
                 pltpu.VMEM((tok, width), BF), DMA((3,))],
        flops=6 * tok * width * width, moved=6 * MIB, vmem=16 * MIB, name="tail")

    core = swap(send, "dp", 1)
    spot = lambda d, c, m: d * span + (c * low + m) * per
    two = lambda first: [(keep, first), (core, first)]
    group = [(spare, two(width))]
    sum_x = line.move(
        [(2 * low * per, two(span)), (spare, two(span + width))],
        *[[(per, two(spot(d, c, m))) for d in range(2) for c in (2, 3)] for m in range(1, low)], name="reduce_core")
    first_x = swap(sum_x[0], "dp", far)
    second_low = [swap(x, "expert", m + 1) for m, x in enumerate(sum_x[1:])]
    first = line.move(
        *[[(per, two(spot(0, c, m)) + [(first_x, (c * low + m) * per)]) for c in (0, 1)]
          + [(spare, two(width) + [(first_x, 2 * low * per)])] for m in range(low)], name="reduce_x")
    first_low = [swap(x, "expert", m) for m, x in enumerate(first) if m]
    second = line.move(
        *[[(per, two(spot(d, c, 0)) + [(x, (d * 2 + i) * per) for x in second_low]) for i, c in enumerate((2, 3))]
          for d in (1, 0)], name="reduce_y")
    second_x = swap(second[0], "dp", far)
    router_terms = [(x, 2 * per) for x in [first[0], *first_low]]
    blocks = line.move(
        *[[(per, [(x, c * per) for x in [first[0], *first_low]]), (spare, router_terms)] for c in (0, 1)],
        *[[(per, [(second[1], c * per), (second_x, c * per)]), (spare, router_terms)] for c in (0, 1)], name="reduce_xy")
    blocks = [blocks[0]] + [swap(blocks[c], "expert", masks[c] * low) for c in (1, 2, 3)]
    own = line.move([(per + spare, [(b, 0) for b in blocks])], name="reduce_z")[0]
    quarters = [own] + [swap(own, "dp", m) for m in range(1, dp)]

    def final_body(info_ref, *refs):
        out_ref, router_ref = refs[dp:]
        for m in range(dp):
            at = pl.ds(pl.multiple_of(info_ref[1 + m] * part, LANES), part)
            out_ref[:, at] = refs[m][:per, :].astype(F32)
            table = refs[m][per:, :].astype(F32)
            rows = lax.broadcasted_iota(jnp.int32, table.shape, 0)
            router_ref[:, at] = jnp.sum(jnp.where(rows == info_ref[0], table, 0.0), axis=0, keepdims=True)

    grad_w_out, grad_w_router = line.call(
        final_body, [shape((per, width), F32), shape((1, width), F32)], (info, *quarters),
        specs=[SMEM] + [VMEM] * dp, name="final")

    return (
        output,
        grad_tokens,
        grad_context,
        grad_w_out,
        grad_w_router.reshape(width, 1),
        grad_w_in.reshape(1, width, hidden),
        grad_w_down.reshape(1, hidden, width),
    )


def solution(mesh):
    split = P(("dp", "expert"), None)
    return jax.shard_map(
        on_device,
        mesh=mesh,
        in_specs=(split, split, P(), P(), split, P("expert", None, "dp"), P("expert", "dp", None), split),
        out_specs=(split, split, split, P("expert", None), P(None, "expert"), P("expert", None, "dp"),
                   P("expert", "dp", None)),
        check_vma=False,
    )
```

time: 358 us -> 165 us (0.46)
  waiting for transfers between devices: 162 us -> 69.1 us
  blocking collectives: 80.9 us -> 0 us
  matrix products: 43 us -> 0 us
  starting transfers between devices: 11.9 us -> 51.9 us
  Pallas kernels: 0 us -> 36.6 us
  local copies, waits for them, and re-layouts: 26.2 us -> 5.86 us
  other arithmetic: 18.7 us -> 0.08 us
  between operations: 14.4 us -> 1.01 us
    reduce_scatter x3 -> x0, waiting for transfers between devices: 140 us -> none  [the longest x1 74.1 us: on_device(): lax.psum_scatter(local_out, 'expert', scatter_dimension=0, tiled=True)]
    ppermute x0 -> x52, waiting for transfers between devices: none -> 69.1 us  [swap(): lax.ppermute(x, axis, [(i, i ^ mask) for i in range(lax.axis_size(axis))])]
    ppermute x0 -> x52, starting transfers between devices: none -> 51.9 us  [swap(): lax.ppermute(x, axis, [(i, i ^ mask) for i in range(lax.axis_size(axis))])]
    dot_general x12 -> x0, matrix products: 43 us -> none  [the longest x1 7.71 us: on_device(): jnp.dot(rows_grad, weight_down.T, preferred_element_type=jnp.float32)]
    all_to_all x2 -> x0, blocking collectives: 39.3 us -> none  [the longest x1 21.7 us: on_device(): lax.all_to_all(send_in, 'expert', split_axis=0, concat_axis=0, tiled=True)]
    pallas_call x0 -> x36, Pallas kernels: none -> 36.6 us  [call(): pl.pallas_call(kernel, out_shape=[*outs, shape((8, LANES), F32)], in_spec...]
    unnamed x1 -> x0, blocking collectives: 35.9 us -> none
    all_gather x2 -> x0, waiting for transfers between devices: 15.7 us -> none  [the longest x1 15.7 us: on_device(): group_grad = lax.all_gather(got_grad, 'dp', axis=0, tiled=True)]
  transfers between devices with their start and end apart: 8 -> 52, of which waited for: 5 -> 26; matrix products, arithmetic and copies ran while one was open for 13% -> 0% of each run, Pallas kernels for 0% -> 17%
where the time goes in v2:
time: 165 us; the launch traced here: 164 us
  waiting for transfers between devices  69.1 us (42%)
  starting transfers between devices  51.9 us (31%)
  Pallas kernels  36.6 us (22%)
  local copies, waits for them, and re-layouts  5.86 us (4%)
    ppermute x52, waiting for transfers between devices, swap(): lax.ppermute(x, axis, [(i, i ^ mask) for i in range(lax.axis_size(axis))])  69.1 us
    ppermute x52, starting transfers between devices, swap(): lax.ppermute(x, axis, [(i, i ^ mask) for i in range(lax.axis_size(axis))])  51.9 us
    pallas_call x36, Pallas kernels, call(): pl.pallas_call(kernel, out_shape=[*outs, shape((8, LANES), F32)], in_spec...  36.6 us
    unnamed x24, local copies, waits for them, and re-layouts  5.86 us
  transfers between devices with their start and end apart: 52, of which 26 were waited for; matrix products, arithmetic and copies ran while one was open for 0% of the time, Pallas kernels for 17%

profile of v2, /device:TPU:0, one launch (start us, length us, event | category | flops | bytes accessed | tf_op | source)
XLA Modules:
  0.0 164.5 jit_solution(9961890420419372236)
XLA Ops:
  6.6 2.6 %head.1 = (bf16[128,1024]{1,0:T(8,128)(2,1)S(1)}, bf16[128,1024]{1,0:T(8,128)(2,1)S(1)}, s32[2,128]{1,0:T(2,128)S(1)}, bf16[128,1024]{1,0:T(8,128)(2,1)S(1)}, f3...) custom-call(s32[5]{0:T(128)S(1)} %pad_add_fusion.refs_0_, ...), custom_call_target="tpu_custom_call" | custom-call | flops 268435456 | bytes 4194304 | tf_op jit(solution)/shard_map/head/pallas_call | solution.py:65
  9.2 3.0 %collective-permute-start.1 = (bf16[128,1024]{1,0:T(8,128)(2,1)S(1)}, bf16[128,1024]{1,0:T(8,128)(2,1)S(1)}, u32[]{:S(2)}, u32[]{:S(2)}) collective-permute-start(bf16[128,1024]{1,0:T(8,128)(2,1)S(1)} %get-tuple-element.138), channel_id=1, source_target_pairs={{0,1},{1,0},{2,3},{3,2},{4,5},{5,4},{6,7},{7,6},{8,9},{9,8},{10,11... | collective-permute-start | bytes 786440 | tf_op jit(solution)/shard_map/ppermute | solution.py:117
  12.2 2.6 %collective-permute-start = (bf16[64,1024]{1,0:T(8,128)(2,1)S(1)}, bf16[64,1024]{1,0:T(8,128)(2,1)S(1)}, u32[]{:S(2)}, u32[]{:S(2)}) collective-permute-start(bf16[64,1024]{1,0:T(8,128)(2,1)S(1)} %get-tuple-element.136), channel_id=1, source_target_pairs={{0,4},{1,5},{2,6},{3,7},{4,0},{5,1},{6,2},{7,3},{8,12},{9,13},{10,... | collective-permute-start | bytes 393224 | tf_op jit(solution)/shard_map/ppermute | solution.py:117
  14.8 3.7 %collective-permute-done.1.refs_1_ = bf16[128,1024]{1,0:T(8,128)(2,1)S(1)} collective-permute-done((bf16[128,1024]{1,0:T(8,128)(2,1)S(1)}, bf16[128,1024]{1,0:T(8,128)(2,1)S(1)}, u32[]{:S(2)}, u32[]{:S(2)}) %collective-permute-start.1) | collective-permute-done | bytes 262176 | tf_op jit(solution)/shard_map/ppermute | solution.py:117
  18.5 2.3 %collective-permute-done.refs_1_.refs_2_ = bf16[64,1024]{1,0:T(8,128)(2,1)S(1)} collective-permute-done((bf16[64,1024]{1,0:T(8,128)(2,1)S(1)}, bf16[64,1024]{1,0:T(8,128)(2,1)S(1)}, u32[]{:S(2)}, u32[]{:S(2)}) %collective-permute-start) | collective-permute-done | bytes 131104 | tf_op jit(solution)/shard_map/ppermute | solution.py:117
  22.1 2.8 %collective-permute-start.4 = (bf16[64,1024]{1,0:T(8,128)(2,1)S(1)}, bf16[64,1024]{1,0:T(8,128)(2,1)S(1)}, u32[]{:S(2)}, u32[]{:S(2)}) collective-permute-start(bf16[64,1024]{1,0:T(8,128)(2,1)S(1)} %get-tuple-element.145), channel_id=1, source_target_pairs={{0,6},{1,7},{2,4},{3,5},{4,2},{5,3},{6,0},{7,1},{8,14},{9,15},{10,... | collective-permute-start | bytes 393224 | tf_op jit(solution)/shard_map/ppermute | solution.py:117
  26.4 4.9 %collective-permute-done.4.refs_1_.refs_2_ = bf16[64,1024]{1,0:T(8,128)(2,1)S(1)} collective-permute-done((bf16[64,1024]{1,0:T(8,128)(2,1)S(1)}, bf16[64,1024]{1,0:T(8,128)(2,1)S(1)}, u32[]{:S(2)}, u32[]{:S(2)}) %collective-permute-start.4) | collective-permute-done | bytes 131104 | tf_op jit(solution)/shard_map/ppermute | solution.py:117
  40.1 7.1 %collective-permute-done.8.refs_1_ = bf16[64,1024]{1,0:T(8,128)(2,1)S(1)} collective-permute-done((bf16[64,1024]{1,0:T(8,128)(2,1)S(1)}, bf16[64,1024]{1,0:T(8,128)(2,1)S(1)}, u32[]{:S(2)}, u32[]{:S(2)}) %collective-permute-start.8) | collective-permute-done | bytes 131104 | tf_op jit(solution)/shard_map/ppermute | solution.py:117
  49.5 5.1 %forward.3 = (bf16[512,1024]{1,0:T(8,128)(2,1)S(1)}, bf16[512,1024]{1,0:T(8,128)(2,1)S(1)}, bf16[512,1024]{1,0:T(8,128)(2,1)S(1)}, f32[512,1]{1,0:T(8,128)S(1)},...) custom-call(s32[5]{0:T(128)S(1)} %pad_add_fusion.refs_0_, ...), custom_call_target="tpu_custom_call" | custom-call | flops 2147483648 | bytes 8388608 | tf_op jit(solution)/shard_map/forward/pallas_call | solution.py:65
  56.3 3.1 %forward.4 = (bf16[256,1024]{1,0:T(8,128)(2,1)S(1)}, bf16[256,1024]{1,0:T(8,128)(2,1)S(1)}, bf16[256,1024]{1,0:T(8,128)(2,1)S(1)}, f32[256,1]{1,0:T(8,128)S(1)},...) custom-call(s32[5]{0:T(128)S(1)} %pad_add_fusion.refs_0_, ...), custom_call_target="tpu_custom_call" | custom-call | flops 1073741824 | bytes 8388608 | tf_op jit(solution)/shard_map/forward/pallas_call | solution.py:65
  59.6 3.1 %forward.5 = (bf16[256,1024]{1,0:T(8,128)(2,1)S(1)}, bf16[256,1024]{1,0:T(8,128)(2,1)S(1)}, bf16[256,1024]{1,0:T(8,128)(2,1)S(1)}, f32[256,1]{1,0:T(8,128)S(1)},...) custom-call(s32[5]{0:T(128)S(1)} %pad_add_fusion.refs_0_, ...), custom_call_target="tpu_custom_call" | custom-call | flops 1073741824 | bytes 8388608 | tf_op jit(solution)/shard_map/forward/pallas_call | solution.py:65
  65.1 3.6 %backward.3 = (bf16[512,1024]{1,0:T(8,128)(2,1)S(1)}, bf16[512,1024]{1,0:T(8,128)(2,1)S(1)}, bf16[256,1024]{1,0:T(8,128)(2,1)S(1)}, bf16[256,1024]{1,0:T(8,128)(2,1)S(1)}, f32[8,128]{1,0:T(8,128)S(1)}) custom-call(bf16[128,1024]{1,0:T(8,128)(2,1)S(1)} %get-tuple-element.168.refs_0_, bf16[128,1024]{1,0:T(8,128)(2,1)S(1)} %get-tuple-element.165.refs_1_, ...), custom_call_target="tpu_custom_call" | custom-call | flops 2147483648 | bytes 8388608 | tf_op jit(solution)/shard_map/backward/pallas_call | solution.py:65
  75.5 6.9 %collective-permute-done.17.refs_2_ = bf16[128,1024]{1,0:T(8,128)(2,1)S(1)} collective-permute-done((bf16[128,1024]{1,0:T(8,128)(2,1)S(1)}, bf16[128,1024]{1,0:T(8,128)(2,1)S(1)}, u32[]{:S(2)}, u32[]{:S(2)}) %collective-permute-start.17) | collective-permute-done | bytes 262176 | tf_op jit(solution)/shard_map/ppermute | solution.py:117
  84.2 3.3 %collective-permute-done.28.refs_2_ = bf16[128,1024]{1,0:T(8,128)(2,1)S(1)} collective-permute-done((bf16[128,1024]{1,0:T(8,128)(2,1)S(1)}, bf16[128,1024]{1,0:T(8,128)(2,1)S(1)}, u32[]{:S(2)}, u32[]{:S(2)}) %collective-permute-start.28) | collective-permute-done | bytes 262176 | tf_op jit(solution)/shard_map/ppermute | solution.py:117
  92.6 3.5 %weights.2 = (bf16[1024,1024]{1,0:T(8,128)(2,1)}, f32[8,128]{1,0:T(8,128)S(1)}) custom-call(bf16[512,1024]{1,0:T(8,128)(2,1)S(1)} %get-tuple-element.206.refs_0_, bf16[256,1024]{1,0:T(8,128)(2,1)S(1)} %get-tuple-element.207.refs_1_, bf16[256,1024]{1,0:T(8,128)(2,1)S(1)} %get-tuple-element.208.refs_2_, bf16[512,1024]{1,0:T(8,128)(2,1)S(1)} %get-tuple-element.209.refs_3_, ...), custom_call_target="tpu_custom_call" | custom-call | flops 2147483648 | bytes 6291456 | tf_op jit(solution)/shard_map/weights/pallas_call | solution.py:65
  99.1 3.8 %weights.3 = (bf16[1024,1024]{1,0:T(8,128)(2,1)}, f32[8,128]{1,0:T(8,128)S(1)}) custom-call(bf16[512,1024]{1,0:T(8,128)(2,1)S(1)} %get-tuple-element.216.refs_0_, bf16[256,1024]{1,0:T(8,128)(2,1)S(1)} %get-tuple-element.217.refs_1_, bf16[256,1024]{1,0:T(8,128)(2,1)S(1)} %get-tuple-element.218.refs_2_, bf16[512,1024]{1,0:T(8,128)(2,1)S(1)} %get-tuple-element.219.refs_3_, ...), custom_call_target="tpu_custom_call" | custom-call | flops 2147483648 | bytes 6291456 | tf_op jit(solution)/shard_map/weights/pallas_call | solution.py:65
  108.2 2.8 %collective-permute-start.38 = (bf16[64,1024]{1,0:T(8,128)(2,1)S(1)}, bf16[64,1024]{1,0:T(8,128)(2,1)S(1)}, u32[]{:S(2)}, u32[]{:S(2)}) collective-permute-start(bf16[64,1024]{1,0:T(8,128)(2,1)S(1)} %get-tuple-element.231), channel_id=1, source_target_pairs={{0,4},{1,5},{2,6},{3,7},{4,0},{5,1},{6,2},{7,3},{8,12},{9,13},{10,... | collective-permute-start | bytes 393224 | tf_op jit(solution)/shard_map/ppermute | solution.py:117
  115.2 8.4 %collective-permute-done.29.refs_1_ = bf16[64,1024]{1,0:T(8,128)(2,1)S(1)} collective-permute-done((bf16[64,1024]{1,0:T(8,128)(2,1)S(1)}, bf16[64,1024]{1,0:T(8,128)(2,1)S(1)}, u32[]{:S(2)}, u32[]{:S(2)}) %collective-permute-start.29) | collective-permute-done | bytes 131104 | tf_op jit(solution)/shard_map/ppermute | solution.py:117
  126.3 3.6 %tail.1 = (bf16[128,1024]{1,0:T(8,128)(2,1)}, bf16[128,1024]{1,0:T(8,128)(2,1)}, bf16[2080,256]{1,0:T(8,128)(2,1)S(1)}, bf16[2080,256]{1,0:T(8,128)(2,1)S(1)}, f32[8,128]{1,0:T(8,128)S(1)}) custom-call(s32[5]{0:T(128)S(1)} %pad_add_fusion.refs_0_, bf16[64,1024]{1,0:T(8,128)(2,1)S(1)} %get-tuple-element.230.refs_1_, ...), custom_call_target="tpu_custom_call" | custom-call | flops 805306368 | bytes 6291456 | tf_op jit(solution)/shard_map/tail/pallas_call | solution.py:65
  130.0 2.7 %collective-permute-done.41.refs_1_ = bf16[2080,256]{1,0:T(8,128)(2,1)S(1)} collective-permute-done((bf16[2080,256]{1,0:T(8,128)(2,1)S(1)}, bf16[2080,256]{1,0:T(8,128)(2,1)S(1)}, u32[]{:S(2)}, u32[]{:S(2)}) %collective-permute-start.41) | collective-permute-done | bytes 1064992 | tf_op jit(solution)/shard_map/ppermute | solution.py:117
  135.9 5.5 %collective-permute-done.42.refs_2_ = bf16[528,256]{1,0:T(8,128)(2,1)S(1)} collective-permute-done((bf16[528,256]{1,0:T(8,128)(2,1)S(1)}, bf16[528,256]{1,0:T(8,128)(2,1)S(1)}, u32[]{:S(2)}, u32[]{:S(2)}) %collective-permute-start.42) | collective-permute-done | bytes 270368 | tf_op jit(solution)/shard_map/ppermute | solution.py:117
  144.8 3.5 %collective-permute-done.45.refs_3_ = bf16[256,256]{1,0:T(8,128)(2,1)S(1)} collective-permute-done((bf16[256,256]{1,0:T(8,128)(2,1)S(1)}, bf16[256,256]{1,0:T(8,128)(2,1)S(1)}, u32[]{:S(2)}, u32[]{:S(2)}) %collective-permute-start.45) | collective-permute-done | bytes 131104 | tf_op jit(solution)/shard_map/ppermute | solution.py:117
  152.8 2.6 %collective-permute-done.46.refs_1_ = bf16[144,256]{1,0:T(8,128)(2,1)S(1)} collective-permute-done((bf16[144,256]{1,0:T(8,128)(2,1)S(1)}, bf16[144,256]{1,0:T(8,128)(2,1)S(1)}, u32[]{:S(2)}, u32[]{:S(2)}) %collective-permute-start.46) | collective-permute-done | bytes 73760 | tf_op jit(solution)/shard_map/ppermute | solution.py:117
  158.9 3.0 %collective-permute-done.50.refs_3_ = bf16[144,256]{1,0:T(8,128)(2,1)S(1)} collective-permute-done((bf16[144,256]{1,0:T(8,128)(2,1)S(1)}, bf16[144,256]{1,0:T(8,128)(2,1)S(1)}, u32[]{:S(2)}, u32[]{:S(2)}) %collective-permute-start.50) | collective-permute-done | bytes 73760 | tf_op jit(solution)/shard_map/ppermute | solution.py:117
  (142 shorter events, 70.0 us)
Async XLA Ops:
  9.2 9.3 %collective-permute-start.1 = (bf16[128,1024]{1,0:T(8,128)(2,1)S(1)}, bf16[128,1024]{1,0:T(8,128)(2,1)S(1)}, u32[]{:S(2)}, u32[]{:S(2)}) collective-permute-start(bf16[128,1024]{1,0:T(8,128)(2,1)S(1)} %get-tuple-element.138), channel_id=1, source_target_pairs={{0,1},{1,0},{2,3},{3,2},{4,5},{5,4},{6,7},{7,6},{8,9},{9,8},{10,11... | collective-permute-start | bytes 786440 | tf_op jit(solution)/shard_map/ppermute | solution.py:117
  12.2 8.7 %collective-permute-start = (bf16[64,1024]{1,0:T(8,128)(2,1)S(1)}, bf16[64,1024]{1,0:T(8,128)(2,1)S(1)}, u32[]{:S(2)}, u32[]{:S(2)}) collective-permute-start(bf16[64,1024]{1,0:T(8,128)(2,1)S(1)} %get-tuple-element.136), channel_id=1, source_target_pairs={{0,4},{1,5},{2,6},{3,7},{4,0},{5,1},{6,2},{7,3},{8,12},{9,13},{10,... | collective-permute-start | bytes 393224 | tf_op jit(solution)/shard_map/ppermute | solution.py:117
  22.1 9.1 %collective-permute-start.4 = (bf16[64,1024]{1,0:T(8,128)(2,1)S(1)}, bf16[64,1024]{1,0:T(8,128)(2,1)S(1)}, u32[]{:S(2)}, u32[]{:S(2)}) collective-permute-start(bf16[64,1024]{1,0:T(8,128)(2,1)S(1)} %get-tuple-element.145), channel_id=1, source_target_pairs={{0,6},{1,7},{2,4},{3,5},{4,2},{5,3},{6,0},{7,1},{8,14},{9,15},{10,... | collective-permute-start | bytes 393224 | tf_op jit(solution)/shard_map/ppermute | solution.py:117
  34.3 12.9 %collective-permute-start.6 = (bf16[128,1024]{1,0:T(8,128)(2,1)S(1)}, bf16[128,1024]{1,0:T(8,128)(2,1)S(1)}, u32[]{:S(2)}, u32[]{:S(2)}) collective-permute-start(bf16[128,1024]{1,0:T(8,128)(2,1)S(1)} %get-tuple-element.143.refs_1_), channel_id=1, source_target_pairs={{0,8},{8,0},{16,24},{24,16},{1,9},{9,1},{17,25},{25,17},{2,10},{10... | collective-permute-start | bytes 786440 | tf_op jit(solution)/shard_map/ppermute | solution.py:117
  36.3 12.6 %collective-permute-start.7 = (bf16[128,1024]{1,0:T(8,128)(2,1)S(1)}, bf16[128,1024]{1,0:T(8,128)(2,1)S(1)}, u32[]{:S(2)}, u32[]{:S(2)}) collective-permute-start(bf16[128,1024]{1,0:T(8,128)(2,1)S(1)} %get-tuple-element.149.refs_2_), channel_id=1, source_target_pairs={{0,8},{8,0},{16,24},{24,16},{1,9},{9,1},{17,25},{25,17},{2,10},{10... | collective-permute-start | bytes 786440 | tf_op jit(solution)/shard_map/ppermute | solution.py:117
  36.4 13.1 %collective-permute-start.15 = (bf16[128,1024]{1,0:T(8,128)(2,1)S(1)}, bf16[128,1024]{1,0:T(8,128)(2,1)S(1)}, u32[]{:S(2)}, u32[]{:S(2)}) collective-permute-start(bf16[128,1024]{1,0:T(8,128)(2,1)S(1)} %get-tuple-element.149.refs_2_), channel_id=1, source_target_pairs={{0,16},{8,24},{16,0},{24,8},{1,17},{9,25},{17,1},{25,9},{2,18},{10... | collective-permute-start | bytes 786440 | tf_op jit(solution)/shard_map/ppermute | solution.py:117
  37.9 9.3 %collective-permute-start.8 = (bf16[64,1024]{1,0:T(8,128)(2,1)S(1)}, bf16[64,1024]{1,0:T(8,128)(2,1)S(1)}, u32[]{:S(2)}, u32[]{:S(2)}) collective-permute-start(bf16[64,1024]{1,0:T(8,128)(2,1)S(1)} %get-tuple-element.151), channel_id=1, source_target_pairs={{0,4},{1,5},{2,6},{3,7},{4,0},{5,1},{6,2},{7,3},{8,12},{9,13},{10,... | collective-permute-start | bytes 393224 | tf_op jit(solution)/shard_map/ppermute | solution.py:117
  40.1 16.2 %collective-permute-start.11 = (bf16[128,1024]{1,0:T(8,128)(2,1)S(1)}, bf16[128,1024]{1,0:T(8,128)(2,1)S(1)}, u32[]{:S(2)}, u32[]{:S(2)}) collective-permute-start(bf16[128,1024]{1,0:T(8,128)(2,1)S(1)} %collective-permute-done.10.refs_1_), channel_id=1, source_target_pairs={{0,8},{8,0},{16,24},{24,16},{1,9},{9,1},{17,25},{25,17},{2,10},{10... | collective-permute-start | bytes 786440 | tf_op jit(solution)/shard_map/ppermute | solution.py:117
  49.0 14.4 %collective-permute-start.20 = (bf16[128,1024]{1,0:T(8,128)(2,1)S(1)}, bf16[128,1024]{1,0:T(8,128)(2,1)S(1)}, u32[]{:S(2)}, u32[]{:S(2)}) collective-permute-start(bf16[128,1024]{1,0:T(8,128)(2,1)S(1)} %get-tuple-element.168.refs_0_), channel_id=1, source_target_pairs={{0,16},{8,24},{16,0},{24,8},{1,17},{9,25},{17,1},{25,9},{2,18},{10... | collective-permute-start | bytes 786440 | tf_op jit(solution)/shard_map/ppermute | solution.py:117
  49.5 10.1 %collective-permute-start.16 = (bf16[128,1024]{1,0:T(8,128)(2,1)S(1)}, bf16[128,1024]{1,0:T(8,128)(2,1)S(1)}, u32[]{:S(2)}, u32[]{:S(2)}) collective-permute-start(bf16[128,1024]{1,0:T(8,128)(2,1)S(1)} %collective-permute-done.15.refs_1_), channel_id=1, source_target_pairs={{0,8},{8,0},{16,24},{24,16},{1,9},{9,1},{17,25},{25,17},{2,10},{10... | collective-permute-start | bytes 786440 | tf_op jit(solution)/shard_map/ppermute | solution.py:117
  55.3 8.6 %collective-permute-start.18 = (bf16[128,1024]{1,0:T(8,128)(2,1)S(1)}, bf16[128,1024]{1,0:T(8,128)(2,1)S(1)}, u32[]{:S(2)}, u32[]{:S(2)}) collective-permute-start(bf16[128,1024]{1,0:T(8,128)(2,1)S(1)} %get-tuple-element.165.refs_1_), channel_id=1, source_target_pairs={{0,16},{8,24},{16,0},{24,8},{1,17},{9,25},{17,1},{25,9},{2,18},{10... | collective-permute-start | bytes 786440 | tf_op jit(solution)/shard_map/ppermute | solution.py:117
  63.9 11.6 %collective-permute-start.9 = (bf16[256,1024]{1,0:T(8,128)(2,1)S(1)}, bf16[256,1024]{1,0:T(8,128)(2,1)S(1)}, u32[]{:S(2)}, u32[]{:S(2)}) collective-permute-start(bf16[256,1024]{1,0:T(8,128)(2,1)S(1)} %get-tuple-element.155), channel_id=1, source_target_pairs={{0,8},{8,0},{16,24},{24,16},{1,9},{9,1},{17,25},{25,17},{2,10},{10... | collective-permute-start | bytes 1572872 | tf_op jit(solution)/shard_map/ppermute | solution.py:117
  73.3 9.1 %collective-permute-start.17 = (bf16[128,1024]{1,0:T(8,128)(2,1)S(1)}, bf16[128,1024]{1,0:T(8,128)(2,1)S(1)}, u32[]{:S(2)}, u32[]{:S(2)}) collective-permute-start(bf16[128,1024]{1,0:T(8,128)(2,1)S(1)} %get-tuple-element.164), channel_id=1, source_target_pairs={{0,16},{8,24},{16,0},{24,8},{1,17},{9,25},{17,1},{25,9},{2,18},{10... | collective-permute-start | bytes 786440 | tf_op jit(solution)/shard_map/ppermute | solution.py:117
  74.4 13.1 %collective-permute-start.28 = (bf16[128,1024]{1,0:T(8,128)(2,1)S(1)}, bf16[128,1024]{1,0:T(8,128)(2,1)S(1)}, u32[]{:S(2)}, u32[]{:S(2)}) collective-permute-start(bf16[128,1024]{1,0:T(8,128)(2,1)S(1)} %get-tuple-element.188), channel_id=1, source_target_pairs={{0,16},{8,24},{16,0},{24,8},{1,17},{9,25},{17,1},{25,9},{2,18},{10... | collective-permute-start | bytes 786440 | tf_op jit(solution)/shard_map/ppermute | solution.py:117
  75.3 23.1 %collective-permute-start.33 = (bf16[256,1024]{1,0:T(8,128)(2,1)S(1)}, bf16[256,1024]{1,0:T(8,128)(2,1)S(1)}, u32[]{:S(2)}, u32[]{:S(2)}) collective-permute-start(bf16[256,1024]{1,0:T(8,128)(2,1)S(1)} %get-tuple-element.203), channel_id=1, source_target_pairs={{0,8},{8,0},{16,24},{24,16},{1,9},{9,1},{17,25},{25,17},{2,10},{10... | collective-permute-start | bytes 1572872 | tf_op jit(solution)/shard_map/ppermute | solution.py:117
  82.6 8.6 %collective-permute-start.27 = (bf16[64,1024]{1,0:T(8,128)(2,1)S(1)}, bf16[64,1024]{1,0:T(8,128)(2,1)S(1)}, u32[]{:S(2)}, u32[]{:S(2)}) collective-permute-start(bf16[64,1024]{1,0:T(8,128)(2,1)S(1)} %get-tuple-element.187), channel_id=1, source_target_pairs={{0,1},{1,0},{2,3},{3,2},{4,5},{5,4},{6,7},{7,6},{8,9},{9,8},{10,11... | collective-permute-start | bytes 393224 | tf_op jit(solution)/shard_map/ppermute | solution.py:117
  89.2 9.2 %collective-permute-start.35 = (bf16[128,1024]{1,0:T(8,128)(2,1)S(1)}, bf16[128,1024]{1,0:T(8,128)(2,1)S(1)}, u32[]{:S(2)}, u32[]{:S(2)}) collective-permute-start(bf16[128,1024]{1,0:T(8,128)(2,1)S(1)} %get-tuple-element.205), channel_id=1, source_target_pairs={{0,16},{8,24},{16,0},{24,8},{1,17},{9,25},{17,1},{25,9},{2,18},{10... | collective-permute-start | bytes 786440 | tf_op jit(solution)/shard_map/ppermute | solution.py:117
  90.3 13.6 %collective-permute-start.34 = (bf16[128,1024]{1,0:T(8,128)(2,1)S(1)}, bf16[128,1024]{1,0:T(8,128)(2,1)S(1)}, u32[]{:S(2)}, u32[]{:S(2)}) collective-permute-start(bf16[128,1024]{1,0:T(8,128)(2,1)S(1)} %get-tuple-element.204), channel_id=1, source_target_pairs={{0,16},{8,24},{16,0},{24,8},{1,17},{9,25},{17,1},{25,9},{2,18},{10... | collective-permute-start | bytes 786440 | tf_op jit(solution)/shard_map/ppermute | solution.py:117
  106.2 9.1 %collective-permute-start.32 = (bf16[64,1024]{1,0:T(8,128)(2,1)S(1)}, bf16[64,1024]{1,0:T(8,128)(2,1)S(1)}, u32[]{:S(2)}, u32[]{:S(2)}) collective-permute-start(bf16[64,1024]{1,0:T(8,128)(2,1)S(1)} %get-tuple-element.197), channel_id=1, source_target_pairs={{0,6},{1,7},{2,4},{3,5},{4,2},{5,3},{6,0},{7,1},{8,14},{9,15},{10,... | collective-permute-start | bytes 393224 | tf_op jit(solution)/shard_map/ppermute | solution.py:117
  108.0 15.6 %collective-permute-start.29 = (bf16[64,1024]{1,0:T(8,128)(2,1)S(1)}, bf16[64,1024]{1,0:T(8,128)(2,1)S(1)}, u32[]{:S(2)}, u32[]{:S(2)}) collective-permute-start(bf16[64,1024]{1,0:T(8,128)(2,1)S(1)} %get-tuple-element.192), channel_id=1, source_target_pairs={{0,4},{1,5},{2,6},{3,7},{4,0},{5,1},{6,2},{7,3},{8,12},{9,13},{10,... | collective-permute-start | bytes 393224 | tf_op jit(solution)/shard_map/ppermute | solution.py:117
  108.2 18.2 %collective-permute-start.38 = (bf16[64,1024]{1,0:T(8,128)(2,1)S(1)}, bf16[64,1024]{1,0:T(8,128)(2,1)S(1)}, u32[]{:S(2)}, u32[]{:S(2)}) collective-permute-start(bf16[64,1024]{1,0:T(8,128)(2,1)S(1)} %get-tuple-element.231), channel_id=1, source_target_pairs={{0,4},{1,5},{2,6},{3,7},{4,0},{5,1},{6,2},{7,3},{8,12},{9,13},{10,... | collective-permute-start | bytes 393224 | tf_op jit(solution)/shard_map/ppermute | solution.py:117
  110.9 15.4 %collective-permute-start.39 = (bf16[64,1024]{1,0:T(8,128)(2,1)S(1)}, bf16[64,1024]{1,0:T(8,128)(2,1)S(1)}, u32[]{:S(2)}, u32[]{:S(2)}) collective-permute-start(bf16[64,1024]{1,0:T(8,128)(2,1)S(1)} %get-tuple-element.232), channel_id=1, source_target_pairs={{0,2},{1,3},{2,0},{3,1},{4,6},{5,7},{6,4},{7,5},{8,10},{9,11},{10,... | collective-permute-start | bytes 393224 | tf_op jit(solution)/shard_map/ppermute | solution.py:117
  111.0 15.3 %collective-permute-start.40 = (bf16[64,1024]{1,0:T(8,128)(2,1)S(1)}, bf16[64,1024]{1,0:T(8,128)(2,1)S(1)}, u32[]{:S(2)}, u32[]{:S(2)}) collective-permute-start(bf16[64,1024]{1,0:T(8,128)(2,1)S(1)} %get-tuple-element.233), channel_id=1, source_target_pairs={{0,6},{1,7},{2,4},{3,5},{4,2},{5,3},{6,0},{7,1},{8,14},{9,15},{10,... | collective-permute-start | bytes 393224 | tf_op jit(solution)/shard_map/ppermute | solution.py:117
  134.4 8.7 %collective-permute-start.44 = (bf16[512,256]{1,0:T(8,128)(2,1)S(1)}, bf16[512,256]{1,0:T(8,128)(2,1)S(1)}, u32[]{:S(2)}, u32[]{:S(2)}) collective-permute-start(bf16[512,256]{1,0:T(8,128)(2,1)S(1)} %get-tuple-element.247), channel_id=1, source_target_pairs={{0,1},{1,0},{2,3},{3,2},{4,5},{5,4},{6,7},{7,6},{8,9},{9,8},{10,11... | collective-permute-start | bytes 786440 | tf_op jit(solution)/shard_map/ppermute | solution.py:117
  (40 other events, 348.7 us)

commit v3 on v2

v3 whole, which is shorter than its diff:
```python
import functools

import jax
import jax.numpy as jnp
from jax import lax
from jax.experimental import pallas as pl
from jax.experimental.pallas import tpu as pltpu
from jax.sharding import PartitionSpec as P

GELU_C = 0.7978845608028654
GELU_A = 0.044715
EPSILON = 1e-06
BF = jnp.bfloat16
F32 = jnp.float32
LANES = 128
TILE = 16
MIB = 1024 * 1024
WAIT = 20 * 10**9

NN = (((1,), (0,)), ((), ()))
NT = (((1,), (1,)), ((), ()))
TN = (((0,), (0,)), ((), ()))

VMEM = pl.BlockSpec(memory_space=pltpu.VMEM)
ANY = pl.BlockSpec(memory_space=pl.ANY)
HBM = pl.BlockSpec(memory_space=pltpu.HBM)
DMA = pltpu.SemaphoreType.DMA


def mm(a, b, dims=NN):
    return lax.dot_general(a, b, dims, preferred_element_type=F32)


def shape(dims, dtype=BF):
    return jax.ShapeDtypeStruct(dims, dtype)


def gelu_pair(preact):
    square = preact * preact
    tangent = jnp.tanh(GELU_C * (preact + GELU_A * (square * preact)))
    half = 0.5 * (1.0 + tangent)
    derivative = half + (0.5 * GELU_C) * preact * (1.0 - tangent * tangent) * (
        1.0 + 3.0 * GELU_A * square
    )
    return preact * half, derivative


class Line:
    def __init__(self):
        self.last = None

    def call(self, body, outs, args, specs=None, out_specs=None, scratch=(), flops=0, vmem=8 * MIB, name=None):
        args, specs = list(args), list(specs) if specs is not None else [VMEM] * len(args)
        out_specs = list(out_specs) if out_specs is not None else [VMEM] * len(outs)
        count, given = len(args), len(outs)
        if self.last is not None:
            args.append(self.last)
            specs.append(ANY)

        def kernel(*refs):
            results = refs[len(args) :]
            results[given][...] = jnp.zeros((8, LANES), F32)
            body(*refs[:count], *results[:given], *results[given + 1 :])

        *results, self.last = pl.pallas_call(
            kernel,
            out_shape=[*outs, shape((8, LANES), F32)],
            in_specs=specs,
            out_specs=[*out_specs, VMEM],
            scratch_shapes=scratch,
            compiler_params=pltpu.CompilerParams(vmem_limit_bytes=vmem),
            cost_estimate=pl.CostEstimate(flops=flops, bytes_accessed=0, transcendentals=0),
            name=name,
        )(*args)
        return results

    def move(self, *outputs, flops=0, name="move"):
        arrays, places = [], {}
        aligned = True
        for pieces in outputs:
            for rows, terms in pieces:
                aligned = aligned and rows % TILE == 0
                for array, first in terms:
                    aligned = aligned and first % TILE == 0
                    if id(array) not in places:
                        places[id(array)] = len(arrays)
                        arrays.append(array)
        width = arrays[0].shape[1]
        if not aligned:
            return [
                jnp.concatenate([
                    added(*[a[f : f + rows] for a, f in terms]) if len(terms) > 1 else terms[0][0][terms[0][1] : terms[0][1] + rows]
                    for rows, terms in pieces
                ])
                for pieces in outputs
            ]

        def body(*refs):
            for pieces, out in zip(outputs, refs[len(arrays) :]):
                at = 0
                for rows, terms in pieces:
                    parts = [refs[places[id(a)]][f : f + rows, :] for a, f in terms]
                    if len(parts) > 1:
                        parts = [functools.reduce(jnp.add, [p.astype(F32) for p in parts]).astype(BF)]
                    out[at : at + rows, :] = parts[0]
                    at += rows

        outs = [shape((sum(rows for rows, _ in pieces), width)) for pieces in outputs]
        return self.call(body, outs, arrays, flops=flops, name=name)


def added(*terms):
    return functools.reduce(jnp.add, [t.astype(F32) for t in terms]).astype(BF)


def swap(x, axis, mask):
    return lax.ppermute(x, axis, [(i, i ^ mask) for i in range(lax.axis_size(axis))])


def hot_rows(ids_ref, rel_to, count):
    tok = ids_ref.shape[1]
    rows = lax.broadcasted_iota(jnp.int32, (count, tok), 0)
    return [(rows == (ids_ref[k : k + 1, :] ^ rel_to)).astype(F32) for k in range(2)]


def at_rows(places, total):
    tok = places[0].shape[1]
    rows = lax.broadcasted_iota(jnp.int32, (total, tok), 0)
    return functools.reduce(jnp.add, [(rows == p).astype(F32) for p in places]).astype(BF)


def onehot(column, width):
    lanes = lax.broadcasted_iota(jnp.int32, (column.shape[0], width), 1)
    return (lanes == column).astype(F32)


def on_device(tokens, context, w_out, w_router, expert_ids, w_in, w_down, cotangent):
    tok, width = tokens.shape
    experts = lax.axis_size("expert")
    dp = lax.axis_size("dp")
    far = dp // 2
    cap = 2 * tok // experts
    slots = 2 * tok
    hidden = w_in.shape[2]
    masks = [0, 2, 1, 3]
    low = experts // len(masks)
    shift = low.bit_length() - 1
    chunks = [[0, 1], [2, 3]]
    size = low * cap
    ids_t = expert_ids.T
    router_t = w_router.T
    weight_in, weight_down = w_in[0], w_down[0]
    per = width // experts
    part = width // dp
    line = Line()

    def order(rel):
        high = rel >> shift
        return (high >> 1) | ((high & 1) << 1), rel & (low - 1)

    def head_body(ids_hbm, cot_hbm, tok_hbm, ctx_hbm, w_out_hbm, *refs):
        outs, copies = refs[: low + 8], refs[low + 8 :]
        lows, (placed_ref, resid_ref, inv_ref, normed_ref), sends = outs[:low], outs[low : low + 4], outs[low + 4 :]
        held, sems = copies[:5], copies[5]
        me = lax.axis_index("expert")
        loads = [pltpu.make_async_copy(src, dst, sems.at[i]) for i, (src, dst) in enumerate(
            zip((ids_hbm, ctx_hbm, w_out_hbm, tok_hbm, cot_hbm), held))]
        for load in loads:
            load.start()
        ids_ref, ctx_ref, w_out_ref, tok_ref, cot_ref = held
        loads[0].wait()
        rows = lax.broadcasted_iota(jnp.int32, (tok, tok), 0)
        cols = lax.broadcasted_iota(jnp.int32, (tok, tok), 1)
        upper = (rows < cols).astype(BF)
        hot = hot_rows(ids_ref, me, experts)
        before = [mm(h.astype(BF), upper) for h in hot]
        first = jnp.sum(hot[0], axis=1, keepdims=True)
        rank = [jnp.sum(before[0] * hot[0], axis=0, keepdims=True),
                jnp.sum((before[1] + first) * hot[1], axis=0, keepdims=True)]
        places, spots = [], []
        for k in range(2):
            block, lower = order(ids_ref[k : k + 1, :] ^ me)
            places.append((block * low + lower) * cap + rank[k].astype(jnp.int32))
            placed_ref[k : k + 1, :] = places[k]
            spots.append((lower * len(masks) + block) * cap + rank[k].astype(jnp.int32))
        loads[1].wait()
        loads[2].wait()
        attn = mm(ctx_ref[...], w_out_ref[...])
        loads[3].wait()
        resid = (tok_ref[...].astype(F32) + attn).astype(BF)
        resid_ref[...] = resid
        resid_f = resid.astype(F32)
        inv = lax.rsqrt(jnp.mean(resid_f * resid_f, axis=1, keepdims=True) + EPSILON)
        inv_ref[...] = inv
        normed = (resid_f * inv).astype(BF)
        normed_ref[...] = normed
        moved = mm(at_rows(places, slots), normed).astype(BF)
        for c in range(len(masks)):
            sends[c][...] = moved[c * size : (c + 1) * size, :]
        loads[4].wait()
        moved = mm(at_rows(spots, slots), cot_ref[...]).astype(BF)
        each = slots // low
        for m in range(low):
            lows[m][...] = moved[m * each : (m + 1) * each, :]

    outs = line.call(
        head_body,
        [shape((slots // low, width))] * low + [shape((2, tok), jnp.int32)]
        + [shape((tok, width)), shape((tok, 1), F32), shape((tok, width))] + [shape((size, width))] * 4,
        (ids_t, cotangent, tokens, context, w_out), specs=[HBM] * 5,
        scratch=[pltpu.VMEM((2, tok), jnp.int32), pltpu.VMEM((tok, width), BF), pltpu.VMEM((width, width), BF),
                 pltpu.VMEM((tok, width), BF), pltpu.VMEM((tok, width), BF), DMA((5,))],
        vmem=53 * MIB, name="head")
    cot_low, (placed, resid, inv, normed), sends = outs[:low], outs[low : low + 4], outs[low + 4 :]
    cot_low = [cot_low[0]] + [swap(cot_low[m], "expert", m) for m in range(1, low)]
    norm_high = [sends[0]] + [swap(sends[c], "expert", masks[c] * low) for c in (1, 2, 3)]

    cot_high = line.move(*[[(cap, [(cot_low[m], c * cap)]) for m in range(low)] for c in range(4)], name="pack_cot_z")
    cot_high = [cot_high[0]] + [swap(cot_high[c], "expert", masks[c] * low) for c in (1, 2, 3)]

    norm_low = []
    if low > 1:
        lows = line.move(*[[(cap, [(norm_high[c], m * cap)]) for c in range(4)] for m in range(1, low)], name="pack_norm_y")
        norm_low = [swap(x, "expert", m + 1) for m, x in enumerate(lows)]
    norm_own = line.move(
        [(cap, [piece]) for c in range(4) for piece in [(norm_high[c], 0)] + [(x, c * cap) for x in norm_low]],
        name="pack_norm_x")[0]
    norm_far = swap(norm_own, "dp", far)
    norm_core = swap(norm_own, "dp", 1)
    cot_own = line.move([(size, [(x, 0)]) for x in cot_high], flops=WAIT, name="pack_cot_x")[0]
    cot_far = swap(cot_own, "dp", far)
    cot_core = swap(cot_own, "dp", 1)

    block = 256 if hidden % 256 == 0 else hidden

    def forward(parts, pieces):
        rows = sum(x.shape[0] for x in parts)
        piece = rows // 2 // pieces

        def body(*refs):
            ins = refs[: len(parts)]
            router_ref, in_ref, down_ref, rows_hbm, act_hbm, der_ref, gate_ref, keep_ref = refs[len(parts) : len(parts) + 8]
            sends, (rows_ref, act_ref, total, sems) = refs[len(parts) + 8 : -4], refs[-4:]
            at = 0
            for ref in ins:
                rows_ref[at : at + ref.shape[0], :] = ref[...]
                at += ref.shape[0]
            stores = [pltpu.make_async_copy(rows_ref, rows_hbm, sems.at[0]), pltpu.make_async_copy(act_ref, act_hbm, sems.at[1])]
            stores[0].start()
            for j in range(hidden // block):
                at = slice(j * block, (j + 1) * block)
                value, derivative = gelu_pair(mm(rows_ref[...], in_ref[:, at]))
                act = value.astype(BF)
                act_ref[:, at] = act
                der_ref[:, at] = derivative.astype(BF)
                term = mm(act, down_ref[at, :])
                total[...] = term if j == 0 else total[...] + term
            stores[1].start()
            keep_ref[...] = total[: rows // 2, :].astype(BF)
            for i in range(pieces):
                sends[i][...] = total[rows // 2 + i * piece : rows // 2 + (i + 1) * piece, :].astype(BF)
            logits = mm(rows_ref[...], router_ref[...], NT)
            lanes = lax.broadcasted_iota(jnp.int32, logits.shape, 1)
            picked = jnp.sum(jnp.where(lanes == lax.axis_index("expert"), logits, 0.0), axis=1, keepdims=True)
            gate_ref[...] = jax.nn.sigmoid(picked)
            for store in stores:
                store.wait()

        *results, = line.call(
            body,
            [shape((rows, width)), shape((rows, hidden)), shape((rows, hidden)), shape((rows, 1), F32),
             shape((rows // 2, width))] + [shape((piece, width))] * pieces,
            (*parts, router_t, weight_in, weight_down),
            out_specs=[HBM] * 2 + [VMEM] * (3 + pieces),
            scratch=[pltpu.VMEM((rows, width), BF), pltpu.VMEM((rows, hidden), BF), pltpu.VMEM((rows, width), F32), DMA((2,))],
            vmem=20 * MIB, name="forward")
        return (*results[:5], results[5:])

    def backward(parts, gate, der, pieces):
        rows = sum(x.shape[0] for x in parts)
        piece = rows // 2 // pieces

        def body(*refs):
            ins, refs = refs[: len(parts)], refs[len(parts) :]
            gate_ref, der_ref, in_ref, down_ref, grads_hbm, pre_hbm, keep_ref = refs[:7]
            sends, (grads_ref, pre_ref, total, sems) = refs[7 : 7 + pieces], refs[7 + pieces :]
            first = 0
            for ref in ins:
                at = slice(first, first + ref.shape[0])
                first += ref.shape[0]
                grads_ref[at, :] = (gate_ref[at, :] * ref[...].astype(F32)).astype(BF)
            stores = [pltpu.make_async_copy(grads_ref, grads_hbm, sems.at[0]), pltpu.make_async_copy(pre_ref, pre_hbm, sems.at[1])]
            stores[0].start()
            for j in range(hidden // block):
                at = slice(j * block, (j + 1) * block)
                act_grad = mm(grads_ref[...], down_ref[at, :], NT)
                pre = (act_grad * der_ref[:, at].astype(F32)).astype(BF)
                pre_ref[:, at] = pre
                term = mm(pre, in_ref[:, at], NT)
                total[...] = term if j == 0 else total[...] + term
            stores[1].start()
            keep_ref[...] = total[: rows // 2, :].astype(BF)
            for i in range(pieces):
                sends[i][...] = total[rows // 2 + i * piece : rows // 2 + (i + 1) * piece, :].astype(BF)
            for store in stores:
                store.wait()

        grads, pre, keep, *sends = line.call(
            body,
            [shape((rows, width)), shape((rows, hidden)), shape((rows // 2, width))] + [shape((piece, width))] * pieces,
            (*parts, gate, der, weight_in, weight_down),
            out_specs=[HBM] * 2 + [VMEM] * (1 + pieces),
            scratch=[pltpu.VMEM((rows, width), BF), pltpu.VMEM((rows, hidden), BF), pltpu.VMEM((rows, width), F32), DMA((2,))],
            vmem=20 * MIB, name="backward")
        return grads, pre, keep, sends

    half = slots // 2

    def relay(x):
        whole, *halves = line.move([(slots, [(x, 0)])], *[[(half, [(x, i * half)])] for i in range(2)], name="relay")
        return [whole] + [swap(h, "dp", 1) for h in halves]

    rows_n, act_n, der_n, gate_n, keep_n, send_n = forward([norm_own, norm_core], 1)
    near_out = swap(send_n[0], "dp", 1)
    rows_f, act_f, der_f, gate_f, keep_f, send_f = forward(relay(norm_far), 2)
    core_out = [swap(x, "dp", 1) for x in send_f]
    grads_n, pre_n, ikeep_n, isend_n = backward([cot_own, cot_core], gate_n, der_n, 1)
    near_in = swap(isend_n[0], "dp", 1)
    far_out = line.move([(half, [(keep_f, i * half), (core_out[i], 0)]) for i in range(2)], name="sum_core_out")[0]
    far_out = swap(far_out, "dp", far)
    grads_f, pre_f, ikeep_f, isend_f = backward(relay(cot_far), gate_f, der_f, 2)
    core_in = [swap(x, "dp", 1) for x in isend_f]
    far_in = line.move(*[[(half, [(ikeep_f, i * half), (core_in[i], 0)])] for i in range(2)], name="sum_core_in")
    far_in = [swap(x, "dp", far) for x in far_in]

    def weight_grad(lefts, rights):
        left, right = lefts[0].shape[1], rights[0].shape[1]
        tile = 256 if left % 256 == 0 else left

        def body(*refs):
            count = len(lefts) + len(rights)
            out_hbm, left_ref, right_ref, result, sems = refs[count:]
            loads = []
            for group, ref in ((refs[: len(lefts)], left_ref), (refs[len(lefts) : count], right_ref)):
                at = 0
                for src in group:
                    loads.append(pltpu.make_async_copy(src, ref.at[at : at + src.shape[0], :], sems.at[len(loads)]))
                    loads[-1].start()
                    at += src.shape[0]
            for load in loads:
                load.wait()
            stores = []
            for i in range(left // tile):
                at = slice(i * tile, (i + 1) * tile)
                result[at, :] = mm(left_ref[:, at], right_ref[...], TN).astype(BF)
                stores.append(pltpu.make_async_copy(result.at[at, :], out_hbm.at[at, :], sems.at[count + i]))
                stores[-1].start()
            for store in stores:
                store.wait()

        return line.call(
            body, [shape((left, right))], (*lefts, *rights), specs=[HBM] * (len(lefts) + len(rights)), out_specs=[HBM],
            scratch=[pltpu.VMEM((4 * slots, left), BF), pltpu.VMEM((4 * slots, right), BF), pltpu.VMEM((left, right), BF),
                     DMA((len(lefts) + len(rights) + left // tile,))],
            vmem=20 * MIB, name="weights")[0]

    grad_w_down = weight_grad((act_n, act_f), (grads_n, grads_f))

    quarter = slots // 4
    sums = line.move(
        *[[(quarter, [(x, c * quarter) for x in (keep_n, near_out, far_out)])] for c in range(4)], name="sum_x_out")
    out_high = [swap(x, "expert", masks[c] * low) if masks[c] else x for c, x in enumerate(sums)]

    def gather_in(i):
        terms = lambda at, rows: (rows, [(ikeep_n, i * half + at), (near_in, i * half + at), (far_in[i], at)])
        total, *lows = line.move(
            [terms(0, half)], *[[terms(j * size + m * cap, cap) for j in range(2)] for m in range(1, low)], name="sum_x_in")
        return total, [swap(x, "expert", m + 1) for m, x in enumerate(lows)]

    def send_back(i, total, lows):
        blocks = line.move(
            *[[(cap, [(total, j * size)])] + [(cap, [(x, j * cap)]) for x in lows] for j in range(2)], name="pack_back_z")
        return [swap(b, "expert", masks[c] * low) if masks[c] else b for c, b in zip(chunks[i], blocks)]

    total_a = gather_in(0)
    total_b = gather_in(1)
    out_low = []
    if low > 1:
        out_low = line.move(*[[(cap, [(x, m * cap)]) for x in out_high] for m in range(1, low)], name="pack_out_y")
    back_in = send_back(0, *total_a)
    back_in += send_back(1, *total_b)
    if low > 1:
        out_low = line.move(*[[(4 * cap, [(x, 0)])] for x in out_low], name="pass_out_y")
        out_low = [swap(x, "expert", m + 1) for m, x in enumerate(out_low)]
    grad_w_in = weight_grad((rows_n, rows_f), (pre_n, pre_f))
    back_out = line.move(
        [(cap, [piece]) for c in range(4) for piece in [(out_high[c], 0)] + [(x, c * cap) for x in out_low]],
        name="pack_out")

    spare = -(-experts // TILE) * TILE
    span = width + spare

    def combine_body(*refs):
        back_ref, placed_ref, ids_ref, router_ref, resid_ref, cot_ref, normed_ref, out_ref, table_ref, local_ref = refs
        logits = mm(router_ref[...], normed_ref[...], NT)
        gates = [jax.nn.sigmoid(jnp.sum(logits * h, axis=0, keepdims=True)) for h in hot_rows(ids_ref, 0, experts)]
        ids_f = ids_ref[...].astype(F32)
        cols = jnp.concatenate(gates + [ids_f] * 3, axis=0).T
        held = back_ref[...]
        cot_f = cot_ref[...].astype(F32)
        total = resid_ref[...].astype(F32)
        table = jnp.zeros((tok, LANES), F32)
        for k in range(2):
            gate = cols[:, k : k + 1]
            taken = mm(at_rows([placed_ref[k : k + 1, :]], slots), held, TN)
            total = total + gate * taken
            logit = jnp.sum(cot_f * taken, axis=1, keepdims=True) * gate * (1.0 - gate)
            table = table + onehot(cols[:, 2 + k : 3 + k].astype(jnp.int32), LANES) * logit
        out_ref[...] = total.astype(BF)
        table = table.astype(BF)
        table_ref[...] = table
        local_ref[...] = mm(table, normed_ref[...], TN)[:spare, :].astype(BF)

    output, table, local_router = line.call(
        combine_body, [shape((tok, width)), shape((tok, LANES)), shape((spare, width))],
        (*back_out, placed, ids_t, router_t, resid, cotangent, normed),
        name="combine")

    def tail_body(*refs):
        me, mine = lax.axis_index("expert"), lax.axis_index("dp")
        backs = refs[:4]
        (placed_ref, table_ref, router_ref, resid_ref, inv_ref, local_ref, cot_hbm, w_out_hbm, ctx_hbm,
         grad_ref, grad_ctx_ref, keep_ref, send_ref, cot_ref, w_out_ref, ctx_ref, turned, sems) = refs[4:]
        loads = [pltpu.make_async_copy(src, dst, sems.at[i]) for i, (src, dst) in enumerate(
            ((cot_hbm, cot_ref), (ctx_hbm, ctx_ref), (w_out_hbm, w_out_ref)))]
        for load in loads:
            load.start()
        held = jnp.concatenate([b[...] for b in backs], axis=0)
        where = at_rows([placed_ref[k : k + 1, :] for k in range(2)], slots)
        normed_grad = mm(where, held, TN) + mm(table_ref[:, :experts], router_ref[...])
        resid_f = resid_ref[...].astype(F32)
        inv_col = inv_ref[...]
        mean_term = jnp.mean(normed_grad * resid_f, axis=1, keepdims=True)
        loads[0].wait()
        grad = (cot_ref[...].astype(F32) + inv_col * normed_grad
                - (inv_col * inv_col * inv_col * mean_term) * resid_f).astype(BF)
        grad_ref[...] = grad
        outs = [(send_ref if m % 2 else keep_ref, (m // 2) * span) for m in range(dp)]
        for m, (out, base) in enumerate(outs):
            at = pl.ds(pl.multiple_of((mine ^ m) * part, LANES), part)
            turned[:, m * part : (m + 1) * part] = grad_ref[:, at]
            out[base + width : base + span, :] = local_ref[:, at]
        loads[1].wait()
        tile = max(per, LANES)
        for i in range(width // tile):
            block = mm(ctx_ref[:, i * tile : (i + 1) * tile], turned[...], TN).astype(BF)
            for j in range(tile // per):
                spot, lower = order((i * (tile // per) + j) ^ me)
                to = (spot * low + lower) * per
                for m, (out, base) in enumerate(outs):
                    out[pl.ds(pl.multiple_of(base + to, TILE), per), :] = (
                        block[j * per : (j + 1) * per, m * part : (m + 1) * part])
        loads[2].wait()
        grad_ctx_ref[...] = mm(grad, w_out_ref[...], NT).astype(BF)

    grad_tokens, grad_context, keep, send = line.call(
        tail_body,
        [shape((tok, width)), shape((tok, width)), shape((far * span, part)), shape((far * span, part))],
        (*back_in, placed, table, router_t, resid, inv, local_router, cotangent, w_out, context),
        specs=[VMEM] * 10 + [HBM] * 3,
        scratch=[pltpu.VMEM((tok, width), BF), pltpu.VMEM((width, width), BF), pltpu.VMEM((tok, width), BF),
                 pltpu.VMEM((tok, width), BF), DMA((3,))],
        vmem=16 * MIB, name="tail")

    core = swap(send, "dp", 1)
    spot = lambda d, c, m: d * span + (c * low + m) * per
    two = lambda first: [(keep, first), (core, first)]
    group = [(spare, two(width))]
    sum_x = line.move(
        [(2 * low * per, two(span)), (spare, two(span + width))],
        *[[(per, two(spot(d, c, m))) for d in range(2) for c in (2, 3)] for m in range(1, low)], name="reduce_core")
    first_x = swap(sum_x[0], "dp", far)
    second_low = [swap(x, "expert", m + 1) for m, x in enumerate(sum_x[1:])]
    first = line.move(
        *[[(per, two(spot(0, c, m)) + [(first_x, (c * low + m) * per)]) for c in (0, 1)]
          + [(spare, two(width) + [(first_x, 2 * low * per)])] for m in range(low)], name="reduce_x")
    first_low = [swap(x, "expert", m) for m, x in enumerate(first) if m]
    second = line.move(
        *[[(per, two(spot(d, c, 0)) + [(x, (d * 2 + i) * per) for x in second_low]) for i, c in enumerate((2, 3))]
          for d in (1, 0)], name="reduce_y")
    second_x = swap(second[0], "dp", far)
    router_terms = [(x, 2 * per) for x in [first[0], *first_low]]
    blocks = line.move(
        *[[(per, [(x, c * per) for x in [first[0], *first_low]]), (spare, router_terms)] for c in (0, 1)],
        *[[(per, [(second[1], c * per), (second_x, c * per)]), (spare, router_terms)] for c in (0, 1)], name="reduce_xy")
    blocks = [blocks[0]] + [swap(blocks[c], "expert", masks[c] * low) for c in (1, 2, 3)]
    own = line.move([(per + spare, [(b, 0) for b in blocks])], name="reduce_z")[0]
    quarters = [own] + [swap(own, "dp", m) for m in range(1, dp)]

    def final_body(*refs):
        me, mine = lax.axis_index("expert"), lax.axis_index("dp")
        out_ref, router_ref = refs[dp:]
        for m in range(dp):
            at = pl.ds(pl.multiple_of((mine ^ m) * part, LANES), part)
            out_ref[:, at] = refs[m][:per, :].astype(F32)
            table = refs[m][per:, :].astype(F32)
            rows = lax.broadcasted_iota(jnp.int32, table.shape, 0)
            router_ref[:, at] = jnp.sum(jnp.where(rows == me, table, 0.0), axis=0, keepdims=True)

    grad_w_out, grad_w_router = line.call(
        final_body, [shape((per, width), F32), shape((1, width), F32)], quarters, name="final")

    return (
        output,
        grad_tokens,
        grad_context,
        grad_w_out,
        grad_w_router.reshape(width, 1),
        grad_w_in.reshape(1, width, hidden),
        grad_w_down.reshape(1, hidden, width),
    )


def solution(mesh):
    split = P(("dp", "expert"), None)
    return jax.shard_map(
        on_device,
        mesh=mesh,
        in_specs=(split, split, P(), P(), split, P("expert", None, "dp"), P("expert", "dp", None), split),
        out_specs=(split, split, split, P("expert", None), P(None, "expert"), P("expert", None, "dp"),
                   P("expert", "dp", None)),
        check_vma=False,
    )
```

time: 165 us -> 143 us (0.87)
  waiting for transfers between devices: 69.1 us -> 55.3 us
  local copies, waits for them, and re-layouts: 5.86 us -> 2.86 us
  starting transfers between devices: 51.9 us -> 49.2 us
  Pallas kernels: 36.6 us -> 34.1 us
    ppermute x52 -> x45, waiting for transfers between devices: 69.1 us -> 55.3 us  [swap(): lax.ppermute(x, axis, [(i, i ^ mask) for i in range(lax.axis_size(axis))])]
    unnamed x24 -> x18, local copies, waits for them, and re-layouts: 5.86 us -> 2.86 us
    ppermute x52 -> x45, starting transfers between devices: 51.9 us -> 49.2 us  [swap(): lax.ppermute(x, axis, [(i, i ^ mask) for i in range(lax.axis_size(axis))])]
    pallas_call x36 -> x31, Pallas kernels: 36.6 us -> 34.1 us  [call(): pl.pallas_call(kernel, out_shape=[*outs, shape((8, LANES), F32)], in_spec...]
  transfers between devices with their start and end apart: 52 -> 45, of which waited for: 26 -> 23; matrix products, arithmetic and copies ran while one was open for 0% -> 0% of each run, Pallas kernels for 17% -> 18%
where the time goes in v3:
time: 143 us; the launch traced here: 142 us
  waiting for transfers between devices  55.3 us (39%)
  starting transfers between devices  49.2 us (34%)
  Pallas kernels  34.1 us (24%)
  local copies, waits for them, and re-layouts  2.86 us (2%)
    ppermute x45, waiting for transfers between devices, swap(): lax.ppermute(x, axis, [(i, i ^ mask) for i in range(lax.axis_size(axis))])  55.3 us
    ppermute x45, starting transfers between devices, swap(): lax.ppermute(x, axis, [(i, i ^ mask) for i in range(lax.axis_size(axis))])  49.2 us
    pallas_call x31, Pallas kernels, call(): pl.pallas_call(kernel, out_shape=[*outs, shape((8, LANES), F32)], in_spec...  34.1 us
  transfers between devices with their start and end apart: 45, of which 23 were waited for; matrix products, arithmetic and copies ran while one was open for 0% of the time, Pallas kernels for 18%

profile of v3, /device:TPU:0, one launch (start us, length us, event | category | flops | bytes accessed | tf_op | source)
XLA Modules:
  0.0 142.4 jit_solution(14123866649537033309)
XLA Ops:
  1.3 3.6 %head.1 = (bf16[128,1024]{1,0:T(8,128)(2,1)S(1)}, bf16[128,1024]{1,0:T(8,128)(2,1)}, s32[2,128]{1,0:T(2,128)S(1)}, bf16[128,1024]{1,0:T(8,128)(2,1)}, f32[128,1]...) custom-call(s32[2,128]{1,0:T(2,128)S(1)} %bitcast.19, ...), custom_call_target="tpu_custom_call" | custom-call | tf_op jit(solution)/shard_map/head/pallas_call | solution.py:65
  5.0 3.0 %collective-permute-start.3 = (bf16[128,1024]{1,0:T(8,128)(2,1)}, bf16[128,1024]{1,0:T(8,128)(2,1)S(1)}, u32[]{:S(2)}, u32[]{:S(2)}) collective-permute-start(bf16[128,1024]{1,0:T(8,128)(2,1)} %get-tuple-element.127), channel_id=1, source_target_pairs={{0,1},{1,0},{2,3},{3,2},{4,5},{5,4},{6,7},{7,6},{8,9},{9,8},{10,11... | collective-permute-start | bytes 786440 | tf_op jit(solution)/shard_map/ppermute | solution.py:117
  8.0 2.6 %collective-permute-start = (bf16[64,1024]{1,0:T(8,128)(2,1)S(1)}, bf16[64,1024]{1,0:T(8,128)(2,1)S(1)}, u32[]{:S(2)}, u32[]{:S(2)}) collective-permute-start(bf16[64,1024]{1,0:T(8,128)(2,1)S(1)} %get-tuple-element.123), channel_id=1, source_target_pairs={{0,4},{1,5},{2,6},{3,7},{4,0},{5,1},{6,2},{7,3},{8,12},{9,13},{10,... | collective-permute-start | bytes 393224 | tf_op jit(solution)/shard_map/ppermute | solution.py:117
  14.5 6.1 %collective-permute-done.refs_1_.refs_2_ = bf16[64,1024]{1,0:T(8,128)(2,1)S(1)} collective-permute-done((bf16[64,1024]{1,0:T(8,128)(2,1)S(1)}, bf16[64,1024]{1,0:T(8,128)(2,1)S(1)}, u32[]{:S(2)}, u32[]{:S(2)}) %collective-permute-start) | collective-permute-done | bytes 131104 | tf_op jit(solution)/shard_map/ppermute | solution.py:117
  21.1 4.3 %collective-permute-start.6 = (bf16[64,1024]{1,0:T(8,128)(2,1)S(1)}, bf16[64,1024]{1,0:T(8,128)(2,1)S(1)}, u32[]{:S(2)}, u32[]{:S(2)}) collective-permute-start(bf16[64,1024]{1,0:T(8,128)(2,1)S(1)} %get-tuple-element.134), channel_id=1, source_target_pairs={{0,4},{1,5},{2,6},{3,7},{4,0},{5,1},{6,2},{7,3},{8,12},{9,13},{10,... | collective-permute-start | bytes 393224 | tf_op jit(solution)/shard_map/ppermute | solution.py:117
  28.8 6.0 %collective-permute-done.6.refs_1_ = bf16[64,1024]{1,0:T(8,128)(2,1)S(1)} collective-permute-done((bf16[64,1024]{1,0:T(8,128)(2,1)S(1)}, bf16[64,1024]{1,0:T(8,128)(2,1)S(1)}, u32[]{:S(2)}, u32[]{:S(2)}) %collective-permute-start.6) | collective-permute-done | bytes 131104 | tf_op jit(solution)/shard_map/ppermute | solution.py:117
  37.9 4.5 %forward.2 = (bf16[512,1024]{1,0:T(8,128)(2,1)S(1)}, bf16[512,1024]{1,0:T(8,128)(2,1)S(1)}, bf16[512,1024]{1,0:T(8,128)(2,1)S(1)}, f32[512,1]{1,0:T(8,128)S(1)},...) custom-call(bf16[256,1024]{1,0:T(8,128)(2,1)S(1)} %get-tuple-element.132.refs_0_, ...), custom_call_target="tpu_custom_call" | custom-call | tf_op jit(solution)/shard_map/forward/pallas_call | solution.py:65
  44.7 4.5 %forward.3 = (bf16[512,1024]{1,0:T(8,128)(2,1)S(1)}, bf16[512,1024]{1,0:T(8,128)(2,1)S(1)}, bf16[512,1024]{1,0:T(8,128)(2,1)S(1)}, f32[512,1]{1,0:T(8,128)S(1)},...) custom-call(bf16[256,1024]{1,0:T(8,128)(2,1)S(1)} %get-tuple-element, ...), custom_call_target="tpu_custom_call" | custom-call | tf_op jit(solution)/shard_map/forward/pallas_call | solution.py:65
  49.8 3.4 %backward.2 = (bf16[512,1024]{1,0:T(8,128)(2,1)S(1)}, bf16[512,1024]{1,0:T(8,128)(2,1)S(1)}, bf16[256,1024]{1,0:T(8,128)(2,1)S(1)}, bf16[256,1024]{1,0:T(8,128)(2,1)S(1)}, f32[8,128]{1,0:T(8,128)S(1)}) custom-call(bf16[256,1024]{1,0:T(8,128)(2,1)S(1)} %get-tuple-element.149.refs_0_, bf16[256,1024]{1,0:T(8,128)(2,1)S(1)} %collective-permute-done.15.refs_1_, ...), custom_call_target="tpu_custom_call" | custom-call | tf_op jit(solution)/shard_map/backward/pallas_call | solution.py:65
  53.4 4.1 %collective-permute-done.17.refs_0_ = bf16[256,1024]{1,0:T(8,128)(2,1)S(1)} collective-permute-done((bf16[256,1024]{1,0:T(8,128)(2,1)S(1)}, bf16[256,1024]{1,0:T(8,128)(2,1)S(1)}, u32[]{:S(2)}, u32[]{:S(2)}) %collective-permute-start.17) | collective-permute-done | bytes 524320 | tf_op jit(solution)/shard_map/ppermute | solution.py:117
  59.7 3.6 %backward.3 = (bf16[512,1024]{1,0:T(8,128)(2,1)S(1)}, bf16[512,1024]{1,0:T(8,128)(2,1)S(1)}, bf16[256,1024]{1,0:T(8,128)(2,1)S(1)}, bf16[128,1024]{1,0:T(8,128)(...) custom-call(bf16[256,1024]{1,0:T(8,128)(2,1)S(1)} %get-tuple-element.159.refs_0_, ...), custom_call_target="tpu_custom_call" | custom-call | tf_op jit(solution)/shard_map/backward/pallas_call | solution.py:65
  67.5 3.5 %weights.2 = (bf16[1024,1024]{1,0:T(8,128)(2,1)}, f32[8,128]{1,0:T(8,128)S(1)}) custom-call(bf16[512,1024]{1,0:T(8,128)(2,1)S(1)} %get-tuple-element.155.refs_0_, bf16[512,1024]{1,0:T(8,128)(2,1)S(1)} %get-tuple-element.156.refs_1_, bf16[512,1024]{1,0:T(8,128)(2,1)S(1)} %get-tuple-element.157.refs_2_, bf16[512,1024]{1,0:T(8,128)(2,1)S(1)} %get-tuple-element.165.refs_3_, ...), custom_call_target="tpu_custom_call" | custom-call | tf_op jit(solution)/shard_map/weights/pallas_call | solution.py:65
  73.1 3.9 %collective-permute-start.22 = (bf16[64,1024]{1,0:T(8,128)(2,1)S(1)}, bf16[64,1024]{1,0:T(8,128)(2,1)S(1)}, u32[]{:S(2)}, u32[]{:S(2)}) collective-permute-start(bf16[64,1024]{1,0:T(8,128)(2,1)S(1)} %get-tuple-element.173), channel_id=1, source_target_pairs={{0,4},{1,5},{2,6},{3,7},{4,0},{5,1},{6,2},{7,3},{8,12},{9,13},{10,... | collective-permute-start | bytes 393224 | tf_op jit(solution)/shard_map/ppermute | solution.py:117
  80.2 3.5 %collective-permute-done.26.refs_2_ = bf16[128,1024]{1,0:T(8,128)(2,1)S(1)} collective-permute-done((bf16[128,1024]{1,0:T(8,128)(2,1)S(1)}, bf16[128,1024]{1,0:T(8,128)(2,1)S(1)}, u32[]{:S(2)}, u32[]{:S(2)}) %collective-permute-start.26) | collective-permute-done | bytes 262176 | tf_op jit(solution)/shard_map/ppermute | solution.py:117
  86.4 2.5 %collective-permute-done.28.refs_1_ = bf16[64,1024]{1,0:T(8,128)(2,1)S(1)} collective-permute-done((bf16[64,1024]{1,0:T(8,128)(2,1)S(1)}, bf16[64,1024]{1,0:T(8,128)(2,1)S(1)}, u32[]{:S(2)}, u32[]{:S(2)}) %collective-permute-start.28) | collective-permute-done | bytes 131104 | tf_op jit(solution)/shard_map/ppermute | solution.py:117
  94.9 3.5 %weights.3 = (bf16[1024,1024]{1,0:T(8,128)(2,1)}, f32[8,128]{1,0:T(8,128)S(1)}) custom-call(bf16[512,1024]{1,0:T(8,128)(2,1)S(1)} %get-tuple-element.192.refs_0_, bf16[512,1024]{1,0:T(8,128)(2,1)S(1)} %get-tuple-element.193.refs_1_, bf16[512,1024]{1,0:T(8,128)(2,1)S(1)} %get-tuple-element.194.refs_2_, bf16[512,1024]{1,0:T(8,128)(2,1)S(1)} %get-tuple-element.195.refs_3_, ...), custom_call_target="tpu_custom_call" | custom-call | tf_op jit(solution)/shard_map/weights/pallas_call | solution.py:65
  101.0 4.2 %collective-permute-done.31.refs_1_ = bf16[64,1024]{1,0:T(8,128)(2,1)S(1)} collective-permute-done((bf16[64,1024]{1,0:T(8,128)(2,1)S(1)}, bf16[64,1024]{1,0:T(8,128)(2,1)S(1)}, u32[]{:S(2)}, u32[]{:S(2)}) %collective-permute-start.31) | collective-permute-done | bytes 131104 | tf_op jit(solution)/shard_map/ppermute | solution.py:117
  105.2 3.3 %tail.1 = (bf16[128,1024]{1,0:T(8,128)(2,1)}, bf16[128,1024]{1,0:T(8,128)(2,1)}, bf16[2080,256]{1,0:T(8,128)(2,1)S(1)}, bf16[2080,256]{1,0:T(8,128)(2,1)S(1)}, f32[8,128]{1,0:T(8,128)S(1)}) custom-call(bf16[64,1024]{1,0:T(8,128)(2,1)S(1)} %get-tuple-element.204.refs_0_, bf16[64,1024]{1,0:T(8,128)(2,1)S(1)} %collective-permute-done.31.refs_1_, ...), custom_call_target="tpu_custom_call" | custom-call | tf_op jit(solution)/shard_map/tail/pallas_call | solution.py:65
  108.6 2.7 %collective-permute-done.34.refs_1_ = bf16[2080,256]{1,0:T(8,128)(2,1)S(1)} collective-permute-done((bf16[2080,256]{1,0:T(8,128)(2,1)S(1)}, bf16[2080,256]{1,0:T(8,128)(2,1)S(1)}, u32[]{:S(2)}, u32[]{:S(2)}) %collective-permute-start.34) | collective-permute-done | bytes 1064992 | tf_op jit(solution)/shard_map/ppermute | solution.py:117
  114.0 5.9 %collective-permute-done.35.refs_2_ = bf16[528,256]{1,0:T(8,128)(2,1)S(1)} collective-permute-done((bf16[528,256]{1,0:T(8,128)(2,1)S(1)}, bf16[528,256]{1,0:T(8,128)(2,1)S(1)}, u32[]{:S(2)}, u32[]{:S(2)}) %collective-permute-start.35) | collective-permute-done | bytes 270368 | tf_op jit(solution)/shard_map/ppermute | solution.py:117
  122.9 3.4 %collective-permute-done.38.refs_3_ = bf16[256,256]{1,0:T(8,128)(2,1)S(1)} collective-permute-done((bf16[256,256]{1,0:T(8,128)(2,1)S(1)}, bf16[256,256]{1,0:T(8,128)(2,1)S(1)}, u32[]{:S(2)}, u32[]{:S(2)}) %collective-permute-start.38) | collective-permute-done | bytes 131104 | tf_op jit(solution)/shard_map/ppermute | solution.py:117
  126.5 2.6 %collective-permute-start.40 = (bf16[144,256]{1,0:T(8,128)(2,1)S(1)}, bf16[144,256]{1,0:T(8,128)(2,1)S(1)}, u32[]{:S(2)}, u32[]{:S(2)}) collective-permute-start(bf16[144,256]{1,0:T(8,128)(2,1)S(1)} %get-tuple-element.228), channel_id=1, source_target_pairs={{0,2},{1,3},{2,0},{3,1},{4,6},{5,7},{6,4},{7,5},{8,10},{9,11},{10,... | collective-permute-start | bytes 221192 | tf_op jit(solution)/shard_map/ppermute | solution.py:117
  133.0 2.2 %collective-permute-done.41.refs_3_ = bf16[144,256]{1,0:T(8,128)(2,1)S(1)} collective-permute-done((bf16[144,256]{1,0:T(8,128)(2,1)S(1)}, bf16[144,256]{1,0:T(8,128)(2,1)S(1)}, u32[]{:S(2)}, u32[]{:S(2)}) %collective-permute-start.41) | collective-permute-done | bytes 73760 | tf_op jit(solution)/shard_map/ppermute | solution.py:117
  137.2 2.7 %collective-permute-done.44.refs_3_ = bf16[144,256]{1,0:T(8,128)(2,1)S(1)} collective-permute-done((bf16[144,256]{1,0:T(8,128)(2,1)S(1)}, bf16[144,256]{1,0:T(8,128)(2,1)S(1)}, u32[]{:S(2)}, u32[]{:S(2)}) %collective-permute-start.44) | collective-permute-done | bytes 73760 | tf_op jit(solution)/shard_map/ppermute | solution.py:117
  (115 shorter events, 51.6 us)
Async XLA Ops:
  5.0 9.5 %collective-permute-start.3 = (bf16[128,1024]{1,0:T(8,128)(2,1)}, bf16[128,1024]{1,0:T(8,128)(2,1)S(1)}, u32[]{:S(2)}, u32[]{:S(2)}) collective-permute-start(bf16[128,1024]{1,0:T(8,128)(2,1)} %get-tuple-element.127), channel_id=1, source_target_pairs={{0,1},{1,0},{2,3},{3,2},{4,5},{5,4},{6,7},{7,6},{8,9},{9,8},{10,11... | collective-permute-start | bytes 786440 | tf_op jit(solution)/shard_map/ppermute | solution.py:117
  8.0 12.6 %collective-permute-start = (bf16[64,1024]{1,0:T(8,128)(2,1)S(1)}, bf16[64,1024]{1,0:T(8,128)(2,1)S(1)}, u32[]{:S(2)}, u32[]{:S(2)}) collective-permute-start(bf16[64,1024]{1,0:T(8,128)(2,1)S(1)} %get-tuple-element.123), channel_id=1, source_target_pairs={{0,4},{1,5},{2,6},{3,7},{4,0},{5,1},{6,2},{7,3},{8,12},{9,13},{10,... | collective-permute-start | bytes 393224 | tf_op jit(solution)/shard_map/ppermute | solution.py:117
  10.6 10.1 %collective-permute-start.1 = (bf16[64,1024]{1,0:T(8,128)(2,1)S(1)}, bf16[64,1024]{1,0:T(8,128)(2,1)S(1)}, u32[]{:S(2)}, u32[]{:S(2)}) collective-permute-start(bf16[64,1024]{1,0:T(8,128)(2,1)S(1)} %get-tuple-element.124), channel_id=1, source_target_pairs={{0,2},{1,3},{2,0},{3,1},{4,6},{5,7},{6,4},{7,5},{8,10},{9,11},{10,... | collective-permute-start | bytes 393224 | tf_op jit(solution)/shard_map/ppermute | solution.py:117
  12.1 8.5 %collective-permute-start.2 = (bf16[64,1024]{1,0:T(8,128)(2,1)S(1)}, bf16[64,1024]{1,0:T(8,128)(2,1)S(1)}, u32[]{:S(2)}, u32[]{:S(2)}) collective-permute-start(bf16[64,1024]{1,0:T(8,128)(2,1)S(1)} %get-tuple-element.125), channel_id=1, source_target_pairs={{0,6},{1,7},{2,4},{3,5},{4,2},{5,3},{6,0},{7,1},{8,14},{9,15},{10,... | collective-permute-start | bytes 393224 | tf_op jit(solution)/shard_map/ppermute | solution.py:117
  21.1 13.6 %collective-permute-start.6 = (bf16[64,1024]{1,0:T(8,128)(2,1)S(1)}, bf16[64,1024]{1,0:T(8,128)(2,1)S(1)}, u32[]{:S(2)}, u32[]{:S(2)}) collective-permute-start(bf16[64,1024]{1,0:T(8,128)(2,1)S(1)} %get-tuple-element.134), channel_id=1, source_target_pairs={{0,4},{1,5},{2,6},{3,7},{4,0},{5,1},{6,2},{7,3},{8,12},{9,13},{10,... | collective-permute-start | bytes 393224 | tf_op jit(solution)/shard_map/ppermute | solution.py:117
  25.4 10.2 %collective-permute-start.7 = (bf16[64,1024]{1,0:T(8,128)(2,1)S(1)}, bf16[64,1024]{1,0:T(8,128)(2,1)S(1)}, u32[]{:S(2)}, u32[]{:S(2)}) collective-permute-start(bf16[64,1024]{1,0:T(8,128)(2,1)S(1)} %get-tuple-element.135), channel_id=1, source_target_pairs={{0,2},{1,3},{2,0},{3,1},{4,6},{5,7},{6,4},{7,5},{8,10},{9,11},{10,... | collective-permute-start | bytes 393224 | tf_op jit(solution)/shard_map/ppermute | solution.py:117
  25.4 10.2 %collective-permute-start.8 = (bf16[64,1024]{1,0:T(8,128)(2,1)S(1)}, bf16[64,1024]{1,0:T(8,128)(2,1)S(1)}, u32[]{:S(2)}, u32[]{:S(2)}) collective-permute-start(bf16[64,1024]{1,0:T(8,128)(2,1)S(1)} %get-tuple-element.136), channel_id=1, source_target_pairs={{0,6},{1,7},{2,4},{3,5},{4,2},{5,3},{6,0},{7,1},{8,14},{9,15},{10,... | collective-permute-start | bytes 393224 | tf_op jit(solution)/shard_map/ppermute | solution.py:117
  27.2 15.2 %collective-permute-start.10 = (bf16[256,1024]{1,0:T(8,128)(2,1)S(1)}, bf16[256,1024]{1,0:T(8,128)(2,1)S(1)}, u32[]{:S(2)}, u32[]{:S(2)}) collective-permute-start(bf16[256,1024]{1,0:T(8,128)(2,1)S(1)} %get-tuple-element.132.refs_0_), channel_id=1, source_target_pairs={{0,16},{8,24},{16,0},{24,8},{1,17},{9,25},{17,1},{25,9},{2,18},{10... | collective-permute-start | bytes 1572872 | tf_op jit(solution)/shard_map/ppermute | solution.py:117
  43.2 14.3 %collective-permute-start.17 = (bf16[256,1024]{1,0:T(8,128)(2,1)S(1)}, bf16[256,1024]{1,0:T(8,128)(2,1)S(1)}, u32[]{:S(2)}, u32[]{:S(2)}) collective-permute-start(bf16[256,1024]{1,0:T(8,128)(2,1)S(1)} %get-tuple-element.149.refs_0_), channel_id=1, source_target_pairs={{0,16},{8,24},{16,0},{24,8},{1,17},{9,25},{17,1},{25,9},{2,18},{10... | collective-permute-start | bytes 1572872 | tf_op jit(solution)/shard_map/ppermute | solution.py:117
  58.1 12.9 %collective-permute-start.9 = (bf16[256,1024]{1,0:T(8,128)(2,1)S(1)}, bf16[256,1024]{1,0:T(8,128)(2,1)S(1)}, u32[]{:S(2)}, u32[]{:S(2)}) collective-permute-start(bf16[256,1024]{1,0:T(8,128)(2,1)S(1)} %get-tuple-element.140), channel_id=1, source_target_pairs={{0,8},{8,0},{16,24},{24,16},{1,9},{9,1},{17,25},{25,17},{2,10},{10... | collective-permute-start | bytes 1572872 | tf_op jit(solution)/shard_map/ppermute | solution.py:117
  58.2 14.7 %collective-permute-start.16 = (bf16[256,1024]{1,0:T(8,128)(2,1)S(1)}, bf16[256,1024]{1,0:T(8,128)(2,1)S(1)}, u32[]{:S(2)}, u32[]{:S(2)}) collective-permute-start(bf16[256,1024]{1,0:T(8,128)(2,1)S(1)} %get-tuple-element.154), channel_id=1, source_target_pairs={{0,16},{8,24},{16,0},{24,8},{1,17},{9,25},{17,1},{25,9},{2,18},{10... | collective-permute-start | bytes 1572872 | tf_op jit(solution)/shard_map/ppermute | solution.py:117
  63.9 13.1 %collective-permute-start.25 = (bf16[256,1024]{1,0:T(8,128)(2,1)S(1)}, bf16[256,1024]{1,0:T(8,128)(2,1)S(1)}, u32[]{:S(2)}, u32[]{:S(2)}) collective-permute-start(bf16[256,1024]{1,0:T(8,128)(2,1)S(1)} %get-tuple-element.177), channel_id=1, source_target_pairs={{0,8},{8,0},{16,24},{24,16},{1,9},{9,1},{17,25},{25,17},{2,10},{10... | collective-permute-start | bytes 1572872 | tf_op jit(solution)/shard_map/ppermute | solution.py:117
  65.4 13.1 %collective-permute-start.27 = (bf16[128,1024]{1,0:T(8,128)(2,1)S(1)}, bf16[128,1024]{1,0:T(8,128)(2,1)S(1)}, u32[]{:S(2)}, u32[]{:S(2)}) collective-permute-start(bf16[128,1024]{1,0:T(8,128)(2,1)S(1)} %get-tuple-element.179), channel_id=1, source_target_pairs={{0,16},{8,24},{16,0},{24,8},{1,17},{9,25},{17,1},{25,9},{2,18},{10... | collective-permute-start | bytes 786440 | tf_op jit(solution)/shard_map/ppermute | solution.py:117
  66.8 16.9 %collective-permute-start.26 = (bf16[128,1024]{1,0:T(8,128)(2,1)S(1)}, bf16[128,1024]{1,0:T(8,128)(2,1)S(1)}, u32[]{:S(2)}, u32[]{:S(2)}) collective-permute-start(bf16[128,1024]{1,0:T(8,128)(2,1)S(1)} %get-tuple-element.178), channel_id=1, source_target_pairs={{0,16},{8,24},{16,0},{24,8},{1,17},{9,25},{17,1},{25,9},{2,18},{10... | collective-permute-start | bytes 786440 | tf_op jit(solution)/shard_map/ppermute | solution.py:117
  73.1 13.0 %collective-permute-start.22 = (bf16[64,1024]{1,0:T(8,128)(2,1)S(1)}, bf16[64,1024]{1,0:T(8,128)(2,1)S(1)}, u32[]{:S(2)}, u32[]{:S(2)}) collective-permute-start(bf16[64,1024]{1,0:T(8,128)(2,1)S(1)} %get-tuple-element.173), channel_id=1, source_target_pairs={{0,4},{1,5},{2,6},{3,7},{4,0},{5,1},{6,2},{7,3},{8,12},{9,13},{10,... | collective-permute-start | bytes 393224 | tf_op jit(solution)/shard_map/ppermute | solution.py:117
  77.0 9.4 %collective-permute-start.23 = (bf16[64,1024]{1,0:T(8,128)(2,1)S(1)}, bf16[64,1024]{1,0:T(8,128)(2,1)S(1)}, u32[]{:S(2)}, u32[]{:S(2)}) collective-permute-start(bf16[64,1024]{1,0:T(8,128)(2,1)S(1)} %get-tuple-element.174), channel_id=1, source_target_pairs={{0,2},{1,3},{2,0},{3,1},{4,6},{5,7},{6,4},{7,5},{8,10},{9,11},{10,... | collective-permute-start | bytes 393224 | tf_op jit(solution)/shard_map/ppermute | solution.py:117
  77.0 9.4 %collective-permute-start.24 = (bf16[64,1024]{1,0:T(8,128)(2,1)S(1)}, bf16[64,1024]{1,0:T(8,128)(2,1)S(1)}, u32[]{:S(2)}, u32[]{:S(2)}) collective-permute-start(bf16[64,1024]{1,0:T(8,128)(2,1)S(1)} %get-tuple-element.175), channel_id=1, source_target_pairs={{0,6},{1,7},{2,4},{3,5},{4,2},{5,3},{6,0},{7,1},{8,14},{9,15},{10,... | collective-permute-start | bytes 393224 | tf_op jit(solution)/shard_map/ppermute | solution.py:117
  78.6 7.7 %collective-permute-start.29 = (bf16[64,1024]{1,0:T(8,128)(2,1)S(1)}, bf16[64,1024]{1,0:T(8,128)(2,1)S(1)}, u32[]{:S(2)}, u32[]{:S(2)}) collective-permute-start(bf16[64,1024]{1,0:T(8,128)(2,1)S(1)} %get-tuple-element.187), channel_id=1, source_target_pairs={{0,1},{1,0},{2,3},{3,2},{4,5},{5,4},{6,7},{7,6},{8,9},{9,8},{10,11... | collective-permute-start | bytes 393224 | tf_op jit(solution)/shard_map/ppermute | solution.py:117
  89.0 9.5 %collective-permute-start.30 = (bf16[128,1024]{1,0:T(8,128)(2,1)S(1)}, bf16[128,1024]{1,0:T(8,128)(2,1)S(1)}, u32[]{:S(2)}, u32[]{:S(2)}) collective-permute-start(bf16[128,1024]{1,0:T(8,128)(2,1)S(1)} %get-tuple-element.191), channel_id=1, source_target_pairs={{0,1},{1,0},{2,3},{3,2},{4,5},{5,4},{6,7},{7,6},{8,9},{9,8},{10,11... | collective-permute-start | bytes 786440 | tf_op jit(solution)/shard_map/ppermute | solution.py:117
  90.6 9.6 %collective-permute-start.32 = (bf16[64,1024]{1,0:T(8,128)(2,1)S(1)}, bf16[64,1024]{1,0:T(8,128)(2,1)S(1)}, u32[]{:S(2)}, u32[]{:S(2)}) collective-permute-start(bf16[64,1024]{1,0:T(8,128)(2,1)S(1)} %get-tuple-element.206), channel_id=1, source_target_pairs={{0,2},{1,3},{2,0},{3,1},{4,6},{5,7},{6,4},{7,5},{8,10},{9,11},{10,... | collective-permute-start | bytes 393224 | tf_op jit(solution)/shard_map/ppermute | solution.py:117
  92.8 8.2 %collective-permute-start.33 = (bf16[64,1024]{1,0:T(8,128)(2,1)S(1)}, bf16[64,1024]{1,0:T(8,128)(2,1)S(1)}, u32[]{:S(2)}, u32[]{:S(2)}) collective-permute-start(bf16[64,1024]{1,0:T(8,128)(2,1)S(1)} %get-tuple-element.207), channel_id=1, source_target_pairs={{0,6},{1,7},{2,4},{3,5},{4,2},{5,3},{6,0},{7,1},{8,14},{9,15},{10,... | collective-permute-start | bytes 393224 | tf_op jit(solution)/shard_map/ppermute | solution.py:117
  94.8 10.4 %collective-permute-start.31 = (bf16[64,1024]{1,0:T(8,128)(2,1)S(1)}, bf16[64,1024]{1,0:T(8,128)(2,1)S(1)}, u32[]{:S(2)}, u32[]{:S(2)}) collective-permute-start(bf16[64,1024]{1,0:T(8,128)(2,1)S(1)} %get-tuple-element.205), channel_id=1, source_target_pairs={{0,4},{1,5},{2,6},{3,7},{4,0},{5,1},{6,2},{7,3},{8,12},{9,13},{10,... | collective-permute-start | bytes 393224 | tf_op jit(solution)/shard_map/ppermute | solution.py:117
  111.4 8.6 %collective-permute-start.35 = (bf16[528,256]{1,0:T(8,128)(2,1)S(1)}, bf16[528,256]{1,0:T(8,128)(2,1)S(1)}, u32[]{:S(2)}, u32[]{:S(2)}) collective-permute-start(bf16[528,256]{1,0:T(8,128)(2,1)S(1)} %get-tuple-element.217), channel_id=1, source_target_pairs={{0,16},{8,24},{16,0},{24,8},{1,17},{9,25},{17,1},{25,9},{2,18},{10... | collective-permute-start | bytes 811016 | tf_op jit(solution)/shard_map/ppermute | solution.py:117
  112.9 8.2 %collective-permute-start.37 = (bf16[512,256]{1,0:T(8,128)(2,1)S(1)}, bf16[512,256]{1,0:T(8,128)(2,1)S(1)}, u32[]{:S(2)}, u32[]{:S(2)}) collective-permute-start(bf16[512,256]{1,0:T(8,128)(2,1)S(1)} %get-tuple-element.221), channel_id=1, source_target_pairs={{0,1},{1,0},{2,3},{3,2},{4,5},{5,4},{6,7},{7,6},{8,9},{9,8},{10,11... | collective-permute-start | bytes 786440 | tf_op jit(solution)/shard_map/ppermute | solution.py:117
  (30 other events, 128.0 us)

commit v4 on v3

--- a/solution.py
+++ b/solution.py
@@ -16,6 +16,7 @@
 TILE = 16
 MIB = 1024 * 1024
 WAIT = 20 * 10**9
+PIECES = 4
 
 NN = (((1,), (0,)), ((), ()))
 NT = (((1,), (1,)), ((), ()))
@@ -74,7 +75,7 @@
         )(*args)
         return results
 
-    def move(self, *outputs, flops=0, name="move"):
+    def move(self, *outputs, flops=0, hold=(), name="move"):
         arrays, places = [], {}
         aligned = True
         for pieces in outputs:
@@ -96,7 +97,7 @@
             ]
 
         def body(*refs):
-            for pieces, out in zip(outputs, refs[len(arrays) :]):
+            for pieces, out in zip(outputs, refs[len(arrays) + len(hold) :]):
                 at = 0
                 for rows, terms in pieces:
                     parts = [refs[places[id(a)]][f : f + rows, :] for a, f in terms]
@@ -106,7 +107,7 @@
                     at += rows
 
         outs = [shape((sum(rows for rows, _ in pieces), width)) for pieces in outputs]
-        return self.call(body, outs, arrays, flops=flops, name=name)
+        return self.call(body, outs, arrays + list(hold), flops=flops, name=name)
 
 
 def added(*terms):
@@ -159,7 +160,7 @@
         return (high >> 1) | ((high & 1) << 1), rel & (low - 1)
 
     def head_body(ids_hbm, cot_hbm, tok_hbm, ctx_hbm, w_out_hbm, *refs):
-        outs, copies = refs[: low + 8], refs[low + 8 :]
+        outs, copies = refs[: 2 * low + 7], refs[2 * low + 7 :]
         lows, (placed_ref, resid_ref, inv_ref, normed_ref), sends = outs[:low], outs[low : low + 4], outs[low + 4 :]
         held, sems = copies[:5], copies[5]
         me = lax.axis_index("expert")
@@ -195,8 +196,10 @@
         normed = (resid_f * inv).astype(BF)
         normed_ref[...] = normed
         moved = mm(at_rows(places, slots), normed).astype(BF)
-        for c in range(len(masks)):
-            sends[c][...] = moved[c * size : (c + 1) * size, :]
+        for m in range(low):
+            sends[m][...] = moved[m * cap : (m + 1) * cap, :]
+        for c in range(1, 4):
+            sends[low + c - 1][...] = moved[c * size : (c + 1) * size, :]
         loads[4].wait()
         moved = mm(at_rows(spots, slots), cot_ref[...]).astype(BF)
         each = slots // low
@@ -206,29 +209,33 @@
     outs = line.call(
         head_body,
         [shape((slots // low, width))] * low + [shape((2, tok), jnp.int32)]
-        + [shape((tok, width)), shape((tok, 1), F32), shape((tok, width))] + [shape((size, width))] * 4,
+        + [shape((tok, width)), shape((tok, 1), F32), shape((tok, width))] + [shape((cap, width))] * low + [shape((size, width))] * 3,
         (ids_t, cotangent, tokens, context, w_out), specs=[HBM] * 5,
         scratch=[pltpu.VMEM((2, tok), jnp.int32), pltpu.VMEM((tok, width), BF), pltpu.VMEM((width, width), BF),
                  pltpu.VMEM((tok, width), BF), pltpu.VMEM((tok, width), BF), DMA((5,))],
         vmem=53 * MIB, name="head")
     cot_low, (placed, resid, inv, normed), sends = outs[:low], outs[low : low + 4], outs[low + 4 :]
     cot_low = [cot_low[0]] + [swap(cot_low[m], "expert", m) for m in range(1, low)]
-    norm_high = [sends[0]] + [swap(sends[c], "expert", masks[c] * low) for c in (1, 2, 3)]
-
-    cot_high = line.move(*[[(cap, [(cot_low[m], c * cap)]) for m in range(low)] for c in range(4)], name="pack_cot_z")
-    cot_high = [cot_high[0]] + [swap(cot_high[c], "expert", masks[c] * low) for c in (1, 2, 3)]
-
-    norm_low = []
-    if low > 1:
-        lows = line.move(*[[(cap, [(norm_high[c], m * cap)]) for c in range(4)] for m in range(1, low)], name="pack_norm_y")
-        norm_low = [swap(x, "expert", m + 1) for m, x in enumerate(lows)]
-    norm_own = line.move(
-        [(cap, [piece]) for c in range(4) for piece in [(norm_high[c], 0)] + [(x, c * cap) for x in norm_low]],
-        name="pack_norm_x")[0]
-    norm_far = swap(norm_own, "dp", far)
+    norm_zero = [sends[0]] + [swap(sends[m], "expert", m) for m in range(1, low)]
+    norm_high = [None] + [swap(sends[low + c - 1], "expert", masks[c] * low) for c in (1, 2, 3)]
+    halves = [range(low)[: low // 2], range(low)[low // 2 :]]
+    early = line.move(
+        *[[(cap, [(norm_zero[m], 0)]) for m in part] for part in halves],
+        *[[(cap, [(cot_low[m], c * cap)]) for m in range(low)] for c in range(4)], hold=(weight_in, weight_down), name="pack_zero")
+    early, cot_high = early[:2], [swap(x, "expert", masks[c] * low) if masks[c] else x for c, x in enumerate(early[2:])]
+    early_far = [swap(x, "dp", far) for x in early]
+
+    whole = lambda *arrays: [(x.shape[0], [(x, 0)]) for x in arrays]
+    norm_far, *lows = line.move(
+        whole(*early_far),
+        *[[(cap, [(norm_high[c], m * cap)]) for c in (1, 2, 3)] for m in range(1, low)], name="pack_norm_y")
+    lows = [swap(x, "expert", m + 1) for m, x in enumerate(lows)]
+    rest = [(cap, [piece]) for c in (1, 2, 3) for piece in [(norm_high[c], 0)] + [(x, (c - 1) * cap) for x in lows]]
+    norm_own, norm_rest = line.move(whole(*early) + rest, rest, name="pack_norm_x")
+    norm_far = [norm_far, swap(norm_rest, "dp", far)]
     norm_core = swap(norm_own, "dp", 1)
-    cot_own = line.move([(size, [(x, 0)]) for x in cot_high], flops=WAIT, name="pack_cot_x")[0]
-    cot_far = swap(cot_own, "dp", far)
+    cot_own = line.move(whole(*cot_high), flops=WAIT, name="pack_cot_x")[0]
+    cot_far = [swap(cot_own, "dp", far)]
     cot_core = swap(cot_own, "dp", 1)
 
     block = 256 if hidden % 256 == 0 else hidden
@@ -316,22 +323,28 @@
 
     half = slots // 2
 
-    def relay(x):
-        whole, *halves = line.move([(slots, [(x, 0)])], *[[(half, [(x, i * half)])] for i in range(2)], name="relay")
-        return [whole] + [swap(h, "dp", 1) for h in halves]
+    def relay(x, pieces):
+        each = slots // pieces
+        first, second = x[0], x[-1]
+        cut = first.shape[0]
+        spans = [[(lo, hi) for lo, hi in ((i * each, min((i + 1) * each, cut)), (max(i * each, cut), (i + 1) * each)) if lo < hi]
+                 for i in range(pieces)]
+        taken = [[(hi - lo, [(first, lo) if hi <= cut else (second, lo - cut)]) for lo, hi in span] for span in spans]
+        joined, *parts = line.move(whole(*x), *taken, name="relay")
+        return [joined] + [swap(part, "dp", 1) for part in parts]
 
     rows_n, act_n, der_n, gate_n, keep_n, send_n = forward([norm_own, norm_core], 1)
     near_out = swap(send_n[0], "dp", 1)
-    rows_f, act_f, der_f, gate_f, keep_f, send_f = forward(relay(norm_far), 2)
+    rows_f, act_f, der_f, gate_f, keep_f, send_f = forward(relay(norm_far, PIECES), PIECES)
     core_out = [swap(x, "dp", 1) for x in send_f]
+    far_out = line.move([(x.shape[0], [(keep_f, i * x.shape[0]), (x, 0)]) for i, x in enumerate(core_out)], name="sum_core_out")[0]
+    far_out = swap(far_out, "dp", far)
+    cot_far = relay(cot_far, 2)
     grads_n, pre_n, ikeep_n, isend_n = backward([cot_own, cot_core], gate_n, der_n, 1)
     near_in = swap(isend_n[0], "dp", 1)
-    far_out = line.move([(half, [(keep_f, i * half), (core_out[i], 0)]) for i in range(2)], name="sum_core_out")[0]
-    far_out = swap(far_out, "dp", far)
-    grads_f, pre_f, ikeep_f, isend_f = backward(relay(cot_far), gate_f, der_f, 2)
+    grads_f, pre_f, ikeep_f, isend_f = backward(cot_far, gate_f, der_f, 2)
     core_in = [swap(x, "dp", 1) for x in isend_f]
-    far_in = line.move(*[[(half, [(ikeep_f, i * half), (core_in[i], 0)])] for i in range(2)], name="sum_core_in")
-    far_in = [swap(x, "dp", far) for x in far_in]
+    far_in = [swap(line.move([(half, [(ikeep_f, 0), (core_in[0], 0)])], name="sum_core_in")[0], "dp", far)]
 
     def weight_grad(lefts, rights):
         left, right = lefts[0].shape[1], rights[0].shape[1]
@@ -365,6 +378,7 @@
             vmem=20 * MIB, name="weights")[0]
 
     grad_w_down = weight_grad((act_n, act_f), (grads_n, grads_f))
+    far_in.append(swap(line.move([(half, [(ikeep_f, half), (core_in[1], 0)])], name="sum_core_in")[0], "dp", far))
 
     quarter = slots // 4
     sums = line.move(
@@ -390,11 +404,11 @@
     back_in = send_back(0, *total_a)
     back_in += send_back(1, *total_b)
     if low > 1:
-        out_low = line.move(*[[(4 * cap, [(x, 0)])] for x in out_low], name="pass_out_y")
-        out_low = [swap(x, "expert", m + 1) for m, x in enumerate(out_low)]
-    grad_w_in = weight_grad((rows_n, rows_f), (pre_n, pre_f))
+        out_low = line.move(*[[(2 * cap, [(x, i * 2 * cap)])] for x in out_low for i in range(2)], name="pass_out_y")
+        out_low = [swap(x, "expert", i // 2 + 1) for i, x in enumerate(out_low)]
+    back_a = line.move([(x.shape[0], [(x, 0)]) for x in back_in[:2]], name="pack_back")[0]
     back_out = line.move(
-        [(cap, [piece]) for c in range(4) for piece in [(out_high[c], 0)] + [(x, c * cap) for x in out_low]],
+        [(cap, [piece]) for c in range(4) for piece in [(out_high[c], 0)] + [(out_low[2 * m + c // 2], c % 2 * cap) for m in range(low - 1)]],
         name="pack_out")
 
     spare = -(-experts // TILE) * TILE
@@ -426,13 +440,29 @@
         (*back_out, placed, ids_t, router_t, resid, cotangent, normed),
         name="combine")
 
+    tile = max(per, LANES)
+
+    def products(odd, ctx_ref, grad_ref, local_ref, turned, out):
+        me, mine = lax.axis_index("expert"), lax.axis_index("dp")
+        for d in range(far):
+            at = pl.ds(pl.multiple_of((mine ^ (2 * d + odd)) * part, LANES), part)
+            turned[:, d * part : (d + 1) * part] = grad_ref[:, at]
+            out[d * span + width : (d + 1) * span, :] = local_ref[:, at]
+        for i in range(width // tile):
+            block = mm(ctx_ref[:, i * tile : (i + 1) * tile], turned[...], TN).astype(BF)
+            for j in range(tile // per):
+                spot, lower = order((i * (tile // per) + j) ^ me)
+                to = (spot * low + lower) * per
+                for d in range(far):
+                    out[pl.ds(pl.multiple_of(d * span + to, TILE), per), :] = (
+                        block[j * per : (j + 1) * per, d * part : (d + 1) * part])
+
     def tail_body(*refs):
-        me, mine = lax.axis_index("expert"), lax.axis_index("dp")
-        backs = refs[:4]
-        (placed_ref, table_ref, router_ref, resid_ref, inv_ref, local_ref, cot_hbm, w_out_hbm, ctx_hbm,
-         grad_ref, grad_ctx_ref, keep_ref, send_ref, cot_ref, w_out_ref, ctx_ref, turned, sems) = refs[4:]
+        backs = refs[:3]
+        (placed_ref, table_ref, router_ref, resid_ref, inv_ref, local_ref, cot_hbm, ctx_hbm,
+         grad_out, grad_ref, ctx_ref, send_ref, cot_ref, turned, sems) = refs[3:]
         loads = [pltpu.make_async_copy(src, dst, sems.at[i]) for i, (src, dst) in enumerate(
-            ((cot_hbm, cot_ref), (ctx_hbm, ctx_ref), (w_out_hbm, w_out_ref)))]
+            ((cot_hbm, cot_ref), (ctx_hbm, ctx_ref)))]
         for load in loads:
             load.start()
         held = jnp.concatenate([b[...] for b in backs], axis=0)
@@ -442,43 +472,35 @@
         inv_col = inv_ref[...]
         mean_term = jnp.mean(normed_grad * resid_f, axis=1, keepdims=True)
         loads[0].wait()
-        grad = (cot_ref[...].astype(F32) + inv_col * normed_grad
-                - (inv_col * inv_col * inv_col * mean_term) * resid_f).astype(BF)
-        grad_ref[...] = grad
-        outs = [(send_ref if m % 2 else keep_ref, (m // 2) * span) for m in range(dp)]
-        for m, (out, base) in enumerate(outs):
-            at = pl.ds(pl.multiple_of((mine ^ m) * part, LANES), part)
-            turned[:, m * part : (m + 1) * part] = grad_ref[:, at]
-            out[base + width : base + span, :] = local_ref[:, at]
+        grad_ref[...] = (cot_ref[...].astype(F32) + inv_col * normed_grad
+                         - (inv_col * inv_col * inv_col * mean_term) * resid_f).astype(BF)
         loads[1].wait()
-        tile = max(per, LANES)
-        for i in range(width // tile):
-            block = mm(ctx_ref[:, i * tile : (i + 1) * tile], turned[...], TN).astype(BF)
-            for j in range(tile // per):
-                spot, lower = order((i * (tile // per) + j) ^ me)
-                to = (spot * low + lower) * per
-                for m, (out, base) in enumerate(outs):
-                    out[pl.ds(pl.multiple_of(base + to, TILE), per), :] = (
-                        block[j * per : (j + 1) * per, m * part : (m + 1) * part])
-        loads[2].wait()
-        grad_ctx_ref[...] = mm(grad, w_out_ref[...], NT).astype(BF)
-
-    grad_tokens, grad_context, keep, send = line.call(
-        tail_body,
-        [shape((tok, width)), shape((tok, width)), shape((far * span, part)), shape((far * span, part))],
-        (*back_in, placed, table, router_t, resid, inv, local_router, cotangent, w_out, context),
-        specs=[VMEM] * 10 + [HBM] * 3,
-        scratch=[pltpu.VMEM((tok, width), BF), pltpu.VMEM((width, width), BF), pltpu.VMEM((tok, width), BF),
-                 pltpu.VMEM((tok, width), BF), DMA((3,))],
+        grad_out[...] = grad_ref[...]
+        products(1, ctx_ref, grad_ref, local_ref, turned, send_ref)
+
+    grad_tokens, grad_near, ctx_near, send = line.call(
+        tail_body, [shape((tok, width))] * 3 + [ shape((far * span, part))],
+        (back_a, *back_in[2:], placed, table, router_t, resid, inv, local_router, cotangent, context),
+        specs=[VMEM] * 9 + [HBM] * 2,
+        scratch=[pltpu.VMEM((tok, width), BF), pltpu.VMEM((tok, far * part), BF), DMA((2,))],
         vmem=16 * MIB, name="tail")
-
     core = swap(send, "dp", 1)
+
+    def keep_body(ctx_ref, grad_ref, local_ref, w_out_ref, grad_ctx_ref, keep_ref, turned):
+        products(0, ctx_ref, grad_ref, local_ref, turned, keep_ref)
+        grad_ctx_ref[...] = mm(grad_ref[...], w_out_ref[...], NT).astype(BF)
+
+    grad_context, keep = line.call(
+        keep_body, [shape((tok, width)), shape((far * span, part))], (ctx_near, grad_near, local_router, w_out),
+        scratch=[pltpu.VMEM((tok, far * part), BF)], vmem=16 * MIB, name="keep")
+
     spot = lambda d, c, m: d * span + (c * low + m) * per
     two = lambda first: [(keep, first), (core, first)]
     group = [(spare, two(width))]
     sum_x = line.move(
         [(2 * low * per, two(span)), (spare, two(span + width))],
         *[[(per, two(spot(d, c, m))) for d in range(2) for c in (2, 3)] for m in range(1, low)], name="reduce_core")
+    grad_w_in = weight_grad((rows_n, rows_f), (pre_n, pre_f))
     first_x = swap(sum_x[0], "dp", far)
     second_low = [swap(x, "expert", m + 1) for m, x in enumerate(sum_x[1:])]
     first = line.move(

time: 143 us -> 131 us (0.916)
  waiting for transfers between devices: 55.3 us -> 43.6 us
    ppermute x45 -> x53, waiting for transfers between devices: 55.3 us -> 43.6 us  [swap(): lax.ppermute(x, axis, [(i, i ^ mask) for i in range(lax.axis_size(axis))])]
    ppermute x45 -> x53, starting transfers between devices: 49.2 us -> 48.3 us  [swap(): lax.ppermute(x, axis, [(i, i ^ mask) for i in range(lax.axis_size(axis))])]
    pallas_call x31 -> x34, Pallas kernels: 34.1 us -> 34.8 us  [call(): pl.pallas_call(kernel, out_shape=[*outs, shape((8, LANES), F32)], in_spec...]
  transfers between devices with their start and end apart: 45 -> 53, of which waited for: 23 -> 28; matrix products, arithmetic and copies ran while one was open for 0% -> 0% of each run, Pallas kernels for 18% -> 22%
where the time goes in v4:
time: 131 us; the launch traced here: 130 us
  starting transfers between devices  48.3 us (37%)
  waiting for transfers between devices  43.6 us (33%)
  Pallas kernels  34.8 us (27%)
  local copies, waits for them, and re-layouts  2.67 us (2%)
    ppermute x53, starting transfers between devices, swap(): lax.ppermute(x, axis, [(i, i ^ mask) for i in range(lax.axis_size(axis))])  48.3 us
    ppermute x53, waiting for transfers between devices, swap(): lax.ppermute(x, axis, [(i, i ^ mask) for i in range(lax.axis_size(axis))])  43.6 us
    pallas_call x34, Pallas kernels, call(): pl.pallas_call(kernel, out_shape=[*outs, shape((8, LANES), F32)], in_spec...  34.8 us
    unnamed x20, local copies, waits for them, and re-layouts  2.67 us
  transfers between devices with their start and end apart: 53, of which 28 were waited for; matrix products, arithmetic and copies ran while one was open for 0% of the time, Pallas kernels for 22%

profile of v4, /device:TPU:0, one launch (start us, length us, event | category | flops | bytes accessed | tf_op | source)
XLA Modules:
  0.0 130.5 jit_solution(3539843481119688294)
XLA Ops:
  1.5 3.6 %head.1 = (bf16[128,1024]{1,0:T(8,128)(2,1)S(1)}, bf16[128,1024]{1,0:T(8,128)(2,1)}, s32[2,128]{1,0:T(2,128)S(1)}, bf16[128,1024]{1,0:T(8,128)(2,1)}, f32[128,1]...) custom-call(s32[2,128]{1,0:T(2,128)S(1)} %bitcast.21, ...), custom_call_target="tpu_custom_call" | custom-call | tf_op jit(solution)/shard_map/head/pallas_call | solution.py:66
  5.1 3.0 %collective-permute-start.1 = (bf16[128,1024]{1,0:T(8,128)(2,1)}, bf16[128,1024]{1,0:T(8,128)(2,1)S(1)}, u32[]{:S(2)}, u32[]{:S(2)}) collective-permute-start(bf16[128,1024]{1,0:T(8,128)(2,1)} %get-tuple-element.141), channel_id=1, source_target_pairs={{0,1},{1,0},{2,3},{3,2},{4,5},{5,4},{6,7},{7,6},{8,9},{9,8},{10,11... | collective-permute-start | bytes 786440 | tf_op jit(solution)/shard_map/ppermute | solution.py:118
  8.2 3.0 %collective-permute-start.2 = (bf16[64,1024]{1,0:T(8,128)(2,1)S(1)}, bf16[64,1024]{1,0:T(8,128)(2,1)S(1)}, u32[]{:S(2)}, u32[]{:S(2)}) collective-permute-start(bf16[64,1024]{1,0:T(8,128)(2,1)S(1)} %get-tuple-element.145), channel_id=1, source_target_pairs={{0,4},{1,5},{2,6},{3,7},{4,0},{5,1},{6,2},{7,3},{8,12},{9,13},{10,... | collective-permute-start | bytes 393224 | tf_op jit(solution)/shard_map/ppermute | solution.py:118
  12.8 3.2 %collective-permute-done.refs_1_ = bf16[32,1024]{1,0:T(8,128)(2,1)S(1)} collective-permute-done((bf16[32,1024]{1,0:T(8,128)(2,1)S(1)}, bf16[32,1024]{1,0:T(8,128)(2,1)S(1)}, u32[]{:S(2)}, u32[]{:S(2)}) %collective-permute-start) | collective-permute-done | bytes 65568 | tf_op jit(solution)/shard_map/ppermute | solution.py:118
  25.4 2.6 %collective-permute-start.9 = (bf16[64,1024]{1,0:T(8,128)(2,1)S(1)}, bf16[64,1024]{1,0:T(8,128)(2,1)S(1)}, u32[]{:S(2)}, u32[]{:S(2)}) collective-permute-start(bf16[64,1024]{1,0:T(8,128)(2,1)S(1)} %get-tuple-element.153), channel_id=1, source_target_pairs={{0,4},{1,5},{2,6},{3,7},{4,0},{5,1},{6,2},{7,3},{8,12},{9,13},{10,... | collective-permute-start | bytes 393224 | tf_op jit(solution)/shard_map/ppermute | solution.py:118
  30.6 6.4 %collective-permute-done.9.refs_1_ = bf16[64,1024]{1,0:T(8,128)(2,1)S(1)} collective-permute-done((bf16[64,1024]{1,0:T(8,128)(2,1)S(1)}, bf16[64,1024]{1,0:T(8,128)(2,1)S(1)}, u32[]{:S(2)}, u32[]{:S(2)}) %collective-permute-start.9) | collective-permute-done | bytes 131104 | tf_op jit(solution)/shard_map/ppermute | solution.py:118
  38.6 4.7 %forward.2 = (bf16[512,1024]{1,0:T(8,128)(2,1)S(1)}, bf16[512,1024]{1,0:T(8,128)(2,1)S(1)}, bf16[512,1024]{1,0:T(8,128)(2,1)S(1)}, f32[512,1]{1,0:T(8,128)S(1)},...) custom-call(bf16[256,1024]{1,0:T(8,128)(2,1)S(1)} %get-tuple-element.151.refs_0_, ...), custom_call_target="tpu_custom_call" | custom-call | tf_op jit(solution)/shard_map/forward/pallas_call | solution.py:66
  45.5 4.5 %forward.3 = (bf16[512,1024]{1,0:T(8,128)(2,1)S(1)}, bf16[512,1024]{1,0:T(8,128)(2,1)S(1)}, bf16[512,1024]{1,0:T(8,128)(2,1)S(1)}, f32[512,1]{1,0:T(8,128)S(1)},...) custom-call(bf16[256,1024]{1,0:T(8,128)(2,1)S(1)} %get-tuple-element, ...), custom_call_target="tpu_custom_call" | custom-call | tf_op jit(solution)/shard_map/forward/pallas_call | solution.py:66
  55.1 3.4 %backward.2 = (bf16[512,1024]{1,0:T(8,128)(2,1)S(1)}, bf16[512,1024]{1,0:T(8,128)(2,1)S(1)}, bf16[256,1024]{1,0:T(8,128)(2,1)S(1)}, bf16[256,1024]{1,0:T(8,128)(2,1)S(1)}, f32[8,128]{1,0:T(8,128)S(1)}) custom-call(bf16[256,1024]{1,0:T(8,128)(2,1)S(1)} %get-tuple-element.176.refs_0_, bf16[256,1024]{1,0:T(8,128)(2,1)S(1)} %collective-permute-done.26.refs_1_, ...), custom_call_target="tpu_custom_call" | custom-call | tf_op jit(solution)/shard_map/backward/pallas_call | solution.py:66
  58.6 3.6 %backward.3 = (bf16[512,1024]{1,0:T(8,128)(2,1)S(1)}, bf16[512,1024]{1,0:T(8,128)(2,1)S(1)}, bf16[256,1024]{1,0:T(8,128)(2,1)S(1)}, bf16[128,1024]{1,0:T(8,128)(...) custom-call(bf16[256,1024]{1,0:T(8,128)(2,1)S(1)} %get-tuple-element.178.refs_0_, ...), custom_call_target="tpu_custom_call" | custom-call | tf_op jit(solution)/shard_map/backward/pallas_call | solution.py:66
  64.7 3.5 %weights.2 = (bf16[1024,1024]{1,0:T(8,128)(2,1)}, f32[8,128]{1,0:T(8,128)S(1)}) custom-call(bf16[512,1024]{1,0:T(8,128)(2,1)S(1)} %get-tuple-element.189.refs_0_, bf16[512,1024]{1,0:T(8,128)(2,1)S(1)} %get-tuple-element.190.refs_1_, bf16[512,1024]{1,0:T(8,128)(2,1)S(1)} %get-tuple-element.191.refs_2_, bf16[512,1024]{1,0:T(8,128)(2,1)S(1)} %get-tuple-element.192.refs_3_, ...), custom_call_target="tpu_custom_call" | custom-call | tf_op jit(solution)/shard_map/weights/pallas_call | solution.py:66
  69.9 2.9 %collective-permute-start.29 = (bf16[64,1024]{1,0:T(8,128)(2,1)S(1)}, bf16[64,1024]{1,0:T(8,128)(2,1)S(1)}, u32[]{:S(2)}, u32[]{:S(2)}) collective-permute-start(bf16[64,1024]{1,0:T(8,128)(2,1)S(1)} %get-tuple-element.199), channel_id=1, source_target_pairs={{0,4},{1,5},{2,6},{3,7},{4,0},{5,1},{6,2},{7,3},{8,12},{9,13},{10,... | collective-permute-start | bytes 393224 | tf_op jit(solution)/shard_map/ppermute | solution.py:118
  75.2 4.0 %collective-permute-done.33.refs_2_ = bf16[128,1024]{1,0:T(8,128)(2,1)S(1)} collective-permute-done((bf16[128,1024]{1,0:T(8,128)(2,1)S(1)}, bf16[128,1024]{1,0:T(8,128)(2,1)S(1)}, u32[]{:S(2)}, u32[]{:S(2)}) %collective-permute-start.33) | collective-permute-done | bytes 262176 | tf_op jit(solution)/shard_map/ppermute | solution.py:118
  81.1 2.0 %collective-permute-done.31.refs_3_.refs_5_ = bf16[64,1024]{1,0:T(8,128)(2,1)S(1)} collective-permute-done((bf16[64,1024]{1,0:T(8,128)(2,1)S(1)}, bf16[64,1024]{1,0:T(8,128)(2,1)S(1)}, u32[]{:S(2)}, u32[]{:S(2)}) %collective-permute-start.31) | collective-permute-done | bytes 131104 | tf_op jit(solution)/shard_map/ppermute | solution.py:118
  83.2 2.7 %collective-permute-start.39 = (bf16[64,1024]{1,0:T(8,128)(2,1)S(1)}, bf16[64,1024]{1,0:T(8,128)(2,1)S(1)}, u32[]{:S(2)}, u32[]{:S(2)}) collective-permute-start(bf16[64,1024]{1,0:T(8,128)(2,1)S(1)} %get-tuple-element.220), channel_id=1, source_target_pairs={{0,4},{1,5},{2,6},{3,7},{4,0},{5,1},{6,2},{7,3},{8,12},{9,13},{10,... | collective-permute-start | bytes 393224 | tf_op jit(solution)/shard_map/ppermute | solution.py:118
  88.5 2.5 %collective-permute-start.41 = (bf16[64,1024]{1,0:T(8,128)(2,1)S(1)}, bf16[64,1024]{1,0:T(8,128)(2,1)S(1)}, u32[]{:S(2)}, u32[]{:S(2)}) collective-permute-start(bf16[64,1024]{1,0:T(8,128)(2,1)S(1)} %get-tuple-element.231), channel_id=1, source_target_pairs={{0,6},{1,7},{2,4},{3,5},{4,2},{5,3},{6,0},{7,1},{8,14},{9,15},{10,... | collective-permute-start | bytes 393224 | tf_op jit(solution)/shard_map/ppermute | solution.py:118
  98.0 1.8 %keep.1 = (bf16[128,1024]{1,0:T(8,128)(2,1)}, bf16[2080,256]{1,0:T(8,128)(2,1)S(1)}, f32[8,128]{1,0:T(8,128)S(1)}) custom-call(bf16[128,1024]{1,0:T(8,128)(2,1)S(1)} %get-tuple-element.237.refs_0_, bf16[128,1024]{1,0:T(8,128)(2,1)S(1)} %get-tuple-element.238.refs_1_, bf16[16,1024]{1,0:T(8,128)(2,1)S(1)} %get-tuple-element.234.refs_8_.refs_2_, ...), custom_call_target="tpu_custom_call" | custom-call | tf_op jit(solution)/shard_map/keep/pallas_call | solution.py:66
  102.3 3.8 %weights.3 = (bf16[1024,1024]{1,0:T(8,128)(2,1)}, f32[8,128]{1,0:T(8,128)S(1)}) custom-call(bf16[512,1024]{1,0:T(8,128)(2,1)S(1)} %get-tuple-element.245.refs_0_, bf16[512,1024]{1,0:T(8,128)(2,1)S(1)} %get-tuple-element.246.refs_1_, bf16[512,1024]{1,0:T(8,128)(2,1)S(1)} %get-tuple-element.247.refs_2_, bf16[512,1024]{1,0:T(8,128)(2,1)S(1)} %get-tuple-element.248.refs_3_, ...), custom_call_target="tpu_custom_call" | custom-call | tf_op jit(solution)/shard_map/weights/pallas_call | solution.py:66
  106.1 3.2 %collective-permute-done.43.refs_2_ = bf16[528,256]{1,0:T(8,128)(2,1)S(1)} collective-permute-done((bf16[528,256]{1,0:T(8,128)(2,1)S(1)}, bf16[528,256]{1,0:T(8,128)(2,1)S(1)}, u32[]{:S(2)}, u32[]{:S(2)}) %collective-permute-start.43) | collective-permute-done | bytes 270368 | tf_op jit(solution)/shard_map/ppermute | solution.py:118
  111.2 4.0 %collective-permute-done.46.refs_3_ = bf16[256,256]{1,0:T(8,128)(2,1)S(1)} collective-permute-done((bf16[256,256]{1,0:T(8,128)(2,1)S(1)}, bf16[256,256]{1,0:T(8,128)(2,1)S(1)}, u32[]{:S(2)}, u32[]{:S(2)}) %collective-permute-start.46) | collective-permute-done | bytes 131104 | tf_op jit(solution)/shard_map/ppermute | solution.py:118
  117.9 1.8 %collective-permute-start.49 = (bf16[144,256]{1,0:T(8,128)(2,1)S(1)}, bf16[144,256]{1,0:T(8,128)(2,1)S(1)}, u32[]{:S(2)}, u32[]{:S(2)}) collective-permute-start(bf16[144,256]{1,0:T(8,128)(2,1)S(1)} %get-tuple-element.261), channel_id=1, source_target_pairs={{0,6},{1,7},{2,4},{3,5},{4,2},{5,3},{6,0},{7,1},{8,14},{9,15},{10,... | collective-permute-start | bytes 221192 | tf_op jit(solution)/shard_map/ppermute | solution.py:118
  119.7 2.4 %collective-permute-done.47.refs_1_ = bf16[144,256]{1,0:T(8,128)(2,1)S(1)} collective-permute-done((bf16[144,256]{1,0:T(8,128)(2,1)S(1)}, bf16[144,256]{1,0:T(8,128)(2,1)S(1)}, u32[]{:S(2)}, u32[]{:S(2)}) %collective-permute-start.47) | collective-permute-done | bytes 73760 | tf_op jit(solution)/shard_map/ppermute | solution.py:118
  122.1 1.9 %collective-permute-done.49.refs_3_ = bf16[144,256]{1,0:T(8,128)(2,1)S(1)} collective-permute-done((bf16[144,256]{1,0:T(8,128)(2,1)S(1)}, bf16[144,256]{1,0:T(8,128)(2,1)S(1)}, u32[]{:S(2)}, u32[]{:S(2)}) %collective-permute-start.49) | collective-permute-done | bytes 73760 | tf_op jit(solution)/shard_map/ppermute | solution.py:118
  126.0 2.7 %collective-permute-done.52.refs_3_ = bf16[144,256]{1,0:T(8,128)(2,1)S(1)} collective-permute-done((bf16[144,256]{1,0:T(8,128)(2,1)S(1)}, bf16[144,256]{1,0:T(8,128)(2,1)S(1)}, u32[]{:S(2)}, u32[]{:S(2)}) %collective-permute-start.52) | collective-permute-done | bytes 73760 | tf_op jit(solution)/shard_map/ppermute | solution.py:118
  (136 shorter events, 51.9 us)
Async XLA Ops:
  5.1 11.0 %collective-permute-start.1 = (bf16[128,1024]{1,0:T(8,128)(2,1)}, bf16[128,1024]{1,0:T(8,128)(2,1)S(1)}, u32[]{:S(2)}, u32[]{:S(2)}) collective-permute-start(bf16[128,1024]{1,0:T(8,128)(2,1)} %get-tuple-element.141), channel_id=1, source_target_pairs={{0,1},{1,0},{2,3},{3,2},{4,5},{5,4},{6,7},{7,6},{8,9},{9,8},{10,11... | collective-permute-start | bytes 786440 | tf_op jit(solution)/shard_map/ppermute | solution.py:118
  8.1 7.9 %collective-permute-start = (bf16[32,1024]{1,0:T(8,128)(2,1)S(1)}, bf16[32,1024]{1,0:T(8,128)(2,1)S(1)}, u32[]{:S(2)}, u32[]{:S(2)}) collective-permute-start(bf16[32,1024]{1,0:T(8,128)(2,1)S(1)} %get-tuple-element.139), channel_id=1, source_target_pairs={{0,1},{1,0},{2,3},{3,2},{4,5},{5,4},{6,7},{7,6},{8,9},{9,8},{10,11... | collective-permute-start | bytes 196616 | tf_op jit(solution)/shard_map/ppermute | solution.py:118
  8.2 12.8 %collective-permute-start.2 = (bf16[64,1024]{1,0:T(8,128)(2,1)S(1)}, bf16[64,1024]{1,0:T(8,128)(2,1)S(1)}, u32[]{:S(2)}, u32[]{:S(2)}) collective-permute-start(bf16[64,1024]{1,0:T(8,128)(2,1)S(1)} %get-tuple-element.145), channel_id=1, source_target_pairs={{0,4},{1,5},{2,6},{3,7},{4,0},{5,1},{6,2},{7,3},{8,12},{9,13},{10,... | collective-permute-start | bytes 393224 | tf_op jit(solution)/shard_map/ppermute | solution.py:118
  11.2 9.8 %collective-permute-start.5 = (bf16[64,1024]{1,0:T(8,128)(2,1)S(1)}, bf16[64,1024]{1,0:T(8,128)(2,1)S(1)}, u32[]{:S(2)}, u32[]{:S(2)}) collective-permute-start(bf16[64,1024]{1,0:T(8,128)(2,1)S(1)} %get-tuple-element.146), channel_id=1, source_target_pairs={{0,2},{1,3},{2,0},{3,1},{4,6},{5,7},{6,4},{7,5},{8,10},{9,11},{10,... | collective-permute-start | bytes 393224 | tf_op jit(solution)/shard_map/ppermute | solution.py:118
  12.8 8.2 %collective-permute-start.6 = (bf16[64,1024]{1,0:T(8,128)(2,1)S(1)}, bf16[64,1024]{1,0:T(8,128)(2,1)S(1)}, u32[]{:S(2)}, u32[]{:S(2)}) collective-permute-start(bf16[64,1024]{1,0:T(8,128)(2,1)S(1)} %get-tuple-element.147), channel_id=1, source_target_pairs={{0,6},{1,7},{2,4},{3,5},{4,2},{5,3},{6,0},{7,1},{8,14},{9,15},{10,... | collective-permute-start | bytes 393224 | tf_op jit(solution)/shard_map/ppermute | solution.py:118
  25.4 11.6 %collective-permute-start.9 = (bf16[64,1024]{1,0:T(8,128)(2,1)S(1)}, bf16[64,1024]{1,0:T(8,128)(2,1)S(1)}, u32[]{:S(2)}, u32[]{:S(2)}) collective-permute-start(bf16[64,1024]{1,0:T(8,128)(2,1)S(1)} %get-tuple-element.153), channel_id=1, source_target_pairs={{0,4},{1,5},{2,6},{3,7},{4,0},{5,1},{6,2},{7,3},{8,12},{9,13},{10,... | collective-permute-start | bytes 393224 | tf_op jit(solution)/shard_map/ppermute | solution.py:118
  28.0 9.0 %collective-permute-start.10 = (bf16[64,1024]{1,0:T(8,128)(2,1)S(1)}, bf16[64,1024]{1,0:T(8,128)(2,1)S(1)}, u32[]{:S(2)}, u32[]{:S(2)}) collective-permute-start(bf16[64,1024]{1,0:T(8,128)(2,1)S(1)} %get-tuple-element.154), channel_id=1, source_target_pairs={{0,2},{1,3},{2,0},{3,1},{4,6},{5,7},{6,4},{7,5},{8,10},{9,11},{10,... | collective-permute-start | bytes 393224 | tf_op jit(solution)/shard_map/ppermute | solution.py:118
  29.5 7.4 %collective-permute-start.11 = (bf16[64,1024]{1,0:T(8,128)(2,1)S(1)}, bf16[64,1024]{1,0:T(8,128)(2,1)S(1)}, u32[]{:S(2)}, u32[]{:S(2)}) collective-permute-start(bf16[64,1024]{1,0:T(8,128)(2,1)S(1)} %get-tuple-element.155), channel_id=1, source_target_pairs={{0,6},{1,7},{2,4},{3,5},{4,2},{5,3},{6,0},{7,1},{8,14},{9,15},{10,... | collective-permute-start | bytes 393224 | tf_op jit(solution)/shard_map/ppermute | solution.py:118
  29.8 13.4 %collective-permute-start.13 = (bf16[192,1024]{1,0:T(8,128)(2,1)S(1)}, bf16[192,1024]{1,0:T(8,128)(2,1)S(1)}, u32[]{:S(2)}, u32[]{:S(2)}) collective-permute-start(bf16[192,1024]{1,0:T(8,128)(2,1)S(1)} %get-tuple-element.161), channel_id=1, source_target_pairs={{0,16},{8,24},{16,0},{24,8},{1,17},{9,25},{17,1},{25,9},{2,18},{10... | collective-permute-start | bytes 1179656 | tf_op jit(solution)/shard_map/ppermute | solution.py:118
  30.6 7.7 %collective-permute-start.8 = (bf16[256,1024]{1,0:T(8,128)(2,1)S(1)}, bf16[256,1024]{1,0:T(8,128)(2,1)S(1)}, u32[]{:S(2)}, u32[]{:S(2)}) collective-permute-start(bf16[256,1024]{1,0:T(8,128)(2,1)S(1)} %get-tuple-element.151.refs_0_), channel_id=1, source_target_pairs={{0,8},{8,0},{16,24},{24,16},{1,9},{9,1},{17,25},{25,17},{2,10},{10... | collective-permute-start | bytes 1572872 | tf_op jit(solution)/shard_map/ppermute | solution.py:118
  37.0 15.9 %collective-permute-start.23 = (bf16[256,1024]{1,0:T(8,128)(2,1)S(1)}, bf16[256,1024]{1,0:T(8,128)(2,1)S(1)}, u32[]{:S(2)}, u32[]{:S(2)}) collective-permute-start(bf16[256,1024]{1,0:T(8,128)(2,1)S(1)} %get-tuple-element.176.refs_0_), channel_id=1, source_target_pairs={{0,16},{8,24},{16,0},{24,8},{1,17},{9,25},{17,1},{25,9},{2,18},{10... | collective-permute-start | bytes 1572872 | tf_op jit(solution)/shard_map/ppermute | solution.py:118
  53.6 16.0 %collective-permute-start.12 = (bf16[256,1024]{1,0:T(8,128)(2,1)S(1)}, bf16[256,1024]{1,0:T(8,128)(2,1)S(1)}, u32[]{:S(2)}, u32[]{:S(2)}) collective-permute-start(bf16[256,1024]{1,0:T(8,128)(2,1)S(1)} %get-tuple-element.159), channel_id=1, source_target_pairs={{0,8},{8,0},{16,24},{24,16},{1,9},{9,1},{17,25},{25,17},{2,10},{10... | collective-permute-start | bytes 1572872 | tf_op jit(solution)/shard_map/ppermute | solution.py:118
  53.9 15.8 %collective-permute-start.22 = (bf16[256,1024]{1,0:T(8,128)(2,1)S(1)}, bf16[256,1024]{1,0:T(8,128)(2,1)S(1)}, u32[]{:S(2)}, u32[]{:S(2)}) collective-permute-start(bf16[256,1024]{1,0:T(8,128)(2,1)S(1)} %get-tuple-element.175), channel_id=1, source_target_pairs={{0,16},{8,24},{16,0},{24,8},{1,17},{9,25},{17,1},{25,9},{2,18},{10... | collective-permute-start | bytes 1572872 | tf_op jit(solution)/shard_map/ppermute | solution.py:118
  62.3 10.7 %collective-permute-start.32 = (bf16[256,1024]{1,0:T(8,128)(2,1)S(1)}, bf16[256,1024]{1,0:T(8,128)(2,1)S(1)}, u32[]{:S(2)}, u32[]{:S(2)}) collective-permute-start(bf16[256,1024]{1,0:T(8,128)(2,1)S(1)} %get-tuple-element.203), channel_id=1, source_target_pairs={{0,8},{8,0},{16,24},{24,16},{1,9},{9,1},{17,25},{25,17},{2,10},{10... | collective-permute-start | bytes 1572872 | tf_op jit(solution)/shard_map/ppermute | solution.py:118
  63.9 10.6 %collective-permute-start.34 = (bf16[128,1024]{1,0:T(8,128)(2,1)S(1)}, bf16[128,1024]{1,0:T(8,128)(2,1)S(1)}, u32[]{:S(2)}, u32[]{:S(2)}) collective-permute-start(bf16[128,1024]{1,0:T(8,128)(2,1)S(1)} %get-tuple-element.205), channel_id=1, source_target_pairs={{0,16},{8,24},{16,0},{24,8},{1,17},{9,25},{17,1},{25,9},{2,18},{10... | collective-permute-start | bytes 786440 | tf_op jit(solution)/shard_map/ppermute | solution.py:118
  68.3 10.9 %collective-permute-start.33 = (bf16[128,1024]{1,0:T(8,128)(2,1)S(1)}, bf16[128,1024]{1,0:T(8,128)(2,1)S(1)}, u32[]{:S(2)}, u32[]{:S(2)}) collective-permute-start(bf16[128,1024]{1,0:T(8,128)(2,1)S(1)} %get-tuple-element.204), channel_id=1, source_target_pairs={{0,16},{8,24},{16,0},{24,8},{1,17},{9,25},{17,1},{25,9},{2,18},{10... | collective-permute-start | bytes 786440 | tf_op jit(solution)/shard_map/ppermute | solution.py:118
  69.9 11.3 %collective-permute-start.29 = (bf16[64,1024]{1,0:T(8,128)(2,1)S(1)}, bf16[64,1024]{1,0:T(8,128)(2,1)S(1)}, u32[]{:S(2)}, u32[]{:S(2)}) collective-permute-start(bf16[64,1024]{1,0:T(8,128)(2,1)S(1)} %get-tuple-element.199), channel_id=1, source_target_pairs={{0,4},{1,5},{2,6},{3,7},{4,0},{5,1},{6,2},{7,3},{8,12},{9,13},{10,... | collective-permute-start | bytes 393224 | tf_op jit(solution)/shard_map/ppermute | solution.py:118
  72.8 8.4 %collective-permute-start.30 = (bf16[64,1024]{1,0:T(8,128)(2,1)S(1)}, bf16[64,1024]{1,0:T(8,128)(2,1)S(1)}, u32[]{:S(2)}, u32[]{:S(2)}) collective-permute-start(bf16[64,1024]{1,0:T(8,128)(2,1)S(1)} %get-tuple-element.200), channel_id=1, source_target_pairs={{0,2},{1,3},{2,0},{3,1},{4,6},{5,7},{6,4},{7,5},{8,10},{9,11},{10,... | collective-permute-start | bytes 393224 | tf_op jit(solution)/shard_map/ppermute | solution.py:118
  73.0 10.2 %collective-permute-start.31 = (bf16[64,1024]{1,0:T(8,128)(2,1)S(1)}, bf16[64,1024]{1,0:T(8,128)(2,1)S(1)}, u32[]{:S(2)}, u32[]{:S(2)}) collective-permute-start(bf16[64,1024]{1,0:T(8,128)(2,1)S(1)} %get-tuple-element.201), channel_id=1, source_target_pairs={{0,6},{1,7},{2,4},{3,5},{4,2},{5,3},{6,0},{7,1},{8,14},{9,15},{10,... | collective-permute-start | bytes 393224 | tf_op jit(solution)/shard_map/ppermute | solution.py:118
  74.7 8.5 %collective-permute-start.36 = (bf16[64,1024]{1,0:T(8,128)(2,1)S(1)}, bf16[64,1024]{1,0:T(8,128)(2,1)S(1)}, u32[]{:S(2)}, u32[]{:S(2)}) collective-permute-start(bf16[64,1024]{1,0:T(8,128)(2,1)S(1)} %get-tuple-element.213), channel_id=1, source_target_pairs={{0,1},{1,0},{2,3},{3,2},{4,5},{5,4},{6,7},{7,6},{8,9},{9,8},{10,11... | collective-permute-start | bytes 393224 | tf_op jit(solution)/shard_map/ppermute | solution.py:118
  83.2 8.5 %collective-permute-start.39 = (bf16[64,1024]{1,0:T(8,128)(2,1)S(1)}, bf16[64,1024]{1,0:T(8,128)(2,1)S(1)}, u32[]{:S(2)}, u32[]{:S(2)}) collective-permute-start(bf16[64,1024]{1,0:T(8,128)(2,1)S(1)} %get-tuple-element.220), channel_id=1, source_target_pairs={{0,4},{1,5},{2,6},{3,7},{4,0},{5,1},{6,2},{7,3},{8,12},{9,13},{10,... | collective-permute-start | bytes 393224 | tf_op jit(solution)/shard_map/ppermute | solution.py:118
  88.5 7.6 %collective-permute-start.41 = (bf16[64,1024]{1,0:T(8,128)(2,1)S(1)}, bf16[64,1024]{1,0:T(8,128)(2,1)S(1)}, u32[]{:S(2)}, u32[]{:S(2)}) collective-permute-start(bf16[64,1024]{1,0:T(8,128)(2,1)S(1)} %get-tuple-element.231), channel_id=1, source_target_pairs={{0,6},{1,7},{2,4},{3,5},{4,2},{5,3},{6,0},{7,1},{8,14},{9,15},{10,... | collective-permute-start | bytes 393224 | tf_op jit(solution)/shard_map/ppermute | solution.py:118
  100.7 8.6 %collective-permute-start.43 = (bf16[528,256]{1,0:T(8,128)(2,1)S(1)}, bf16[528,256]{1,0:T(8,128)(2,1)S(1)}, u32[]{:S(2)}, u32[]{:S(2)}) collective-permute-start(bf16[528,256]{1,0:T(8,128)(2,1)S(1)} %get-tuple-element.244), channel_id=1, source_target_pairs={{0,16},{8,24},{16,0},{24,8},{1,17},{9,25},{17,1},{25,9},{2,18},{10... | collective-permute-start | bytes 811016 | tf_op jit(solution)/shard_map/ppermute | solution.py:118
  101.8 8.2 %collective-permute-start.45 = (bf16[512,256]{1,0:T(8,128)(2,1)S(1)}, bf16[512,256]{1,0:T(8,128)(2,1)S(1)}, u32[]{:S(2)}, u32[]{:S(2)}) collective-permute-start(bf16[512,256]{1,0:T(8,128)(2,1)S(1)} %get-tuple-element.253), channel_id=1, source_target_pairs={{0,1},{1,0},{2,3},{3,2},{4,5},{5,4},{6,7},{7,6},{8,9},{9,8},{10,11... | collective-permute-start | bytes 786440 | tf_op jit(solution)/shard_map/ppermute | solution.py:118
  (39 other events, 223.8 us)

commit v5 on v4

--- a/solution.py
+++ b/solution.py
@@ -234,20 +234,16 @@
     norm_own, norm_rest = line.move(whole(*early) + rest, rest, name="pack_norm_x")
     norm_far = [norm_far, swap(norm_rest, "dp", far)]
     norm_core = swap(norm_own, "dp", 1)
-    cot_own = line.move(whole(*cot_high), flops=WAIT, name="pack_cot_x")[0]
-    cot_far = [swap(cot_own, "dp", far)]
-    cot_core = swap(cot_own, "dp", 1)
-
     block = 256 if hidden % 256 == 0 else hidden
 
     def forward(parts, pieces):
         rows = sum(x.shape[0] for x in parts)
-        piece = rows // 2 // pieces
+        piece = rows // pieces
 
         def body(*refs):
             ins = refs[: len(parts)]
-            router_ref, in_ref, down_ref, rows_hbm, act_hbm, der_ref, gate_ref, keep_ref = refs[len(parts) : len(parts) + 8]
-            sends, (rows_ref, act_ref, total, sems) = refs[len(parts) + 8 : -4], refs[-4:]
+            router_ref, in_ref, down_ref, rows_hbm, act_hbm, der_ref, gate_ref = refs[len(parts) : len(parts) + 7]
+            sums, (rows_ref, act_ref, total, sems) = refs[len(parts) + 7 : -4], refs[-4:]
             at = 0
             for ref in ins:
                 rows_ref[at : at + ref.shape[0], :] = ref[...]
@@ -263,9 +259,8 @@
                 term = mm(act, down_ref[at, :])
                 total[...] = term if j == 0 else total[...] + term
             stores[1].start()
-            keep_ref[...] = total[: rows // 2, :].astype(BF)
             for i in range(pieces):
-                sends[i][...] = total[rows // 2 + i * piece : rows // 2 + (i + 1) * piece, :].astype(BF)
+                sums[i][...] = total[i * piece : (i + 1) * piece, :].astype(BF)
             logits = mm(rows_ref[...], router_ref[...], NT)
             lanes = lax.broadcasted_iota(jnp.int32, logits.shape, 1)
             picked = jnp.sum(jnp.where(lanes == lax.axis_index("expert"), logits, 0.0), axis=1, keepdims=True)
@@ -275,22 +270,22 @@
 
         *results, = line.call(
             body,
-            [shape((rows, width)), shape((rows, hidden)), shape((rows, hidden)), shape((rows, 1), F32),
-             shape((rows // 2, width))] + [shape((piece, width))] * pieces,
+            [shape((rows, width)), shape((rows, hidden)), shape((rows, hidden)), shape((rows, 1), F32)]
+            + [shape((piece, width))] * pieces,
             (*parts, router_t, weight_in, weight_down),
-            out_specs=[HBM] * 2 + [VMEM] * (3 + pieces),
+            out_specs=[HBM] * 2 + [VMEM] * (2 + pieces),
             scratch=[pltpu.VMEM((rows, width), BF), pltpu.VMEM((rows, hidden), BF), pltpu.VMEM((rows, width), F32), DMA((2,))],
             vmem=20 * MIB, name="forward")
-        return (*results[:5], results[5:])
+        return (*results[:4], results[4:])
 
     def backward(parts, gate, der, pieces):
         rows = sum(x.shape[0] for x in parts)
-        piece = rows // 2 // pieces
+        piece = rows // pieces
 
         def body(*refs):
             ins, refs = refs[: len(parts)], refs[len(parts) :]
-            gate_ref, der_ref, in_ref, down_ref, grads_hbm, pre_hbm, keep_ref = refs[:7]
-            sends, (grads_ref, pre_ref, total, sems) = refs[7 : 7 + pieces], refs[7 + pieces :]
+            gate_ref, der_ref, in_ref, down_ref, grads_hbm, pre_hbm = refs[:6]
+            sums, (grads_ref, pre_ref, total, sems) = refs[6 : 6 + pieces], refs[6 + pieces :]
             first = 0
             for ref in ins:
                 at = slice(first, first + ref.shape[0])
@@ -306,20 +301,19 @@
                 term = mm(pre, in_ref[:, at], NT)
                 total[...] = term if j == 0 else total[...] + term
             stores[1].start()
-            keep_ref[...] = total[: rows // 2, :].astype(BF)
             for i in range(pieces):
-                sends[i][...] = total[rows // 2 + i * piece : rows // 2 + (i + 1) * piece, :].astype(BF)
+                sums[i][...] = total[i * piece : (i + 1) * piece, :].astype(BF)
             for store in stores:
                 store.wait()
 
-        grads, pre, keep, *sends = line.call(
+        grads, pre, *sums = line.call(
             body,
-            [shape((rows, width)), shape((rows, hidden)), shape((rows // 2, width))] + [shape((piece, width))] * pieces,
+            [shape((rows, width)), shape((rows, hidden))] + [shape((piece, width))] * pieces,
             (*parts, gate, der, weight_in, weight_down),
-            out_specs=[HBM] * 2 + [VMEM] * (1 + pieces),
+            out_specs=[HBM] * 2 + [VMEM] * pieces,
             scratch=[pltpu.VMEM((rows, width), BF), pltpu.VMEM((rows, hidden), BF), pltpu.VMEM((rows, width), F32), DMA((2,))],
             vmem=20 * MIB, name="backward")
-        return grads, pre, keep, sends
+        return grads, pre, sums
 
     half = slots // 2
 
@@ -333,17 +327,27 @@
         joined, *parts = line.move(whole(*x), *taken, name="relay")
         return [joined] + [swap(part, "dp", 1) for part in parts]
 
-    rows_n, act_n, der_n, gate_n, keep_n, send_n = forward([norm_own, norm_core], 1)
-    near_out = swap(send_n[0], "dp", 1)
-    rows_f, act_f, der_f, gate_f, keep_f, send_f = forward(relay(norm_far, PIECES), PIECES)
-    core_out = [swap(x, "dp", 1) for x in send_f]
-    far_out = line.move([(x.shape[0], [(keep_f, i * x.shape[0]), (x, 0)]) for i, x in enumerate(core_out)], name="sum_core_out")[0]
+    own = forward([norm_own], 1)
+    cot_own = line.move(whole(*cot_high), flops=WAIT, name="pack_cot_x")[0]
+    cot_far = [swap(cot_own, "dp", far)]
+    cot_core = swap(cot_own, "dp", 1)
+    near = forward([norm_core], 1)
+    near_out = swap(near[4][0], "dp", 1)
+    whole_far, *pieces_far = relay(norm_far, PIECES)
+    away = forward([whole_far], 1)
+    cross = forward(pieces_far, PIECES)
+    core_out = [swap(x, "dp", 1) for x in cross[4]]
+    own_in = backward([cot_own], gate=own[3], der=own[2], pieces=1)
+    far_out = line.move([(x.shape[0], [(away[4][0], i * x.shape[0]), (x, 0)]) for i, x in enumerate(core_out)], name="sum_core_out")[0]
     far_out = swap(far_out, "dp", far)
-    cot_far = relay(cot_far, 2)
-    grads_n, pre_n, ikeep_n, isend_n = backward([cot_own, cot_core], gate_n, der_n, 1)
-    near_in = swap(isend_n[0], "dp", 1)
-    grads_f, pre_f, ikeep_f, isend_f = backward(cot_far, gate_f, der_f, 2)
-    core_in = [swap(x, "dp", 1) for x in isend_f]
+    whole_far, *pieces_far = relay(cot_far, 2)
+    near_back = backward([cot_core], gate=near[3], der=near[2], pieces=1)
+    near_in = swap(near_back[2][0], "dp", 1)
+    away_in = backward([whole_far], gate=away[3], der=away[2], pieces=1)
+    cross_back = backward(pieces_far, gate=cross[3], der=cross[2], pieces=2)
+    core_in = [swap(x, "dp", 1) for x in cross_back[2]]
+    fronts, backs = (own, near, away, cross), (own_in, near_back, away_in, cross_back)
+    keep_n, ikeep_n, ikeep_f = own[4][0], own_in[2][0], away_in[2][0]
     far_in = [swap(line.move([(half, [(ikeep_f, 0), (core_in[0], 0)])], name="sum_core_in")[0], "dp", far)]
 
     def weight_grad(lefts, rights):
@@ -377,13 +381,12 @@
                      DMA((len(lefts) + len(rights) + left // tile,))],
             vmem=20 * MIB, name="weights")[0]
 
-    grad_w_down = weight_grad((act_n, act_f), (grads_n, grads_f))
-    far_in.append(swap(line.move([(half, [(ikeep_f, half), (core_in[1], 0)])], name="sum_core_in")[0], "dp", far))
-
     quarter = slots // 4
     sums = line.move(
         *[[(quarter, [(x, c * quarter) for x in (keep_n, near_out, far_out)])] for c in range(4)], name="sum_x_out")
     out_high = [swap(x, "expert", masks[c] * low) if masks[c] else x for c, x in enumerate(sums)]
+
+    far_in.append(swap(line.move([(half, [(ikeep_f, half), (core_in[1], 0)])], name="sum_core_in")[0], "dp", far))
 
     def gather_in(i):
         terms = lambda at, rows: (rows, [(ikeep_n, i * half + at), (near_in, i * half + at), (far_in[i], at)])
@@ -397,6 +400,7 @@
         return [swap(b, "expert", masks[c] * low) if masks[c] else b for c, b in zip(chunks[i], blocks)]
 
     total_a = gather_in(0)
+    grad_w_down = weight_grad([f[1] for f in fronts], [b[0] for b in backs])
     total_b = gather_in(1)
     out_low = []
     if low > 1:
@@ -500,7 +504,7 @@
     sum_x = line.move(
         [(2 * low * per, two(span)), (spare, two(span + width))],
         *[[(per, two(spot(d, c, m))) for d in range(2) for c in (2, 3)] for m in range(1, low)], name="reduce_core")
-    grad_w_in = weight_grad((rows_n, rows_f), (pre_n, pre_f))
+    grad_w_in = weight_grad([f[0] for f in fronts], [b[1] for b in backs])
     first_x = swap(sum_x[0], "dp", far)
     second_low = [swap(x, "expert", m + 1) for m, x in enumerate(sum_x[1:])]
     first = line.move(

time: 131 us -> 129 us (0.985)
  waiting for transfers between devices: 43.6 us -> 37.5 us
  starting transfers between devices: 48.3 us -> 51.6 us
  Pallas kernels: 34.8 us -> 36.6 us
    ppermute x53, waiting for transfers between devices: 43.6 us -> 37.5 us  [swap(): lax.ppermute(x, axis, [(i, i ^ mask) for i in range(lax.axis_size(axis))])]
    ppermute x53, starting transfers between devices: 48.3 us -> 51.6 us  [swap(): lax.ppermute(x, axis, [(i, i ^ mask) for i in range(lax.axis_size(axis))])]
    pallas_call x34 -> x38, Pallas kernels: 34.8 us -> 36.6 us  [call(): pl.pallas_call(kernel, out_shape=[*outs, shape((8, LANES), F32)], in_spec...]
  transfers between devices with their start and end apart: 53 -> 53, of which waited for: 28 -> 21; matrix products, arithmetic and copies ran while one was open for 0% -> 0% of each run, Pallas kernels for 22% -> 23%
where the time goes in v5:
time: 129 us
  starting transfers between devices  51.6 us (40%)
  waiting for transfers between devices  37.5 us (29%)
  Pallas kernels  36.6 us (28%)
  local copies, waits for them, and re-layouts  2.45 us (2%)
    ppermute x53, starting transfers between devices, swap(): lax.ppermute(x, axis, [(i, i ^ mask) for i in range(lax.axis_size(axis))])  51.6 us
    ppermute x53, waiting for transfers between devices, swap(): lax.ppermute(x, axis, [(i, i ^ mask) for i in range(lax.axis_size(axis))])  37.5 us
    pallas_call x38, Pallas kernels, call(): pl.pallas_call(kernel, out_shape=[*outs, shape((8, LANES), F32)], in_spec...  36.6 us
  transfers between devices with their start and end apart: 53, of which 21 were waited for; matrix products, arithmetic and copies ran while one was open for 0% of the time, Pallas kernels for 23%

profile of v5, /device:TPU:0, one launch (start us, length us, event | category | flops | bytes accessed | tf_op | source)
XLA Modules:
  0.0 129.3 jit_solution(5517440651217401692)
XLA Ops:
  1.5 3.6 %head.1 = (bf16[128,1024]{1,0:T(8,128)(2,1)S(1)}, bf16[128,1024]{1,0:T(8,128)(2,1)}, s32[2,128]{1,0:T(2,128)S(1)}, bf16[128,1024]{1,0:T(8,128)(2,1)}, f32[128,1]...) custom-call(s32[2,128]{1,0:T(2,128)S(1)} %bitcast.31, ...), custom_call_target="tpu_custom_call" | custom-call | tf_op jit(solution)/shard_map/head/pallas_call | solution.py:66
  5.1 3.0 %collective-permute-start.1 = (bf16[128,1024]{1,0:T(8,128)(2,1)}, bf16[128,1024]{1,0:T(8,128)(2,1)S(1)}, u32[]{:S(2)}, u32[]{:S(2)}) collective-permute-start(bf16[128,1024]{1,0:T(8,128)(2,1)} %get-tuple-element.157), channel_id=1, source_target_pairs={{0,1},{1,0},{2,3},{3,2},{4,5},{5,4},{6,7},{7,6},{8,9},{9,8},{10,11... | collective-permute-start | bytes 786440 | tf_op jit(solution)/shard_map/ppermute | solution.py:118
  8.2 3.0 %collective-permute-start.2 = (bf16[64,1024]{1,0:T(8,128)(2,1)S(1)}, bf16[64,1024]{1,0:T(8,128)(2,1)S(1)}, u32[]{:S(2)}, u32[]{:S(2)}) collective-permute-start(bf16[64,1024]{1,0:T(8,128)(2,1)S(1)} %get-tuple-element.161), channel_id=1, source_target_pairs={{0,4},{1,5},{2,6},{3,7},{4,0},{5,1},{6,2},{7,3},{8,12},{9,13},{10,... | collective-permute-start | bytes 393224 | tf_op jit(solution)/shard_map/ppermute | solution.py:118
  12.8 3.2 %collective-permute-done.refs_1_ = bf16[32,1024]{1,0:T(8,128)(2,1)S(1)} collective-permute-done((bf16[32,1024]{1,0:T(8,128)(2,1)S(1)}, bf16[32,1024]{1,0:T(8,128)(2,1)S(1)}, u32[]{:S(2)}, u32[]{:S(2)}) %collective-permute-start) | collective-permute-done | bytes 65568 | tf_op jit(solution)/shard_map/ppermute | solution.py:118
  25.4 2.6 %collective-permute-start.9 = (bf16[64,1024]{1,0:T(8,128)(2,1)S(1)}, bf16[64,1024]{1,0:T(8,128)(2,1)S(1)}, u32[]{:S(2)}, u32[]{:S(2)}) collective-permute-start(bf16[64,1024]{1,0:T(8,128)(2,1)S(1)} %get-tuple-element.171), channel_id=1, source_target_pairs={{0,4},{1,5},{2,6},{3,7},{4,0},{5,1},{6,2},{7,3},{8,12},{9,13},{10,... | collective-permute-start | bytes 393224 | tf_op jit(solution)/shard_map/ppermute | solution.py:118
  30.6 2.6 %forward.4 = (bf16[256,1024]{1,0:T(8,128)(2,1)S(1)}, bf16[256,1024]{1,0:T(8,128)(2,1)S(1)}, bf16[256,1024]{1,0:T(8,128)(2,1)S(1)}, f32[256,1]{1,0:T(8,128)S(1)},...) custom-call(bf16[256,1024]{1,0:T(8,128)(2,1)S(1)} %get-tuple-element.167.refs_0_, bf16[8,1024]{1,0:T(8,128)(2,1)S(1)} %bitcast.25, ...), custom_call_target="tpu_custom_call" | custom-call | tf_op jit(solution)/shard_map/forward/pallas_call | solution.py:66
  33.2 3.8 %collective-permute-done.9.refs_1_ = bf16[64,1024]{1,0:T(8,128)(2,1)S(1)} collective-permute-done((bf16[64,1024]{1,0:T(8,128)(2,1)S(1)}, bf16[64,1024]{1,0:T(8,128)(2,1)S(1)}, u32[]{:S(2)}, u32[]{:S(2)}) %collective-permute-start.9) | collective-permute-done | bytes 131104 | tf_op jit(solution)/shard_map/ppermute | solution.py:118
  38.3 2.5 %forward.5 = (bf16[256,1024]{1,0:T(8,128)(2,1)S(1)}, bf16[256,1024]{1,0:T(8,128)(2,1)S(1)}, bf16[256,1024]{1,0:T(8,128)(2,1)S(1)}, f32[256,1]{1,0:T(8,128)S(1)},...) custom-call(bf16[256,1024]{1,0:T(8,128)(2,1)S(1)} %collective-permute-done.8.refs_0_, bf16[8,1024]{1,0:T(8,128)(2,1)S(1)} %bitcast.26, ...), custom_call_target="tpu_custom_call" | custom-call | tf_op jit(solution)/shard_map/forward/pallas_call | solution.py:66
  42.1 2.5 %forward.6 = (bf16[256,1024]{1,0:T(8,128)(2,1)S(1)}, bf16[256,1024]{1,0:T(8,128)(2,1)S(1)}, bf16[256,1024]{1,0:T(8,128)(2,1)S(1)}, f32[256,1]{1,0:T(8,128)S(1)},...) custom-call(bf16[256,1024]{1,0:T(8,128)(2,1)S(1)} %get-tuple-element.180.refs_0_, bf16[8,1024]{1,0:T(8,128)(2,1)S(1)} %bitcast.27, ...), custom_call_target="tpu_custom_call" | custom-call | tf_op jit(solution)/shard_map/forward/pallas_call | solution.py:66
  44.7 2.5 %forward.7 = (bf16[256,1024]{1,0:T(8,128)(2,1)S(1)}, bf16[256,1024]{1,0:T(8,128)(2,1)S(1)}, bf16[256,1024]{1,0:T(8,128)(2,1)S(1)}, f32[256,1]{1,0:T(8,128)S(1)},...) custom-call(bf16[64,1024]{1,0:T(8,128)(2,1)S(1)} %collective-permute, ...), custom_call_target="tpu_custom_call" | custom-call | tf_op jit(solution)/shard_map/forward/pallas_call | solution.py:66
  52.7 2.1 %backward.5 = (bf16[256,1024]{1,0:T(8,128)(2,1)S(1)}, bf16[256,1024]{1,0:T(8,128)(2,1)S(1)}, bf16[256,1024]{1,0:T(8,128)(2,1)S(1)}, f32[8,128]{1,0:T(8,128)S(1)}) custom-call(bf16[256,1024]{1,0:T(8,128)(2,1)S(1)} %collective-permute-done.24.refs_0_, f32[256,1]{1,0:T(8,128)S(1)} %get-tuple-element.202.refs_1_, ...), custom_call_target="tpu_custom_call" | custom-call | tf_op jit(solution)/shard_map/backward/pallas_call | solution.py:66
  56.7 1.9 %backward.7 = (bf16[256,1024]{1,0:T(8,128)(2,1)S(1)}, bf16[256,1024]{1,0:T(8,128)(2,1)S(1)}, bf16[128,1024]{1,0:T(8,128)(2,1)S(1)}, bf16[128,1024]{1,0:T(8,128)(2,1)S(1)}, f32[8,128]{1,0:T(8,128)S(1)}) custom-call(bf16[128,1024]{1,0:T(8,128)(2,1)S(1)} %collective-permute-done.25.refs_0_, bf16[128,1024]{1,0:T(8,128)(2,1)S(1)} %collective-permute-done.26.refs_1_, ...), custom_call_target="tpu_custom_call" | custom-call | tf_op jit(solution)/shard_map/backward/pallas_call | solution.py:66
  61.6 5.1 %collective-permute-done.22.refs_2_ = bf16[256,1024]{1,0:T(8,128)(2,1)S(1)} collective-permute-done((bf16[256,1024]{1,0:T(8,128)(2,1)S(1)}, bf16[256,1024]{1,0:T(8,128)(2,1)S(1)}, u32[]{:S(2)}, u32[]{:S(2)}) %collective-permute-start.22) | collective-permute-done | bytes 524320 | tf_op jit(solution)/shard_map/ppermute | solution.py:118
  67.8 3.1 %collective-permute-start.28 = (bf16[64,1024]{1,0:T(8,128)(2,1)S(1)}, bf16[64,1024]{1,0:T(8,128)(2,1)S(1)}, u32[]{:S(2)}, u32[]{:S(2)}) collective-permute-start(bf16[64,1024]{1,0:T(8,128)(2,1)S(1)} %get-tuple-element.216), channel_id=1, source_target_pairs={{0,4},{1,5},{2,6},{3,7},{4,0},{5,1},{6,2},{7,3},{8,12},{9,13},{10,... | collective-permute-start | bytes 393224 | tf_op jit(solution)/shard_map/ppermute | solution.py:118
  72.4 2.0 %collective-permute-start.36 = (bf16[64,1024]{1,0:T(8,128)(2,1)S(1)}, bf16[64,1024]{1,0:T(8,128)(2,1)S(1)}, u32[]{:S(2)}, u32[]{:S(2)}) collective-permute-start(bf16[64,1024]{1,0:T(8,128)(2,1)S(1)} %get-tuple-element.241), channel_id=1, source_target_pairs={{0,1},{1,0},{2,3},{3,2},{4,5},{5,4},{6,7},{7,6},{8,9},{9,8},{10,11... | collective-permute-start | bytes 393224 | tf_op jit(solution)/shard_map/ppermute | solution.py:118
  74.4 3.6 %weights.2 = (bf16[1024,1024]{1,0:T(8,128)(2,1)}, f32[8,128]{1,0:T(8,128)S(1)}) custom-call(bf16[256,1024]{1,0:T(8,128)(2,1)S(1)} %get-tuple-element.224.refs_0_, bf16[256,1024]{1,0:T(8,128)(2,1)S(1)} %get-tuple-element.225.refs_1_, bf16[256,1024]{1,0:T(8,128)(2,1)S(1)} %get-tuple-element.226.refs_2_, bf16[256,1024]{1,0:T(8,128)(2,1)S(1)} %get-tuple-element.227.refs_3_, ...), custom_call_target="tpu_custom_call" | custom-call | tf_op jit(solution)/shard_map/weights/pallas_call | solution.py:66
  80.2 2.6 %collective-permute-start.39 = (bf16[64,1024]{1,0:T(8,128)(2,1)S(1)}, bf16[64,1024]{1,0:T(8,128)(2,1)S(1)}, u32[]{:S(2)}, u32[]{:S(2)}) collective-permute-start(bf16[64,1024]{1,0:T(8,128)(2,1)S(1)} %get-tuple-element.248), channel_id=1, source_target_pairs={{0,4},{1,5},{2,6},{3,7},{4,0},{5,1},{6,2},{7,3},{8,12},{9,13},{10,... | collective-permute-start | bytes 393224 | tf_op jit(solution)/shard_map/ppermute | solution.py:118
  86.6 2.2 %collective-permute-start.41 = (bf16[64,1024]{1,0:T(8,128)(2,1)S(1)}, bf16[64,1024]{1,0:T(8,128)(2,1)S(1)}, u32[]{:S(2)}, u32[]{:S(2)}) collective-permute-start(bf16[64,1024]{1,0:T(8,128)(2,1)S(1)} %get-tuple-element.259), channel_id=1, source_target_pairs={{0,6},{1,7},{2,4},{3,5},{4,2},{5,3},{6,0},{7,1},{8,14},{9,15},{10,... | collective-permute-start | bytes 393224 | tf_op jit(solution)/shard_map/ppermute | solution.py:118
  100.7 3.8 %weights.3 = (bf16[1024,1024]{1,0:T(8,128)(2,1)}, f32[8,128]{1,0:T(8,128)S(1)}) custom-call(bf16[256,1024]{1,0:T(8,128)(2,1)S(1)} %get-tuple-element.273.refs_0_, bf16[256,1024]{1,0:T(8,128)(2,1)S(1)} %get-tuple-element.274.refs_1_, bf16[256,1024]{1,0:T(8,128)(2,1)S(1)} %get-tuple-element.275.refs_2_, bf16[256,1024]{1,0:T(8,128)(2,1)S(1)} %get-tuple-element.276.refs_3_, ...), custom_call_target="tpu_custom_call" | custom-call | tf_op jit(solution)/shard_map/weights/pallas_call | solution.py:66
  104.5 2.0 %collective-permute-done.43.refs_2_ = bf16[528,256]{1,0:T(8,128)(2,1)S(1)} collective-permute-done((bf16[528,256]{1,0:T(8,128)(2,1)S(1)}, bf16[528,256]{1,0:T(8,128)(2,1)S(1)}, u32[]{:S(2)}, u32[]{:S(2)}) %collective-permute-start.43) | collective-permute-done | bytes 270368 | tf_op jit(solution)/shard_map/ppermute | solution.py:118
  109.6 4.0 %collective-permute-done.46.refs_3_ = bf16[256,256]{1,0:T(8,128)(2,1)S(1)} collective-permute-done((bf16[256,256]{1,0:T(8,128)(2,1)S(1)}, bf16[256,256]{1,0:T(8,128)(2,1)S(1)}, u32[]{:S(2)}, u32[]{:S(2)}) %collective-permute-start.46) | collective-permute-done | bytes 131104 | tf_op jit(solution)/shard_map/ppermute | solution.py:118
  116.0 2.1 %collective-permute-start.49 = (bf16[144,256]{1,0:T(8,128)(2,1)S(1)}, bf16[144,256]{1,0:T(8,128)(2,1)S(1)}, u32[]{:S(2)}, u32[]{:S(2)}) collective-permute-start(bf16[144,256]{1,0:T(8,128)(2,1)S(1)} %get-tuple-element.293), channel_id=1, source_target_pairs={{0,6},{1,7},{2,4},{3,5},{4,2},{5,3},{6,0},{7,1},{8,14},{9,15},{10,... | collective-permute-start | bytes 221192 | tf_op jit(solution)/shard_map/ppermute | solution.py:118
  118.1 2.3 %collective-permute-done.47.refs_1_ = bf16[144,256]{1,0:T(8,128)(2,1)S(1)} collective-permute-done((bf16[144,256]{1,0:T(8,128)(2,1)S(1)}, bf16[144,256]{1,0:T(8,128)(2,1)S(1)}, u32[]{:S(2)}, u32[]{:S(2)}) %collective-permute-start.47) | collective-permute-done | bytes 73760 | tf_op jit(solution)/shard_map/ppermute | solution.py:118
  124.2 2.6 %collective-permute-done.52.refs_3_ = bf16[144,256]{1,0:T(8,128)(2,1)S(1)} collective-permute-done((bf16[144,256]{1,0:T(8,128)(2,1)S(1)}, bf16[144,256]{1,0:T(8,128)(2,1)S(1)}, u32[]{:S(2)}, u32[]{:S(2)}) %collective-permute-start.52) | collective-permute-done | bytes 73760 | tf_op jit(solution)/shard_map/ppermute | solution.py:118
  (140 shorter events, 59.3 us)
Async XLA Ops:
  5.1 11.0 %collective-permute-start.1 = (bf16[128,1024]{1,0:T(8,128)(2,1)}, bf16[128,1024]{1,0:T(8,128)(2,1)S(1)}, u32[]{:S(2)}, u32[]{:S(2)}) collective-permute-start(bf16[128,1024]{1,0:T(8,128)(2,1)} %get-tuple-element.157), channel_id=1, source_target_pairs={{0,1},{1,0},{2,3},{3,2},{4,5},{5,4},{6,7},{7,6},{8,9},{9,8},{10,11... | collective-permute-start | bytes 786440 | tf_op jit(solution)/shard_map/ppermute | solution.py:118
  8.1 7.9 %collective-permute-start = (bf16[32,1024]{1,0:T(8,128)(2,1)S(1)}, bf16[32,1024]{1,0:T(8,128)(2,1)S(1)}, u32[]{:S(2)}, u32[]{:S(2)}) collective-permute-start(bf16[32,1024]{1,0:T(8,128)(2,1)S(1)} %get-tuple-element.155), channel_id=1, source_target_pairs={{0,1},{1,0},{2,3},{3,2},{4,5},{5,4},{6,7},{7,6},{8,9},{9,8},{10,11... | collective-permute-start | bytes 196616 | tf_op jit(solution)/shard_map/ppermute | solution.py:118
  8.2 12.8 %collective-permute-start.2 = (bf16[64,1024]{1,0:T(8,128)(2,1)S(1)}, bf16[64,1024]{1,0:T(8,128)(2,1)S(1)}, u32[]{:S(2)}, u32[]{:S(2)}) collective-permute-start(bf16[64,1024]{1,0:T(8,128)(2,1)S(1)} %get-tuple-element.161), channel_id=1, source_target_pairs={{0,4},{1,5},{2,6},{3,7},{4,0},{5,1},{6,2},{7,3},{8,12},{9,13},{10,... | collective-permute-start | bytes 393224 | tf_op jit(solution)/shard_map/ppermute | solution.py:118
  11.2 9.8 %collective-permute-start.5 = (bf16[64,1024]{1,0:T(8,128)(2,1)S(1)}, bf16[64,1024]{1,0:T(8,128)(2,1)S(1)}, u32[]{:S(2)}, u32[]{:S(2)}) collective-permute-start(bf16[64,1024]{1,0:T(8,128)(2,1)S(1)} %get-tuple-element.162), channel_id=1, source_target_pairs={{0,2},{1,3},{2,0},{3,1},{4,6},{5,7},{6,4},{7,5},{8,10},{9,11},{10,... | collective-permute-start | bytes 393224 | tf_op jit(solution)/shard_map/ppermute | solution.py:118
  12.8 8.2 %collective-permute-start.6 = (bf16[64,1024]{1,0:T(8,128)(2,1)S(1)}, bf16[64,1024]{1,0:T(8,128)(2,1)S(1)}, u32[]{:S(2)}, u32[]{:S(2)}) collective-permute-start(bf16[64,1024]{1,0:T(8,128)(2,1)S(1)} %get-tuple-element.163), channel_id=1, source_target_pairs={{0,6},{1,7},{2,4},{3,5},{4,2},{5,3},{6,0},{7,1},{8,14},{9,15},{10,... | collective-permute-start | bytes 393224 | tf_op jit(solution)/shard_map/ppermute | solution.py:118
  25.4 11.6 %collective-permute-start.9 = (bf16[64,1024]{1,0:T(8,128)(2,1)S(1)}, bf16[64,1024]{1,0:T(8,128)(2,1)S(1)}, u32[]{:S(2)}, u32[]{:S(2)}) collective-permute-start(bf16[64,1024]{1,0:T(8,128)(2,1)S(1)} %get-tuple-element.171), channel_id=1, source_target_pairs={{0,4},{1,5},{2,6},{3,7},{4,0},{5,1},{6,2},{7,3},{8,12},{9,13},{10,... | collective-permute-start | bytes 393224 | tf_op jit(solution)/shard_map/ppermute | solution.py:118
  28.0 9.0 %collective-permute-start.10 = (bf16[64,1024]{1,0:T(8,128)(2,1)S(1)}, bf16[64,1024]{1,0:T(8,128)(2,1)S(1)}, u32[]{:S(2)}, u32[]{:S(2)}) collective-permute-start(bf16[64,1024]{1,0:T(8,128)(2,1)S(1)} %get-tuple-element.172), channel_id=1, source_target_pairs={{0,2},{1,3},{2,0},{3,1},{4,6},{5,7},{6,4},{7,5},{8,10},{9,11},{10,... | collective-permute-start | bytes 393224 | tf_op jit(solution)/shard_map/ppermute | solution.py:118
  29.5 7.4 %collective-permute-start.11 = (bf16[64,1024]{1,0:T(8,128)(2,1)S(1)}, bf16[64,1024]{1,0:T(8,128)(2,1)S(1)}, u32[]{:S(2)}, u32[]{:S(2)}) collective-permute-start(bf16[64,1024]{1,0:T(8,128)(2,1)S(1)} %get-tuple-element.173), channel_id=1, source_target_pairs={{0,6},{1,7},{2,4},{3,5},{4,2},{5,3},{6,0},{7,1},{8,14},{9,15},{10,... | collective-permute-start | bytes 393224 | tf_op jit(solution)/shard_map/ppermute | solution.py:118
  29.8 11.1 %collective-permute-start.13 = (bf16[192,1024]{1,0:T(8,128)(2,1)S(1)}, bf16[192,1024]{1,0:T(8,128)(2,1)S(1)}, u32[]{:S(2)}, u32[]{:S(2)}) collective-permute-start(bf16[192,1024]{1,0:T(8,128)(2,1)S(1)} %get-tuple-element.178), channel_id=1, source_target_pairs={{0,16},{8,24},{16,0},{24,8},{1,17},{9,25},{17,1},{25,9},{2,18},{10... | collective-permute-start | bytes 1179656 | tf_op jit(solution)/shard_map/ppermute | solution.py:118
  30.6 7.7 %collective-permute-start.8 = (bf16[256,1024]{1,0:T(8,128)(2,1)S(1)}, bf16[256,1024]{1,0:T(8,128)(2,1)S(1)}, u32[]{:S(2)}, u32[]{:S(2)}) collective-permute-start(bf16[256,1024]{1,0:T(8,128)(2,1)S(1)} %get-tuple-element.167.refs_0_), channel_id=1, source_target_pairs={{0,8},{8,0},{16,24},{24,16},{1,9},{9,1},{17,25},{25,17},{2,10},{10... | collective-permute-start | bytes 1572872 | tf_op jit(solution)/shard_map/ppermute | solution.py:118
  37.0 13.8 %collective-permute-start.23 = (bf16[256,1024]{1,0:T(8,128)(2,1)S(1)}, bf16[256,1024]{1,0:T(8,128)(2,1)S(1)}, u32[]{:S(2)}, u32[]{:S(2)}) collective-permute-start(bf16[256,1024]{1,0:T(8,128)(2,1)S(1)} %get-tuple-element.192.refs_0_), channel_id=1, source_target_pairs={{0,16},{8,24},{16,0},{24,8},{1,17},{9,25},{17,1},{25,9},{2,18},{10... | collective-permute-start | bytes 1572872 | tf_op jit(solution)/shard_map/ppermute | solution.py:118
  51.5 10.1 %collective-permute-start.12 = (bf16[256,1024]{1,0:T(8,128)(2,1)S(1)}, bf16[256,1024]{1,0:T(8,128)(2,1)S(1)}, u32[]{:S(2)}, u32[]{:S(2)}) collective-permute-start(bf16[256,1024]{1,0:T(8,128)(2,1)S(1)} %get-tuple-element.176), channel_id=1, source_target_pairs={{0,8},{8,0},{16,24},{24,16},{1,9},{9,1},{17,25},{25,17},{2,10},{10... | collective-permute-start | bytes 1572872 | tf_op jit(solution)/shard_map/ppermute | solution.py:118
  51.9 14.8 %collective-permute-start.22 = (bf16[256,1024]{1,0:T(8,128)(2,1)S(1)}, bf16[256,1024]{1,0:T(8,128)(2,1)S(1)}, u32[]{:S(2)}, u32[]{:S(2)}) collective-permute-start(bf16[256,1024]{1,0:T(8,128)(2,1)S(1)} %get-tuple-element.197), channel_id=1, source_target_pairs={{0,16},{8,24},{16,0},{24,8},{1,17},{9,25},{17,1},{25,9},{2,18},{10... | collective-permute-start | bytes 1572872 | tf_op jit(solution)/shard_map/ppermute | solution.py:118
  58.7 12.2 %collective-permute-start.31 = (bf16[256,1024]{1,0:T(8,128)(2,1)S(1)}, bf16[256,1024]{1,0:T(8,128)(2,1)S(1)}, u32[]{:S(2)}, u32[]{:S(2)}) collective-permute-start(bf16[256,1024]{1,0:T(8,128)(2,1)S(1)} %get-tuple-element.220), channel_id=1, source_target_pairs={{0,8},{8,0},{16,24},{24,16},{1,9},{9,1},{17,25},{25,17},{2,10},{10... | collective-permute-start | bytes 1572872 | tf_op jit(solution)/shard_map/ppermute | solution.py:118
  59.2 7.7 %collective-permute-start.32 = (bf16[128,1024]{1,0:T(8,128)(2,1)S(1)}, bf16[128,1024]{1,0:T(8,128)(2,1)S(1)}, u32[]{:S(2)}, u32[]{:S(2)}) collective-permute-start(bf16[128,1024]{1,0:T(8,128)(2,1)S(1)} %get-tuple-element.221), channel_id=1, source_target_pairs={{0,8},{8,0},{16,24},{24,16},{1,9},{9,1},{17,25},{25,17},{2,10},{10... | collective-permute-start | bytes 786440 | tf_op jit(solution)/shard_map/ppermute | solution.py:118
  60.2 12.0 %collective-permute-start.34 = (bf16[128,1024]{1,0:T(8,128)(2,1)S(1)}, bf16[128,1024]{1,0:T(8,128)(2,1)S(1)}, u32[]{:S(2)}, u32[]{:S(2)}) collective-permute-start(bf16[128,1024]{1,0:T(8,128)(2,1)S(1)} %get-tuple-element.232), channel_id=1, source_target_pairs={{0,16},{8,24},{16,0},{24,8},{1,17},{9,25},{17,1},{25,9},{2,18},{10... | collective-permute-start | bytes 786440 | tf_op jit(solution)/shard_map/ppermute | solution.py:118
  66.9 11.1 %collective-permute-start.33 = (bf16[128,1024]{1,0:T(8,128)(2,1)S(1)}, bf16[128,1024]{1,0:T(8,128)(2,1)S(1)}, u32[]{:S(2)}, u32[]{:S(2)}) collective-permute-start(bf16[128,1024]{1,0:T(8,128)(2,1)S(1)} %get-tuple-element.223), channel_id=1, source_target_pairs={{0,16},{8,24},{16,0},{24,8},{1,17},{9,25},{17,1},{25,9},{2,18},{10... | collective-permute-start | bytes 786440 | tf_op jit(solution)/shard_map/ppermute | solution.py:118
  67.8 10.8 %collective-permute-start.28 = (bf16[64,1024]{1,0:T(8,128)(2,1)S(1)}, bf16[64,1024]{1,0:T(8,128)(2,1)S(1)}, u32[]{:S(2)}, u32[]{:S(2)}) collective-permute-start(bf16[64,1024]{1,0:T(8,128)(2,1)S(1)} %get-tuple-element.216), channel_id=1, source_target_pairs={{0,4},{1,5},{2,6},{3,7},{4,0},{5,1},{6,2},{7,3},{8,12},{9,13},{10,... | collective-permute-start | bytes 393224 | tf_op jit(solution)/shard_map/ppermute | solution.py:118
  70.8 7.7 %collective-permute-start.29 = (bf16[64,1024]{1,0:T(8,128)(2,1)S(1)}, bf16[64,1024]{1,0:T(8,128)(2,1)S(1)}, u32[]{:S(2)}, u32[]{:S(2)}) collective-permute-start(bf16[64,1024]{1,0:T(8,128)(2,1)S(1)} %get-tuple-element.217), channel_id=1, source_target_pairs={{0,2},{1,3},{2,0},{3,1},{4,6},{5,7},{6,4},{7,5},{8,10},{9,11},{10,... | collective-permute-start | bytes 393224 | tf_op jit(solution)/shard_map/ppermute | solution.py:118
  70.9 9.2 %collective-permute-start.30 = (bf16[64,1024]{1,0:T(8,128)(2,1)S(1)}, bf16[64,1024]{1,0:T(8,128)(2,1)S(1)}, u32[]{:S(2)}, u32[]{:S(2)}) collective-permute-start(bf16[64,1024]{1,0:T(8,128)(2,1)S(1)} %get-tuple-element.218), channel_id=1, source_target_pairs={{0,6},{1,7},{2,4},{3,5},{4,2},{5,3},{6,0},{7,1},{8,14},{9,15},{10,... | collective-permute-start | bytes 393224 | tf_op jit(solution)/shard_map/ppermute | solution.py:118
  72.4 7.7 %collective-permute-start.36 = (bf16[64,1024]{1,0:T(8,128)(2,1)S(1)}, bf16[64,1024]{1,0:T(8,128)(2,1)S(1)}, u32[]{:S(2)}, u32[]{:S(2)}) collective-permute-start(bf16[64,1024]{1,0:T(8,128)(2,1)S(1)} %get-tuple-element.241), channel_id=1, source_target_pairs={{0,1},{1,0},{2,3},{3,2},{4,5},{5,4},{6,7},{7,6},{8,9},{9,8},{10,11... | collective-permute-start | bytes 393224 | tf_op jit(solution)/shard_map/ppermute | solution.py:118
  80.2 8.7 %collective-permute-start.39 = (bf16[64,1024]{1,0:T(8,128)(2,1)S(1)}, bf16[64,1024]{1,0:T(8,128)(2,1)S(1)}, u32[]{:S(2)}, u32[]{:S(2)}) collective-permute-start(bf16[64,1024]{1,0:T(8,128)(2,1)S(1)} %get-tuple-element.248), channel_id=1, source_target_pairs={{0,4},{1,5},{2,6},{3,7},{4,0},{5,1},{6,2},{7,3},{8,12},{9,13},{10,... | collective-permute-start | bytes 393224 | tf_op jit(solution)/shard_map/ppermute | solution.py:118
  98.0 8.6 %collective-permute-start.43 = (bf16[528,256]{1,0:T(8,128)(2,1)S(1)}, bf16[528,256]{1,0:T(8,128)(2,1)S(1)}, u32[]{:S(2)}, u32[]{:S(2)}) collective-permute-start(bf16[528,256]{1,0:T(8,128)(2,1)S(1)} %get-tuple-element.272), channel_id=1, source_target_pairs={{0,16},{8,24},{16,0},{24,8},{1,17},{9,25},{17,1},{25,9},{2,18},{10... | collective-permute-start | bytes 811016 | tf_op jit(solution)/shard_map/ppermute | solution.py:118
  99.6 8.8 %collective-permute-start.45 = (bf16[512,256]{1,0:T(8,128)(2,1)S(1)}, bf16[512,256]{1,0:T(8,128)(2,1)S(1)}, u32[]{:S(2)}, u32[]{:S(2)}) collective-permute-start(bf16[512,256]{1,0:T(8,128)(2,1)S(1)} %get-tuple-element.285), channel_id=1, source_target_pairs={{0,1},{1,0},{2,3},{3,2},{4,5},{5,4},{6,7},{7,6},{8,9},{9,8},{10,11... | collective-permute-start | bytes 786440 | tf_op jit(solution)/shard_map/ppermute | solution.py:118
  (39 other events, 238.5 us)

commit v6 on v5

--- a/solution.py
+++ b/solution.py
@@ -164,11 +164,14 @@
         lows, (placed_ref, resid_ref, inv_ref, normed_ref), sends = outs[:low], outs[low : low + 4], outs[low + 4 :]
         held, sems = copies[:5], copies[5]
         me = lax.axis_index("expert")
-        loads = [pltpu.make_async_copy(src, dst, sems.at[i]) for i, (src, dst) in enumerate(
-            zip((ids_hbm, ctx_hbm, w_out_hbm, tok_hbm, cot_hbm), held))]
+        ids_ref, ctx_ref, w_out_ref, tok_ref, cot_ref = held
+        quarter = width // 4
+        rows_of = [slice(i * quarter, (i + 1) * quarter) for i in range(4)]
+        pairs = [(ids_hbm, ids_ref), (ctx_hbm, ctx_ref)] + [(w_out_hbm.at[r, :], w_out_ref.at[r, :]) for r in rows_of]
+        pairs += [(tok_hbm, tok_ref), (cot_hbm, cot_ref)]
+        loads = [pltpu.make_async_copy(src, dst, sems.at[i]) for i, (src, dst) in enumerate(pairs)]
         for load in loads:
             load.start()
-        ids_ref, ctx_ref, w_out_ref, tok_ref, cot_ref = held
         loads[0].wait()
         rows = lax.broadcasted_iota(jnp.int32, (tok, tok), 0)
         cols = lax.broadcasted_iota(jnp.int32, (tok, tok), 1)
@@ -185,9 +188,12 @@
             placed_ref[k : k + 1, :] = places[k]
             spots.append((lower * len(masks) + block) * cap + rank[k].astype(jnp.int32))
         loads[1].wait()
-        loads[2].wait()
-        attn = mm(ctx_ref[...], w_out_ref[...])
-        loads[3].wait()
+        attn = None
+        for i, r in enumerate(rows_of):
+            loads[2 + i].wait()
+            term = mm(ctx_ref[:, r], w_out_ref[r, :])
+            attn = term if attn is None else attn + term
+        loads[6].wait()
         resid = (tok_ref[...].astype(F32) + attn).astype(BF)
         resid_ref[...] = resid
         resid_f = resid.astype(F32)
@@ -200,7 +206,7 @@
             sends[m][...] = moved[m * cap : (m + 1) * cap, :]
         for c in range(1, 4):
             sends[low + c - 1][...] = moved[c * size : (c + 1) * size, :]
-        loads[4].wait()
+        loads[7].wait()
         moved = mm(at_rows(spots, slots), cot_ref[...]).astype(BF)
         each = slots // low
         for m in range(low):
@@ -212,7 +218,7 @@
         + [shape((tok, width)), shape((tok, 1), F32), shape((tok, width))] + [shape((cap, width))] * low + [shape((size, width))] * 3,
         (ids_t, cotangent, tokens, context, w_out), specs=[HBM] * 5,
         scratch=[pltpu.VMEM((2, tok), jnp.int32), pltpu.VMEM((tok, width), BF), pltpu.VMEM((width, width), BF),
-                 pltpu.VMEM((tok, width), BF), pltpu.VMEM((tok, width), BF), DMA((5,))],
+                 pltpu.VMEM((tok, width), BF), pltpu.VMEM((tok, width), BF), DMA((8,))],
         vmem=53 * MIB, name="head")
     cot_low, (placed, resid, inv, normed), sends = outs[:low], outs[low : low + 4], outs[low + 4 :]
     cot_low = [cot_low[0]] + [swap(cot_low[m], "expert", m) for m in range(1, low)]
@@ -381,6 +387,18 @@
                      DMA((len(lefts) + len(rights) + left // tile,))],
             vmem=20 * MIB, name="weights")[0]
 
+    tile = max(per, LANES)
+
+    def turn_body(ctx_ref, out_ref):
+        for i in range(width // tile):
+            turned = ctx_ref[:, i * tile : (i + 1) * tile].astype(F32).T.astype(BF)
+            for j in range(tile // per):
+                spot, lower = order((i * (tile // per) + j) ^ lax.axis_index("expert"))
+                at = pl.ds(pl.multiple_of((spot * low + lower) * per, TILE), per)
+                out_ref[at, :] = turned[j * per : (j + 1) * per, :]
+
+    context_t = line.call(turn_body, [shape((width, tok))], (context,), name="turn")[0]
+
     quarter = slots // 4
     sums = line.move(
         *[[(quarter, [(x, c * quarter) for x in (keep_n, near_out, far_out)])] for c in range(4)], name="sum_x_out")
@@ -406,10 +424,10 @@
     if low > 1:
         out_low = line.move(*[[(cap, [(x, m * cap)]) for x in out_high] for m in range(1, low)], name="pack_out_y")
     back_in = send_back(0, *total_a)
-    back_in += send_back(1, *total_b)
     if low > 1:
         out_low = line.move(*[[(2 * cap, [(x, i * 2 * cap)])] for x in out_low for i in range(2)], name="pass_out_y")
         out_low = [swap(x, "expert", i // 2 + 1) for i, x in enumerate(out_low)]
+    back_in += send_back(1, *total_b)
     back_a = line.move([(x.shape[0], [(x, 0)]) for x in back_in[:2]], name="pack_back")[0]
     back_out = line.move(
         [(cap, [piece]) for c in range(4) for piece in [(out_high[c], 0)] + [(out_low[2 * m + c // 2], c % 2 * cap) for m in range(low - 1)]],
@@ -444,49 +462,36 @@
         (*back_out, placed, ids_t, router_t, resid, cotangent, normed),
         name="combine")
 
-    tile = max(per, LANES)
-
     def products(odd, ctx_ref, grad_ref, local_ref, turned, out):
-        me, mine = lax.axis_index("expert"), lax.axis_index("dp")
+        mine = lax.axis_index("dp")
         for d in range(far):
             at = pl.ds(pl.multiple_of((mine ^ (2 * d + odd)) * part, LANES), part)
             turned[:, d * part : (d + 1) * part] = grad_ref[:, at]
             out[d * span + width : (d + 1) * span, :] = local_ref[:, at]
-        for i in range(width // tile):
-            block = mm(ctx_ref[:, i * tile : (i + 1) * tile], turned[...], TN).astype(BF)
-            for j in range(tile // per):
-                spot, lower = order((i * (tile // per) + j) ^ me)
-                to = (spot * low + lower) * per
-                for d in range(far):
-                    out[pl.ds(pl.multiple_of(d * span + to, TILE), per), :] = (
-                        block[j * per : (j + 1) * per, d * part : (d + 1) * part])
+        for i in range(0, width, part):
+            block = mm(ctx_ref[i : i + part, :], turned[...]).astype(BF)
+            for d in range(far):
+                out[d * span + i : d * span + i + part, :] = block[:, d * part : (d + 1) * part]
 
     def tail_body(*refs):
         backs = refs[:3]
-        (placed_ref, table_ref, router_ref, resid_ref, inv_ref, local_ref, cot_hbm, ctx_hbm,
-         grad_out, grad_ref, ctx_ref, send_ref, cot_ref, turned, sems) = refs[3:]
-        loads = [pltpu.make_async_copy(src, dst, sems.at[i]) for i, (src, dst) in enumerate(
-            ((cot_hbm, cot_ref), (ctx_hbm, ctx_ref)))]
-        for load in loads:
-            load.start()
+        (placed_ref, table_ref, router_ref, resid_ref, inv_ref, local_ref, cot_ref, ctx_ref,
+         grad_out, grad_ref, send_ref, turned) = refs[3:]
         held = jnp.concatenate([b[...] for b in backs], axis=0)
         where = at_rows([placed_ref[k : k + 1, :] for k in range(2)], slots)
         normed_grad = mm(where, held, TN) + mm(table_ref[:, :experts], router_ref[...])
         resid_f = resid_ref[...].astype(F32)
         inv_col = inv_ref[...]
         mean_term = jnp.mean(normed_grad * resid_f, axis=1, keepdims=True)
-        loads[0].wait()
         grad_ref[...] = (cot_ref[...].astype(F32) + inv_col * normed_grad
                          - (inv_col * inv_col * inv_col * mean_term) * resid_f).astype(BF)
-        loads[1].wait()
         grad_out[...] = grad_ref[...]
         products(1, ctx_ref, grad_ref, local_ref, turned, send_ref)
 
-    grad_tokens, grad_near, ctx_near, send = line.call(
-        tail_body, [shape((tok, width))] * 3 + [ shape((far * span, part))],
-        (back_a, *back_in[2:], placed, table, router_t, resid, inv, local_router, cotangent, context),
-        specs=[VMEM] * 9 + [HBM] * 2,
-        scratch=[pltpu.VMEM((tok, width), BF), pltpu.VMEM((tok, far * part), BF), DMA((2,))],
+    grad_tokens, grad_near, send = line.call(
+        tail_body, [shape((tok, width))] * 2 + [ shape((far * span, part))],
+        (back_a, *back_in[2:], placed, table, router_t, resid, inv, local_router, cotangent, context_t),
+        scratch=[pltpu.VMEM((tok, far * part), BF)],
         vmem=16 * MIB, name="tail")
     core = swap(send, "dp", 1)
 
@@ -495,7 +500,7 @@
         grad_ctx_ref[...] = mm(grad_ref[...], w_out_ref[...], NT).astype(BF)
 
     grad_context, keep = line.call(
-        keep_body, [shape((tok, width)), shape((far * span, part))], (ctx_near, grad_near, local_router, w_out),
+        keep_body, [shape((tok, width)), shape((far * span, part))], (context_t, grad_near, local_router, w_out),
         scratch=[pltpu.VMEM((tok, far * part), BF)], vmem=16 * MIB, name="keep")
 
     spot = lambda d, c, m: d * span + (c * low + m) * per

time: 129 us -> 128 us (level)
    pallas_call x38 -> x39, Pallas kernels: 36.6 us -> 35.9 us  [call(): pl.pallas_call(kernel, out_shape=[*outs, shape((8, LANES), F32)], in_spec...]
  transfers between devices with their start and end apart: 53 -> 53, of which waited for: 21 -> 20; matrix products, arithmetic and copies ran while one was open for 0% -> 0% of each run, Pallas kernels for 23% -> 24%
where the time goes in v6:
time: 128 us
  starting transfers between devices  51 us (40%)
  waiting for transfers between devices  37.4 us (29%)
  Pallas kernels  35.9 us (28%)
  local copies, waits for them, and re-layouts  2.45 us (2%)
    ppermute x53, starting transfers between devices, swap(): lax.ppermute(x, axis, [(i, i ^ mask) for i in range(lax.axis_size(axis))])  51 us
    ppermute x53, waiting for transfers between devices, swap(): lax.ppermute(x, axis, [(i, i ^ mask) for i in range(lax.axis_size(axis))])  37.4 us
    pallas_call x39, Pallas kernels, call(): pl.pallas_call(kernel, out_shape=[*outs, shape((8, LANES), F32)], in_spec...  35.9 us
  transfers between devices with their start and end apart: 53, of which 20 were waited for; matrix products, arithmetic and copies ran while one was open for 0% of the time, Pallas kernels for 24%

profile of v6, /device:TPU:0, one launch (start us, length us, event | category | flops | bytes accessed | tf_op | source)
XLA Modules:
  0.0 127.9 jit_solution(4890648807068475021)
XLA Ops:
  1.5 3.4 %head.1 = (bf16[128,1024]{1,0:T(8,128)(2,1)S(1)}, bf16[128,1024]{1,0:T(8,128)(2,1)}, s32[2,128]{1,0:T(2,128)S(1)}, bf16[128,1024]{1,0:T(8,128)(2,1)}, f32[128,1]...) custom-call(s32[2,128]{1,0:T(2,128)S(1)} %bitcast.31, ...), custom_call_target="tpu_custom_call" | custom-call | tf_op jit(solution)/shard_map/head/pallas_call | solution.py:66
  4.8 3.0 %collective-permute-start.1 = (bf16[128,1024]{1,0:T(8,128)(2,1)}, bf16[128,1024]{1,0:T(8,128)(2,1)S(1)}, u32[]{:S(2)}, u32[]{:S(2)}) collective-permute-start(bf16[128,1024]{1,0:T(8,128)(2,1)} %get-tuple-element.158), channel_id=1, source_target_pairs={{0,1},{1,0},{2,3},{3,2},{4,5},{5,4},{6,7},{7,6},{8,9},{9,8},{10,11... | collective-permute-start | bytes 786440 | tf_op jit(solution)/shard_map/ppermute | solution.py:118
  7.9 3.0 %collective-permute-start.2 = (bf16[64,1024]{1,0:T(8,128)(2,1)S(1)}, bf16[64,1024]{1,0:T(8,128)(2,1)S(1)}, u32[]{:S(2)}, u32[]{:S(2)}) collective-permute-start(bf16[64,1024]{1,0:T(8,128)(2,1)S(1)} %get-tuple-element.162), channel_id=1, source_target_pairs={{0,4},{1,5},{2,6},{3,7},{4,0},{5,1},{6,2},{7,3},{8,12},{9,13},{10,... | collective-permute-start | bytes 393224 | tf_op jit(solution)/shard_map/ppermute | solution.py:118
  12.5 3.3 %collective-permute-done.refs_1_ = bf16[32,1024]{1,0:T(8,128)(2,1)S(1)} collective-permute-done((bf16[32,1024]{1,0:T(8,128)(2,1)S(1)}, bf16[32,1024]{1,0:T(8,128)(2,1)S(1)}, u32[]{:S(2)}, u32[]{:S(2)}) %collective-permute-start) | collective-permute-done | bytes 65568 | tf_op jit(solution)/shard_map/ppermute | solution.py:118
  25.1 2.6 %collective-permute-start.9 = (bf16[64,1024]{1,0:T(8,128)(2,1)S(1)}, bf16[64,1024]{1,0:T(8,128)(2,1)S(1)}, u32[]{:S(2)}, u32[]{:S(2)}) collective-permute-start(bf16[64,1024]{1,0:T(8,128)(2,1)S(1)} %get-tuple-element.172), channel_id=1, source_target_pairs={{0,4},{1,5},{2,6},{3,7},{4,0},{5,1},{6,2},{7,3},{8,12},{9,13},{10,... | collective-permute-start | bytes 393224 | tf_op jit(solution)/shard_map/ppermute | solution.py:118
  30.3 2.5 %forward.4 = (bf16[256,1024]{1,0:T(8,128)(2,1)S(1)}, bf16[256,1024]{1,0:T(8,128)(2,1)S(1)}, bf16[256,1024]{1,0:T(8,128)(2,1)S(1)}, f32[256,1]{1,0:T(8,128)S(1)},...) custom-call(bf16[256,1024]{1,0:T(8,128)(2,1)S(1)} %get-tuple-element.168.refs_0_, bf16[8,1024]{1,0:T(8,128)(2,1)S(1)} %bitcast.25, ...), custom_call_target="tpu_custom_call" | custom-call | tf_op jit(solution)/shard_map/forward/pallas_call | solution.py:66
  32.9 3.8 %collective-permute-done.9.refs_1_ = bf16[64,1024]{1,0:T(8,128)(2,1)S(1)} collective-permute-done((bf16[64,1024]{1,0:T(8,128)(2,1)S(1)}, bf16[64,1024]{1,0:T(8,128)(2,1)S(1)}, u32[]{:S(2)}, u32[]{:S(2)}) %collective-permute-start.9) | collective-permute-done | bytes 131104 | tf_op jit(solution)/shard_map/ppermute | solution.py:118
  38.1 2.5 %forward.5 = (bf16[256,1024]{1,0:T(8,128)(2,1)S(1)}, bf16[256,1024]{1,0:T(8,128)(2,1)S(1)}, bf16[256,1024]{1,0:T(8,128)(2,1)S(1)}, f32[256,1]{1,0:T(8,128)S(1)},...) custom-call(bf16[256,1024]{1,0:T(8,128)(2,1)S(1)} %collective-permute-done.8.refs_0_, bf16[8,1024]{1,0:T(8,128)(2,1)S(1)} %bitcast.26, ...), custom_call_target="tpu_custom_call" | custom-call | tf_op jit(solution)/shard_map/forward/pallas_call | solution.py:66
  41.8 2.5 %forward.6 = (bf16[256,1024]{1,0:T(8,128)(2,1)S(1)}, bf16[256,1024]{1,0:T(8,128)(2,1)S(1)}, bf16[256,1024]{1,0:T(8,128)(2,1)S(1)}, f32[256,1]{1,0:T(8,128)S(1)},...) custom-call(bf16[256,1024]{1,0:T(8,128)(2,1)S(1)} %get-tuple-element.181.refs_0_, bf16[8,1024]{1,0:T(8,128)(2,1)S(1)} %bitcast.27, ...), custom_call_target="tpu_custom_call" | custom-call | tf_op jit(solution)/shard_map/forward/pallas_call | solution.py:66
  44.4 2.5 %forward.7 = (bf16[256,1024]{1,0:T(8,128)(2,1)S(1)}, bf16[256,1024]{1,0:T(8,128)(2,1)S(1)}, bf16[256,1024]{1,0:T(8,128)(2,1)S(1)}, f32[256,1]{1,0:T(8,128)S(1)},...) custom-call(bf16[64,1024]{1,0:T(8,128)(2,1)S(1)} %collective-permute, ...), custom_call_target="tpu_custom_call" | custom-call | tf_op jit(solution)/shard_map/forward/pallas_call | solution.py:66
  52.4 2.1 %backward.5 = (bf16[256,1024]{1,0:T(8,128)(2,1)S(1)}, bf16[256,1024]{1,0:T(8,128)(2,1)S(1)}, bf16[256,1024]{1,0:T(8,128)(2,1)S(1)}, f32[8,128]{1,0:T(8,128)S(1)}) custom-call(bf16[256,1024]{1,0:T(8,128)(2,1)S(1)} %collective-permute-done.24.refs_0_, f32[256,1]{1,0:T(8,128)S(1)} %get-tuple-element.203.refs_1_, ...), custom_call_target="tpu_custom_call" | custom-call | tf_op jit(solution)/shard_map/backward/pallas_call | solution.py:66
  61.4 4.9 %collective-permute-done.22.refs_2_ = bf16[256,1024]{1,0:T(8,128)(2,1)S(1)} collective-permute-done((bf16[256,1024]{1,0:T(8,128)(2,1)S(1)}, bf16[256,1024]{1,0:T(8,128)(2,1)S(1)}, u32[]{:S(2)}, u32[]{:S(2)}) %collective-permute-start.22) | collective-permute-done | bytes 524320 | tf_op jit(solution)/shard_map/ppermute | solution.py:118
  67.5 3.1 %collective-permute-start.28 = (bf16[64,1024]{1,0:T(8,128)(2,1)S(1)}, bf16[64,1024]{1,0:T(8,128)(2,1)S(1)}, u32[]{:S(2)}, u32[]{:S(2)}) collective-permute-start(bf16[64,1024]{1,0:T(8,128)(2,1)S(1)} %get-tuple-element.218), channel_id=1, source_target_pairs={{0,4},{1,5},{2,6},{3,7},{4,0},{5,1},{6,2},{7,3},{8,12},{9,13},{10,... | collective-permute-start | bytes 393224 | tf_op jit(solution)/shard_map/ppermute | solution.py:118
  72.1 2.0 %collective-permute-start.35 = (bf16[64,1024]{1,0:T(8,128)(2,1)S(1)}, bf16[64,1024]{1,0:T(8,128)(2,1)S(1)}, u32[]{:S(2)}, u32[]{:S(2)}) collective-permute-start(bf16[64,1024]{1,0:T(8,128)(2,1)S(1)} %get-tuple-element.241), channel_id=1, source_target_pairs={{0,1},{1,0},{2,3},{3,2},{4,5},{5,4},{6,7},{7,6},{8,9},{9,8},{10,11... | collective-permute-start | bytes 393224 | tf_op jit(solution)/shard_map/ppermute | solution.py:118
  74.1 3.6 %weights.2 = (bf16[1024,1024]{1,0:T(8,128)(2,1)}, f32[8,128]{1,0:T(8,128)S(1)}) custom-call(bf16[256,1024]{1,0:T(8,128)(2,1)S(1)} %get-tuple-element.226.refs_0_, bf16[256,1024]{1,0:T(8,128)(2,1)S(1)} %get-tuple-element.227.refs_1_, bf16[256,1024]{1,0:T(8,128)(2,1)S(1)} %get-tuple-element.228.refs_2_, bf16[256,1024]{1,0:T(8,128)(2,1)S(1)} %get-tuple-element.229.refs_3_, ...), custom_call_target="tpu_custom_call" | custom-call | tf_op jit(solution)/shard_map/weights/pallas_call | solution.py:66
  79.9 2.7 %collective-permute-start.38 = (bf16[64,1024]{1,0:T(8,128)(2,1)S(1)}, bf16[64,1024]{1,0:T(8,128)(2,1)S(1)}, u32[]{:S(2)}, u32[]{:S(2)}) collective-permute-start(bf16[64,1024]{1,0:T(8,128)(2,1)S(1)} %get-tuple-element.247), channel_id=1, source_target_pairs={{0,4},{1,5},{2,6},{3,7},{4,0},{5,1},{6,2},{7,3},{8,12},{9,13},{10,... | collective-permute-start | bytes 393224 | tf_op jit(solution)/shard_map/ppermute | solution.py:118
  85.0 2.9 %collective-permute-start.41 = (bf16[64,1024]{1,0:T(8,128)(2,1)S(1)}, bf16[64,1024]{1,0:T(8,128)(2,1)S(1)}, u32[]{:S(2)}, u32[]{:S(2)}) collective-permute-start(bf16[64,1024]{1,0:T(8,128)(2,1)S(1)} %get-tuple-element.261), channel_id=1, source_target_pairs={{0,6},{1,7},{2,4},{3,5},{4,2},{5,3},{6,0},{7,1},{8,14},{9,15},{10,... | collective-permute-start | bytes 393224 | tf_op jit(solution)/shard_map/ppermute | solution.py:118
  99.3 3.8 %weights.3 = (bf16[1024,1024]{1,0:T(8,128)(2,1)}, f32[8,128]{1,0:T(8,128)S(1)}) custom-call(bf16[256,1024]{1,0:T(8,128)(2,1)S(1)} %get-tuple-element.275.refs_0_, bf16[256,1024]{1,0:T(8,128)(2,1)S(1)} %get-tuple-element.276.refs_1_, bf16[256,1024]{1,0:T(8,128)(2,1)S(1)} %get-tuple-element.277.refs_2_, bf16[256,1024]{1,0:T(8,128)(2,1)S(1)} %get-tuple-element.278.refs_3_, ...), custom_call_target="tpu_custom_call" | custom-call | tf_op jit(solution)/shard_map/weights/pallas_call | solution.py:66
  103.1 2.2 %collective-permute-done.43.refs_2_ = bf16[528,256]{1,0:T(8,128)(2,1)S(1)} collective-permute-done((bf16[528,256]{1,0:T(8,128)(2,1)S(1)}, bf16[528,256]{1,0:T(8,128)(2,1)S(1)}, u32[]{:S(2)}, u32[]{:S(2)}) %collective-permute-start.43) | collective-permute-done | bytes 270368 | tf_op jit(solution)/shard_map/ppermute | solution.py:118
  108.2 4.0 %collective-permute-done.46.refs_3_ = bf16[256,256]{1,0:T(8,128)(2,1)S(1)} collective-permute-done((bf16[256,256]{1,0:T(8,128)(2,1)S(1)}, bf16[256,256]{1,0:T(8,128)(2,1)S(1)}, u32[]{:S(2)}, u32[]{:S(2)}) %collective-permute-start.46) | collective-permute-done | bytes 131104 | tf_op jit(solution)/shard_map/ppermute | solution.py:118
  112.3 1.9 %collective-permute-start.47 = (bf16[144,256]{1,0:T(8,128)(2,1)S(1)}, bf16[144,256]{1,0:T(8,128)(2,1)S(1)}, u32[]{:S(2)}, u32[]{:S(2)}) collective-permute-start(bf16[144,256]{1,0:T(8,128)(2,1)S(1)} %get-tuple-element.293), channel_id=1, source_target_pairs={{0,4},{1,5},{2,6},{3,7},{4,0},{5,1},{6,2},{7,3},{8,12},{9,13},{10,... | collective-permute-start | bytes 221192 | tf_op jit(solution)/shard_map/ppermute | solution.py:118
  114.5 2.2 %collective-permute-start.49 = (bf16[144,256]{1,0:T(8,128)(2,1)S(1)}, bf16[144,256]{1,0:T(8,128)(2,1)S(1)}, u32[]{:S(2)}, u32[]{:S(2)}) collective-permute-start(bf16[144,256]{1,0:T(8,128)(2,1)S(1)} %get-tuple-element.295), channel_id=1, source_target_pairs={{0,6},{1,7},{2,4},{3,5},{4,2},{5,3},{6,0},{7,1},{8,14},{9,15},{10,... | collective-permute-start | bytes 221192 | tf_op jit(solution)/shard_map/ppermute | solution.py:118
  116.7 2.3 %collective-permute-done.47.refs_1_ = bf16[144,256]{1,0:T(8,128)(2,1)S(1)} collective-permute-done((bf16[144,256]{1,0:T(8,128)(2,1)S(1)}, bf16[144,256]{1,0:T(8,128)(2,1)S(1)}, u32[]{:S(2)}, u32[]{:S(2)}) %collective-permute-start.47) | collective-permute-done | bytes 73760 | tf_op jit(solution)/shard_map/ppermute | solution.py:118
  122.8 2.5 %collective-permute-done.52.refs_3_ = bf16[144,256]{1,0:T(8,128)(2,1)S(1)} collective-permute-done((bf16[144,256]{1,0:T(8,128)(2,1)S(1)}, bf16[144,256]{1,0:T(8,128)(2,1)S(1)}, u32[]{:S(2)}, u32[]{:S(2)}) %collective-permute-start.52) | collective-permute-done | bytes 73760 | tf_op jit(solution)/shard_map/ppermute | solution.py:118
  (141 shorter events, 57.5 us)
Async XLA Ops:
  4.8 11.0 %collective-permute-start.1 = (bf16[128,1024]{1,0:T(8,128)(2,1)}, bf16[128,1024]{1,0:T(8,128)(2,1)S(1)}, u32[]{:S(2)}, u32[]{:S(2)}) collective-permute-start(bf16[128,1024]{1,0:T(8,128)(2,1)} %get-tuple-element.158), channel_id=1, source_target_pairs={{0,1},{1,0},{2,3},{3,2},{4,5},{5,4},{6,7},{7,6},{8,9},{9,8},{10,11... | collective-permute-start | bytes 786440 | tf_op jit(solution)/shard_map/ppermute | solution.py:118
  7.9 7.9 %collective-permute-start = (bf16[32,1024]{1,0:T(8,128)(2,1)S(1)}, bf16[32,1024]{1,0:T(8,128)(2,1)S(1)}, u32[]{:S(2)}, u32[]{:S(2)}) collective-permute-start(bf16[32,1024]{1,0:T(8,128)(2,1)S(1)} %get-tuple-element.156), channel_id=1, source_target_pairs={{0,1},{1,0},{2,3},{3,2},{4,5},{5,4},{6,7},{7,6},{8,9},{9,8},{10,11... | collective-permute-start | bytes 196616 | tf_op jit(solution)/shard_map/ppermute | solution.py:118
  7.9 12.8 %collective-permute-start.2 = (bf16[64,1024]{1,0:T(8,128)(2,1)S(1)}, bf16[64,1024]{1,0:T(8,128)(2,1)S(1)}, u32[]{:S(2)}, u32[]{:S(2)}) collective-permute-start(bf16[64,1024]{1,0:T(8,128)(2,1)S(1)} %get-tuple-element.162), channel_id=1, source_target_pairs={{0,4},{1,5},{2,6},{3,7},{4,0},{5,1},{6,2},{7,3},{8,12},{9,13},{10,... | collective-permute-start | bytes 393224 | tf_op jit(solution)/shard_map/ppermute | solution.py:118
  11.0 9.8 %collective-permute-start.5 = (bf16[64,1024]{1,0:T(8,128)(2,1)S(1)}, bf16[64,1024]{1,0:T(8,128)(2,1)S(1)}, u32[]{:S(2)}, u32[]{:S(2)}) collective-permute-start(bf16[64,1024]{1,0:T(8,128)(2,1)S(1)} %get-tuple-element.163), channel_id=1, source_target_pairs={{0,2},{1,3},{2,0},{3,1},{4,6},{5,7},{6,4},{7,5},{8,10},{9,11},{10,... | collective-permute-start | bytes 393224 | tf_op jit(solution)/shard_map/ppermute | solution.py:118
  12.5 8.2 %collective-permute-start.6 = (bf16[64,1024]{1,0:T(8,128)(2,1)S(1)}, bf16[64,1024]{1,0:T(8,128)(2,1)S(1)}, u32[]{:S(2)}, u32[]{:S(2)}) collective-permute-start(bf16[64,1024]{1,0:T(8,128)(2,1)S(1)} %get-tuple-element.164), channel_id=1, source_target_pairs={{0,6},{1,7},{2,4},{3,5},{4,2},{5,3},{6,0},{7,1},{8,14},{9,15},{10,... | collective-permute-start | bytes 393224 | tf_op jit(solution)/shard_map/ppermute | solution.py:118
  25.1 11.6 %collective-permute-start.9 = (bf16[64,1024]{1,0:T(8,128)(2,1)S(1)}, bf16[64,1024]{1,0:T(8,128)(2,1)S(1)}, u32[]{:S(2)}, u32[]{:S(2)}) collective-permute-start(bf16[64,1024]{1,0:T(8,128)(2,1)S(1)} %get-tuple-element.172), channel_id=1, source_target_pairs={{0,4},{1,5},{2,6},{3,7},{4,0},{5,1},{6,2},{7,3},{8,12},{9,13},{10,... | collective-permute-start | bytes 393224 | tf_op jit(solution)/shard_map/ppermute | solution.py:118
  27.7 9.0 %collective-permute-start.10 = (bf16[64,1024]{1,0:T(8,128)(2,1)S(1)}, bf16[64,1024]{1,0:T(8,128)(2,1)S(1)}, u32[]{:S(2)}, u32[]{:S(2)}) collective-permute-start(bf16[64,1024]{1,0:T(8,128)(2,1)S(1)} %get-tuple-element.173), channel_id=1, source_target_pairs={{0,2},{1,3},{2,0},{3,1},{4,6},{5,7},{6,4},{7,5},{8,10},{9,11},{10,... | collective-permute-start | bytes 393224 | tf_op jit(solution)/shard_map/ppermute | solution.py:118
  29.5 11.1 %collective-permute-start.13 = (bf16[192,1024]{1,0:T(8,128)(2,1)S(1)}, bf16[192,1024]{1,0:T(8,128)(2,1)S(1)}, u32[]{:S(2)}, u32[]{:S(2)}) collective-permute-start(bf16[192,1024]{1,0:T(8,128)(2,1)S(1)} %get-tuple-element.179), channel_id=1, source_target_pairs={{0,16},{8,24},{16,0},{24,8},{1,17},{9,25},{17,1},{25,9},{2,18},{10... | collective-permute-start | bytes 1179656 | tf_op jit(solution)/shard_map/ppermute | solution.py:118
  30.3 7.7 %collective-permute-start.8 = (bf16[256,1024]{1,0:T(8,128)(2,1)S(1)}, bf16[256,1024]{1,0:T(8,128)(2,1)S(1)}, u32[]{:S(2)}, u32[]{:S(2)}) collective-permute-start(bf16[256,1024]{1,0:T(8,128)(2,1)S(1)} %get-tuple-element.168.refs_0_), channel_id=1, source_target_pairs={{0,8},{8,0},{16,24},{24,16},{1,9},{9,1},{17,25},{25,17},{2,10},{10... | collective-permute-start | bytes 1572872 | tf_op jit(solution)/shard_map/ppermute | solution.py:118
  36.7 13.8 %collective-permute-start.23 = (bf16[256,1024]{1,0:T(8,128)(2,1)S(1)}, bf16[256,1024]{1,0:T(8,128)(2,1)S(1)}, u32[]{:S(2)}, u32[]{:S(2)}) collective-permute-start(bf16[256,1024]{1,0:T(8,128)(2,1)S(1)} %get-tuple-element.193.refs_0_), channel_id=1, source_target_pairs={{0,16},{8,24},{16,0},{24,8},{1,17},{9,25},{17,1},{25,9},{2,18},{10... | collective-permute-start | bytes 1572872 | tf_op jit(solution)/shard_map/ppermute | solution.py:118
  51.2 10.2 %collective-permute-start.12 = (bf16[256,1024]{1,0:T(8,128)(2,1)S(1)}, bf16[256,1024]{1,0:T(8,128)(2,1)S(1)}, u32[]{:S(2)}, u32[]{:S(2)}) collective-permute-start(bf16[256,1024]{1,0:T(8,128)(2,1)S(1)} %get-tuple-element.177), channel_id=1, source_target_pairs={{0,8},{8,0},{16,24},{24,16},{1,9},{9,1},{17,25},{25,17},{2,10},{10... | collective-permute-start | bytes 1572872 | tf_op jit(solution)/shard_map/ppermute | solution.py:118
  51.6 14.8 %collective-permute-start.22 = (bf16[256,1024]{1,0:T(8,128)(2,1)S(1)}, bf16[256,1024]{1,0:T(8,128)(2,1)S(1)}, u32[]{:S(2)}, u32[]{:S(2)}) collective-permute-start(bf16[256,1024]{1,0:T(8,128)(2,1)S(1)} %get-tuple-element.198), channel_id=1, source_target_pairs={{0,16},{8,24},{16,0},{24,8},{1,17},{9,25},{17,1},{25,9},{2,18},{10... | collective-permute-start | bytes 1572872 | tf_op jit(solution)/shard_map/ppermute | solution.py:118
  58.4 12.2 %collective-permute-start.31 = (bf16[256,1024]{1,0:T(8,128)(2,1)S(1)}, bf16[256,1024]{1,0:T(8,128)(2,1)S(1)}, u32[]{:S(2)}, u32[]{:S(2)}) collective-permute-start(bf16[256,1024]{1,0:T(8,128)(2,1)S(1)} %get-tuple-element.222), channel_id=1, source_target_pairs={{0,8},{8,0},{16,24},{24,16},{1,9},{9,1},{17,25},{25,17},{2,10},{10... | collective-permute-start | bytes 1572872 | tf_op jit(solution)/shard_map/ppermute | solution.py:118
  58.9 7.7 %collective-permute-start.32 = (bf16[128,1024]{1,0:T(8,128)(2,1)S(1)}, bf16[128,1024]{1,0:T(8,128)(2,1)S(1)}, u32[]{:S(2)}, u32[]{:S(2)}) collective-permute-start(bf16[128,1024]{1,0:T(8,128)(2,1)S(1)} %get-tuple-element.223), channel_id=1, source_target_pairs={{0,8},{8,0},{16,24},{24,16},{1,9},{9,1},{17,25},{25,17},{2,10},{10... | collective-permute-start | bytes 786440 | tf_op jit(solution)/shard_map/ppermute | solution.py:118
  60.0 12.1 %collective-permute-start.34 = (bf16[128,1024]{1,0:T(8,128)(2,1)S(1)}, bf16[128,1024]{1,0:T(8,128)(2,1)S(1)}, u32[]{:S(2)}, u32[]{:S(2)}) collective-permute-start(bf16[128,1024]{1,0:T(8,128)(2,1)S(1)} %get-tuple-element.234), channel_id=1, source_target_pairs={{0,16},{8,24},{16,0},{24,8},{1,17},{9,25},{17,1},{25,9},{2,18},{10... | collective-permute-start | bytes 786440 | tf_op jit(solution)/shard_map/ppermute | solution.py:118
  66.6 11.1 %collective-permute-start.33 = (bf16[128,1024]{1,0:T(8,128)(2,1)S(1)}, bf16[128,1024]{1,0:T(8,128)(2,1)S(1)}, u32[]{:S(2)}, u32[]{:S(2)}) collective-permute-start(bf16[128,1024]{1,0:T(8,128)(2,1)S(1)} %get-tuple-element.225), channel_id=1, source_target_pairs={{0,16},{8,24},{16,0},{24,8},{1,17},{9,25},{17,1},{25,9},{2,18},{10... | collective-permute-start | bytes 786440 | tf_op jit(solution)/shard_map/ppermute | solution.py:118
  67.5 10.8 %collective-permute-start.28 = (bf16[64,1024]{1,0:T(8,128)(2,1)S(1)}, bf16[64,1024]{1,0:T(8,128)(2,1)S(1)}, u32[]{:S(2)}, u32[]{:S(2)}) collective-permute-start(bf16[64,1024]{1,0:T(8,128)(2,1)S(1)} %get-tuple-element.218), channel_id=1, source_target_pairs={{0,4},{1,5},{2,6},{3,7},{4,0},{5,1},{6,2},{7,3},{8,12},{9,13},{10,... | collective-permute-start | bytes 393224 | tf_op jit(solution)/shard_map/ppermute | solution.py:118
  70.5 7.7 %collective-permute-start.29 = (bf16[64,1024]{1,0:T(8,128)(2,1)S(1)}, bf16[64,1024]{1,0:T(8,128)(2,1)S(1)}, u32[]{:S(2)}, u32[]{:S(2)}) collective-permute-start(bf16[64,1024]{1,0:T(8,128)(2,1)S(1)} %get-tuple-element.219), channel_id=1, source_target_pairs={{0,2},{1,3},{2,0},{3,1},{4,6},{5,7},{6,4},{7,5},{8,10},{9,11},{10,... | collective-permute-start | bytes 393224 | tf_op jit(solution)/shard_map/ppermute | solution.py:118
  70.6 9.2 %collective-permute-start.30 = (bf16[64,1024]{1,0:T(8,128)(2,1)S(1)}, bf16[64,1024]{1,0:T(8,128)(2,1)S(1)}, u32[]{:S(2)}, u32[]{:S(2)}) collective-permute-start(bf16[64,1024]{1,0:T(8,128)(2,1)S(1)} %get-tuple-element.220), channel_id=1, source_target_pairs={{0,6},{1,7},{2,4},{3,5},{4,2},{5,3},{6,0},{7,1},{8,14},{9,15},{10,... | collective-permute-start | bytes 393224 | tf_op jit(solution)/shard_map/ppermute | solution.py:118
  72.1 7.7 %collective-permute-start.35 = (bf16[64,1024]{1,0:T(8,128)(2,1)S(1)}, bf16[64,1024]{1,0:T(8,128)(2,1)S(1)}, u32[]{:S(2)}, u32[]{:S(2)}) collective-permute-start(bf16[64,1024]{1,0:T(8,128)(2,1)S(1)} %get-tuple-element.241), channel_id=1, source_target_pairs={{0,1},{1,0},{2,3},{3,2},{4,5},{5,4},{6,7},{7,6},{8,9},{9,8},{10,11... | collective-permute-start | bytes 393224 | tf_op jit(solution)/shard_map/ppermute | solution.py:118
  79.9 8.0 %collective-permute-start.38 = (bf16[64,1024]{1,0:T(8,128)(2,1)S(1)}, bf16[64,1024]{1,0:T(8,128)(2,1)S(1)}, u32[]{:S(2)}, u32[]{:S(2)}) collective-permute-start(bf16[64,1024]{1,0:T(8,128)(2,1)S(1)} %get-tuple-element.247), channel_id=1, source_target_pairs={{0,4},{1,5},{2,6},{3,7},{4,0},{5,1},{6,2},{7,3},{8,12},{9,13},{10,... | collective-permute-start | bytes 393224 | tf_op jit(solution)/shard_map/ppermute | solution.py:118
  85.0 7.6 %collective-permute-start.41 = (bf16[64,1024]{1,0:T(8,128)(2,1)S(1)}, bf16[64,1024]{1,0:T(8,128)(2,1)S(1)}, u32[]{:S(2)}, u32[]{:S(2)}) collective-permute-start(bf16[64,1024]{1,0:T(8,128)(2,1)S(1)} %get-tuple-element.261), channel_id=1, source_target_pairs={{0,6},{1,7},{2,4},{3,5},{4,2},{5,3},{6,0},{7,1},{8,14},{9,15},{10,... | collective-permute-start | bytes 393224 | tf_op jit(solution)/shard_map/ppermute | solution.py:118
  96.7 8.6 %collective-permute-start.43 = (bf16[528,256]{1,0:T(8,128)(2,1)S(1)}, bf16[528,256]{1,0:T(8,128)(2,1)S(1)}, u32[]{:S(2)}, u32[]{:S(2)}) collective-permute-start(bf16[528,256]{1,0:T(8,128)(2,1)S(1)} %get-tuple-element.274), channel_id=1, source_target_pairs={{0,16},{8,24},{16,0},{24,8},{1,17},{9,25},{17,1},{25,9},{2,18},{10... | collective-permute-start | bytes 811016 | tf_op jit(solution)/shard_map/ppermute | solution.py:118
  98.2 8.9 %collective-permute-start.45 = (bf16[512,256]{1,0:T(8,128)(2,1)S(1)}, bf16[512,256]{1,0:T(8,128)(2,1)S(1)}, u32[]{:S(2)}, u32[]{:S(2)}) collective-permute-start(bf16[512,256]{1,0:T(8,128)(2,1)S(1)} %get-tuple-element.287), channel_id=1, source_target_pairs={{0,1},{1,0},{2,3},{3,2},{4,5},{5,4},{6,7},{7,6},{8,9},{9,8},{10,11... | collective-permute-start | bytes 786440 | tf_op jit(solution)/shard_map/ppermute | solution.py:118
  (39 other events, 225.4 us)

commit v7 on v6

--- a/solution.py
+++ b/solution.py
@@ -240,7 +240,7 @@
     norm_own, norm_rest = line.move(whole(*early) + rest, rest, name="pack_norm_x")
     norm_far = [norm_far, swap(norm_rest, "dp", far)]
     norm_core = swap(norm_own, "dp", 1)
-    block = 256 if hidden % 256 == 0 else hidden
+    block = hidden
 
     def forward(parts, pieces):
         rows = sum(x.shape[0] for x in parts)

time: 128 us -> 127 us (level)
  Pallas kernels: 35.9 us -> 34.1 us
    pallas_call x39, Pallas kernels: 35.9 us -> 34.1 us  [call(): pl.pallas_call(kernel, out_shape=[*outs, shape((8, LANES), F32)], in_spec...]
  transfers between devices with their start and end apart: 53 -> 53, of which waited for: 20 -> 19; matrix products, arithmetic and copies ran while one was open for 0% -> 0% of each run, Pallas kernels for 24% -> 22%
where the time goes in v7:
time: 127 us
  starting transfers between devices  51.1 us (40%)
  waiting for transfers between devices  38.5 us (30%)
  Pallas kernels  34.1 us (27%)
  local copies, waits for them, and re-layouts  2.45 us (2%)
    ppermute x53, starting transfers between devices, swap(): lax.ppermute(x, axis, [(i, i ^ mask) for i in range(lax.axis_size(axis))])  51.1 us
    ppermute x53, waiting for transfers between devices, swap(): lax.ppermute(x, axis, [(i, i ^ mask) for i in range(lax.axis_size(axis))])  38.5 us
    pallas_call x39, Pallas kernels, call(): pl.pallas_call(kernel, out_shape=[*outs, shape((8, LANES), F32)], in_spec...  34.1 us
  transfers between devices with their start and end apart: 53, of which 19 were waited for; matrix products, arithmetic and copies ran while one was open for 0% of the time, Pallas kernels for 22%

profile of v7, /device:TPU:0, one launch (start us, length us, event | category | flops | bytes accessed | tf_op | source)
XLA Modules:
  0.0 127.2 jit_solution(9124876715944381383)
XLA Ops:
  1.5 3.4 %head.1 = (bf16[128,1024]{1,0:T(8,128)(2,1)S(1)}, bf16[128,1024]{1,0:T(8,128)(2,1)}, s32[2,128]{1,0:T(2,128)S(1)}, bf16[128,1024]{1,0:T(8,128)(2,1)}, f32[128,1]...) custom-call(s32[2,128]{1,0:T(2,128)S(1)} %bitcast.31, ...), custom_call_target="tpu_custom_call" | custom-call | tf_op jit(solution)/shard_map/head/pallas_call | solution.py:66
  4.8 3.0 %collective-permute-start.1 = (bf16[128,1024]{1,0:T(8,128)(2,1)}, bf16[128,1024]{1,0:T(8,128)(2,1)S(1)}, u32[]{:S(2)}, u32[]{:S(2)}) collective-permute-start(bf16[128,1024]{1,0:T(8,128)(2,1)} %get-tuple-element.158), channel_id=1, source_target_pairs={{0,1},{1,0},{2,3},{3,2},{4,5},{5,4},{6,7},{7,6},{8,9},{9,8},{10,11... | collective-permute-start | bytes 786440 | tf_op jit(solution)/shard_map/ppermute | solution.py:118
  7.9 3.0 %collective-permute-start.2 = (bf16[64,1024]{1,0:T(8,128)(2,1)S(1)}, bf16[64,1024]{1,0:T(8,128)(2,1)S(1)}, u32[]{:S(2)}, u32[]{:S(2)}) collective-permute-start(bf16[64,1024]{1,0:T(8,128)(2,1)S(1)} %get-tuple-element.162), channel_id=1, source_target_pairs={{0,4},{1,5},{2,6},{3,7},{4,0},{5,1},{6,2},{7,3},{8,12},{9,13},{10,... | collective-permute-start | bytes 393224 | tf_op jit(solution)/shard_map/ppermute | solution.py:118
  12.5 3.3 %collective-permute-done.refs_1_ = bf16[32,1024]{1,0:T(8,128)(2,1)S(1)} collective-permute-done((bf16[32,1024]{1,0:T(8,128)(2,1)S(1)}, bf16[32,1024]{1,0:T(8,128)(2,1)S(1)}, u32[]{:S(2)}, u32[]{:S(2)}) %collective-permute-start) | collective-permute-done | bytes 65568 | tf_op jit(solution)/shard_map/ppermute | solution.py:118
  25.1 2.6 %collective-permute-start.9 = (bf16[64,1024]{1,0:T(8,128)(2,1)S(1)}, bf16[64,1024]{1,0:T(8,128)(2,1)S(1)}, u32[]{:S(2)}, u32[]{:S(2)}) collective-permute-start(bf16[64,1024]{1,0:T(8,128)(2,1)S(1)} %get-tuple-element.172), channel_id=1, source_target_pairs={{0,4},{1,5},{2,6},{3,7},{4,0},{5,1},{6,2},{7,3},{8,12},{9,13},{10,... | collective-permute-start | bytes 393224 | tf_op jit(solution)/shard_map/ppermute | solution.py:118
  30.3 2.4 %forward.4 = (bf16[256,1024]{1,0:T(8,128)(2,1)S(1)}, bf16[256,1024]{1,0:T(8,128)(2,1)S(1)}, bf16[256,1024]{1,0:T(8,128)(2,1)S(1)}, f32[256,1]{1,0:T(8,128)S(1)},...) custom-call(bf16[256,1024]{1,0:T(8,128)(2,1)S(1)} %get-tuple-element.168.refs_0_, bf16[8,1024]{1,0:T(8,128)(2,1)S(1)} %bitcast.25, ...), custom_call_target="tpu_custom_call" | custom-call | tf_op jit(solution)/shard_map/forward/pallas_call | solution.py:66
  32.8 3.9 %collective-permute-done.9.refs_1_ = bf16[64,1024]{1,0:T(8,128)(2,1)S(1)} collective-permute-done((bf16[64,1024]{1,0:T(8,128)(2,1)S(1)}, bf16[64,1024]{1,0:T(8,128)(2,1)S(1)}, u32[]{:S(2)}, u32[]{:S(2)}) %collective-permute-start.9) | collective-permute-done | bytes 131104 | tf_op jit(solution)/shard_map/ppermute | solution.py:118
  38.1 2.4 %forward.5 = (bf16[256,1024]{1,0:T(8,128)(2,1)S(1)}, bf16[256,1024]{1,0:T(8,128)(2,1)S(1)}, bf16[256,1024]{1,0:T(8,128)(2,1)S(1)}, f32[256,1]{1,0:T(8,128)S(1)},...) custom-call(bf16[256,1024]{1,0:T(8,128)(2,1)S(1)} %collective-permute-done.8.refs_0_, bf16[8,1024]{1,0:T(8,128)(2,1)S(1)} %bitcast.26, ...), custom_call_target="tpu_custom_call" | custom-call | tf_op jit(solution)/shard_map/forward/pallas_call | solution.py:66
  41.7 2.4 %forward.6 = (bf16[256,1024]{1,0:T(8,128)(2,1)S(1)}, bf16[256,1024]{1,0:T(8,128)(2,1)S(1)}, bf16[256,1024]{1,0:T(8,128)(2,1)S(1)}, f32[256,1]{1,0:T(8,128)S(1)},...) custom-call(bf16[256,1024]{1,0:T(8,128)(2,1)S(1)} %get-tuple-element.181.refs_0_, bf16[8,1024]{1,0:T(8,128)(2,1)S(1)} %bitcast.27, ...), custom_call_target="tpu_custom_call" | custom-call | tf_op jit(solution)/shard_map/forward/pallas_call | solution.py:66
  44.1 2.4 %forward.7 = (bf16[256,1024]{1,0:T(8,128)(2,1)S(1)}, bf16[256,1024]{1,0:T(8,128)(2,1)S(1)}, bf16[256,1024]{1,0:T(8,128)(2,1)S(1)}, f32[256,1]{1,0:T(8,128)S(1)},...) custom-call(bf16[64,1024]{1,0:T(8,128)(2,1)S(1)} %collective-permute, ...), custom_call_target="tpu_custom_call" | custom-call | tf_op jit(solution)/shard_map/forward/pallas_call | solution.py:66
  59.8 5.8 %collective-permute-done.22.refs_2_ = bf16[256,1024]{1,0:T(8,128)(2,1)S(1)} collective-permute-done((bf16[256,1024]{1,0:T(8,128)(2,1)S(1)}, bf16[256,1024]{1,0:T(8,128)(2,1)S(1)}, u32[]{:S(2)}, u32[]{:S(2)}) %collective-permute-start.22) | collective-permute-done | bytes 524320 | tf_op jit(solution)/shard_map/ppermute | solution.py:118
  66.7 3.1 %collective-permute-start.28 = (bf16[64,1024]{1,0:T(8,128)(2,1)S(1)}, bf16[64,1024]{1,0:T(8,128)(2,1)S(1)}, u32[]{:S(2)}, u32[]{:S(2)}) collective-permute-start(bf16[64,1024]{1,0:T(8,128)(2,1)S(1)} %get-tuple-element.218), channel_id=1, source_target_pairs={{0,4},{1,5},{2,6},{3,7},{4,0},{5,1},{6,2},{7,3},{8,12},{9,13},{10,... | collective-permute-start | bytes 393224 | tf_op jit(solution)/shard_map/ppermute | solution.py:118
  69.9 1.9 %collective-permute-start.30 = (bf16[64,1024]{1,0:T(8,128)(2,1)S(1)}, bf16[64,1024]{1,0:T(8,128)(2,1)S(1)}, u32[]{:S(2)}, u32[]{:S(2)}) collective-permute-start(bf16[64,1024]{1,0:T(8,128)(2,1)S(1)} %get-tuple-element.220), channel_id=1, source_target_pairs={{0,6},{1,7},{2,4},{3,5},{4,2},{5,3},{6,0},{7,1},{8,14},{9,15},{10,... | collective-permute-start | bytes 393224 | tf_op jit(solution)/shard_map/ppermute | solution.py:118
  73.5 3.6 %weights.2 = (bf16[1024,1024]{1,0:T(8,128)(2,1)}, f32[8,128]{1,0:T(8,128)S(1)}) custom-call(bf16[256,1024]{1,0:T(8,128)(2,1)S(1)} %get-tuple-element.226.refs_0_, bf16[256,1024]{1,0:T(8,128)(2,1)S(1)} %get-tuple-element.227.refs_1_, bf16[256,1024]{1,0:T(8,128)(2,1)S(1)} %get-tuple-element.228.refs_2_, bf16[256,1024]{1,0:T(8,128)(2,1)S(1)} %get-tuple-element.229.refs_3_, ...), custom_call_target="tpu_custom_call" | custom-call | tf_op jit(solution)/shard_map/weights/pallas_call | solution.py:66
  79.9 2.1 %collective-permute-start.38 = (bf16[64,1024]{1,0:T(8,128)(2,1)S(1)}, bf16[64,1024]{1,0:T(8,128)(2,1)S(1)}, u32[]{:S(2)}, u32[]{:S(2)}) collective-permute-start(bf16[64,1024]{1,0:T(8,128)(2,1)S(1)} %get-tuple-element.247), channel_id=1, source_target_pairs={{0,4},{1,5},{2,6},{3,7},{4,0},{5,1},{6,2},{7,3},{8,12},{9,13},{10,... | collective-permute-start | bytes 393224 | tf_op jit(solution)/shard_map/ppermute | solution.py:118
  84.3 3.0 %collective-permute-start.41 = (bf16[64,1024]{1,0:T(8,128)(2,1)S(1)}, bf16[64,1024]{1,0:T(8,128)(2,1)S(1)}, u32[]{:S(2)}, u32[]{:S(2)}) collective-permute-start(bf16[64,1024]{1,0:T(8,128)(2,1)S(1)} %get-tuple-element.261), channel_id=1, source_target_pairs={{0,6},{1,7},{2,4},{3,5},{4,2},{5,3},{6,0},{7,1},{8,14},{9,15},{10,... | collective-permute-start | bytes 393224 | tf_op jit(solution)/shard_map/ppermute | solution.py:118
  87.3 2.1 %collective-permute-done.38.refs_1_ = bf16[64,1024]{1,0:T(8,128)(2,1)S(1)} collective-permute-done((bf16[64,1024]{1,0:T(8,128)(2,1)S(1)}, bf16[64,1024]{1,0:T(8,128)(2,1)S(1)}, u32[]{:S(2)}, u32[]{:S(2)}) %collective-permute-start.38) | collective-permute-done | bytes 131104 | tf_op jit(solution)/shard_map/ppermute | solution.py:118
  98.7 3.8 %weights.3 = (bf16[1024,1024]{1,0:T(8,128)(2,1)}, f32[8,128]{1,0:T(8,128)S(1)}) custom-call(bf16[256,1024]{1,0:T(8,128)(2,1)S(1)} %get-tuple-element.275.refs_0_, bf16[256,1024]{1,0:T(8,128)(2,1)S(1)} %get-tuple-element.276.refs_1_, bf16[256,1024]{1,0:T(8,128)(2,1)S(1)} %get-tuple-element.277.refs_2_, bf16[256,1024]{1,0:T(8,128)(2,1)S(1)} %get-tuple-element.278.refs_3_, ...), custom_call_target="tpu_custom_call" | custom-call | tf_op jit(solution)/shard_map/weights/pallas_call | solution.py:66
  102.5 2.1 %collective-permute-done.43.refs_2_ = bf16[528,256]{1,0:T(8,128)(2,1)S(1)} collective-permute-done((bf16[528,256]{1,0:T(8,128)(2,1)S(1)}, bf16[528,256]{1,0:T(8,128)(2,1)S(1)}, u32[]{:S(2)}, u32[]{:S(2)}) %collective-permute-start.43) | collective-permute-done | bytes 270368 | tf_op jit(solution)/shard_map/ppermute | solution.py:118
  107.6 4.0 %collective-permute-done.46.refs_3_ = bf16[256,256]{1,0:T(8,128)(2,1)S(1)} collective-permute-done((bf16[256,256]{1,0:T(8,128)(2,1)S(1)}, bf16[256,256]{1,0:T(8,128)(2,1)S(1)}, u32[]{:S(2)}, u32[]{:S(2)}) %collective-permute-start.46) | collective-permute-done | bytes 131104 | tf_op jit(solution)/shard_map/ppermute | solution.py:118
  111.6 1.9 %collective-permute-start.47 = (bf16[144,256]{1,0:T(8,128)(2,1)S(1)}, bf16[144,256]{1,0:T(8,128)(2,1)S(1)}, u32[]{:S(2)}, u32[]{:S(2)}) collective-permute-start(bf16[144,256]{1,0:T(8,128)(2,1)S(1)} %get-tuple-element.293), channel_id=1, source_target_pairs={{0,4},{1,5},{2,6},{3,7},{4,0},{5,1},{6,2},{7,3},{8,12},{9,13},{10,... | collective-permute-start | bytes 221192 | tf_op jit(solution)/shard_map/ppermute | solution.py:118
  113.9 2.1 %collective-permute-start.49 = (bf16[144,256]{1,0:T(8,128)(2,1)S(1)}, bf16[144,256]{1,0:T(8,128)(2,1)S(1)}, u32[]{:S(2)}, u32[]{:S(2)}) collective-permute-start(bf16[144,256]{1,0:T(8,128)(2,1)S(1)} %get-tuple-element.295), channel_id=1, source_target_pairs={{0,6},{1,7},{2,4},{3,5},{4,2},{5,3},{6,0},{7,1},{8,14},{9,15},{10,... | collective-permute-start | bytes 221192 | tf_op jit(solution)/shard_map/ppermute | solution.py:118
  116.1 2.3 %collective-permute-done.47.refs_1_ = bf16[144,256]{1,0:T(8,128)(2,1)S(1)} collective-permute-done((bf16[144,256]{1,0:T(8,128)(2,1)S(1)}, bf16[144,256]{1,0:T(8,128)(2,1)S(1)}, u32[]{:S(2)}, u32[]{:S(2)}) %collective-permute-start.47) | collective-permute-done | bytes 73760 | tf_op jit(solution)/shard_map/ppermute | solution.py:118
  122.1 2.5 %collective-permute-done.52.refs_3_ = bf16[144,256]{1,0:T(8,128)(2,1)S(1)} collective-permute-done((bf16[144,256]{1,0:T(8,128)(2,1)S(1)}, bf16[144,256]{1,0:T(8,128)(2,1)S(1)}, u32[]{:S(2)}, u32[]{:S(2)}) %collective-permute-start.52) | collective-permute-done | bytes 73760 | tf_op jit(solution)/shard_map/ppermute | solution.py:118
  (141 shorter events, 57.1 us)
Async XLA Ops:
  4.8 11.0 %collective-permute-start.1 = (bf16[128,1024]{1,0:T(8,128)(2,1)}, bf16[128,1024]{1,0:T(8,128)(2,1)S(1)}, u32[]{:S(2)}, u32[]{:S(2)}) collective-permute-start(bf16[128,1024]{1,0:T(8,128)(2,1)} %get-tuple-element.158), channel_id=1, source_target_pairs={{0,1},{1,0},{2,3},{3,2},{4,5},{5,4},{6,7},{7,6},{8,9},{9,8},{10,11... | collective-permute-start | bytes 786440 | tf_op jit(solution)/shard_map/ppermute | solution.py:118
  7.9 7.9 %collective-permute-start = (bf16[32,1024]{1,0:T(8,128)(2,1)S(1)}, bf16[32,1024]{1,0:T(8,128)(2,1)S(1)}, u32[]{:S(2)}, u32[]{:S(2)}) collective-permute-start(bf16[32,1024]{1,0:T(8,128)(2,1)S(1)} %get-tuple-element.156), channel_id=1, source_target_pairs={{0,1},{1,0},{2,3},{3,2},{4,5},{5,4},{6,7},{7,6},{8,9},{9,8},{10,11... | collective-permute-start | bytes 196616 | tf_op jit(solution)/shard_map/ppermute | solution.py:118
  7.9 12.8 %collective-permute-start.2 = (bf16[64,1024]{1,0:T(8,128)(2,1)S(1)}, bf16[64,1024]{1,0:T(8,128)(2,1)S(1)}, u32[]{:S(2)}, u32[]{:S(2)}) collective-permute-start(bf16[64,1024]{1,0:T(8,128)(2,1)S(1)} %get-tuple-element.162), channel_id=1, source_target_pairs={{0,4},{1,5},{2,6},{3,7},{4,0},{5,1},{6,2},{7,3},{8,12},{9,13},{10,... | collective-permute-start | bytes 393224 | tf_op jit(solution)/shard_map/ppermute | solution.py:118
  11.0 9.8 %collective-permute-start.5 = (bf16[64,1024]{1,0:T(8,128)(2,1)S(1)}, bf16[64,1024]{1,0:T(8,128)(2,1)S(1)}, u32[]{:S(2)}, u32[]{:S(2)}) collective-permute-start(bf16[64,1024]{1,0:T(8,128)(2,1)S(1)} %get-tuple-element.163), channel_id=1, source_target_pairs={{0,2},{1,3},{2,0},{3,1},{4,6},{5,7},{6,4},{7,5},{8,10},{9,11},{10,... | collective-permute-start | bytes 393224 | tf_op jit(solution)/shard_map/ppermute | solution.py:118
  12.5 8.2 %collective-permute-start.6 = (bf16[64,1024]{1,0:T(8,128)(2,1)S(1)}, bf16[64,1024]{1,0:T(8,128)(2,1)S(1)}, u32[]{:S(2)}, u32[]{:S(2)}) collective-permute-start(bf16[64,1024]{1,0:T(8,128)(2,1)S(1)} %get-tuple-element.164), channel_id=1, source_target_pairs={{0,6},{1,7},{2,4},{3,5},{4,2},{5,3},{6,0},{7,1},{8,14},{9,15},{10,... | collective-permute-start | bytes 393224 | tf_op jit(solution)/shard_map/ppermute | solution.py:118
  25.1 11.6 %collective-permute-start.9 = (bf16[64,1024]{1,0:T(8,128)(2,1)S(1)}, bf16[64,1024]{1,0:T(8,128)(2,1)S(1)}, u32[]{:S(2)}, u32[]{:S(2)}) collective-permute-start(bf16[64,1024]{1,0:T(8,128)(2,1)S(1)} %get-tuple-element.172), channel_id=1, source_target_pairs={{0,4},{1,5},{2,6},{3,7},{4,0},{5,1},{6,2},{7,3},{8,12},{9,13},{10,... | collective-permute-start | bytes 393224 | tf_op jit(solution)/shard_map/ppermute | solution.py:118
  27.7 9.0 %collective-permute-start.10 = (bf16[64,1024]{1,0:T(8,128)(2,1)S(1)}, bf16[64,1024]{1,0:T(8,128)(2,1)S(1)}, u32[]{:S(2)}, u32[]{:S(2)}) collective-permute-start(bf16[64,1024]{1,0:T(8,128)(2,1)S(1)} %get-tuple-element.173), channel_id=1, source_target_pairs={{0,2},{1,3},{2,0},{3,1},{4,6},{5,7},{6,4},{7,5},{8,10},{9,11},{10,... | collective-permute-start | bytes 393224 | tf_op jit(solution)/shard_map/ppermute | solution.py:118
  29.5 10.9 %collective-permute-start.13 = (bf16[192,1024]{1,0:T(8,128)(2,1)S(1)}, bf16[192,1024]{1,0:T(8,128)(2,1)S(1)}, u32[]{:S(2)}, u32[]{:S(2)}) collective-permute-start(bf16[192,1024]{1,0:T(8,128)(2,1)S(1)} %get-tuple-element.179), channel_id=1, source_target_pairs={{0,16},{8,24},{16,0},{24,8},{1,17},{9,25},{17,1},{25,9},{2,18},{10... | collective-permute-start | bytes 1179656 | tf_op jit(solution)/shard_map/ppermute | solution.py:118
  30.3 7.7 %collective-permute-start.8 = (bf16[256,1024]{1,0:T(8,128)(2,1)S(1)}, bf16[256,1024]{1,0:T(8,128)(2,1)S(1)}, u32[]{:S(2)}, u32[]{:S(2)}) collective-permute-start(bf16[256,1024]{1,0:T(8,128)(2,1)S(1)} %get-tuple-element.168.refs_0_), channel_id=1, source_target_pairs={{0,8},{8,0},{16,24},{24,16},{1,9},{9,1},{17,25},{25,17},{2,10},{10... | collective-permute-start | bytes 1572872 | tf_op jit(solution)/shard_map/ppermute | solution.py:118
  36.7 13.1 %collective-permute-start.23 = (bf16[256,1024]{1,0:T(8,128)(2,1)S(1)}, bf16[256,1024]{1,0:T(8,128)(2,1)S(1)}, u32[]{:S(2)}, u32[]{:S(2)}) collective-permute-start(bf16[256,1024]{1,0:T(8,128)(2,1)S(1)} %get-tuple-element.193.refs_0_), channel_id=1, source_target_pairs={{0,16},{8,24},{16,0},{24,8},{1,17},{9,25},{17,1},{25,9},{2,18},{10... | collective-permute-start | bytes 1572872 | tf_op jit(solution)/shard_map/ppermute | solution.py:118
  50.5 9.3 %collective-permute-start.12 = (bf16[256,1024]{1,0:T(8,128)(2,1)S(1)}, bf16[256,1024]{1,0:T(8,128)(2,1)S(1)}, u32[]{:S(2)}, u32[]{:S(2)}) collective-permute-start(bf16[256,1024]{1,0:T(8,128)(2,1)S(1)} %get-tuple-element.177), channel_id=1, source_target_pairs={{0,8},{8,0},{16,24},{24,16},{1,9},{9,1},{17,25},{25,17},{2,10},{10... | collective-permute-start | bytes 1572872 | tf_op jit(solution)/shard_map/ppermute | solution.py:118
  50.9 14.8 %collective-permute-start.22 = (bf16[256,1024]{1,0:T(8,128)(2,1)S(1)}, bf16[256,1024]{1,0:T(8,128)(2,1)S(1)}, u32[]{:S(2)}, u32[]{:S(2)}) collective-permute-start(bf16[256,1024]{1,0:T(8,128)(2,1)S(1)} %get-tuple-element.198), channel_id=1, source_target_pairs={{0,16},{8,24},{16,0},{24,8},{1,17},{9,25},{17,1},{25,9},{2,18},{10... | collective-permute-start | bytes 1572872 | tf_op jit(solution)/shard_map/ppermute | solution.py:118
  56.8 13.1 %collective-permute-start.31 = (bf16[256,1024]{1,0:T(8,128)(2,1)S(1)}, bf16[256,1024]{1,0:T(8,128)(2,1)S(1)}, u32[]{:S(2)}, u32[]{:S(2)}) collective-permute-start(bf16[256,1024]{1,0:T(8,128)(2,1)S(1)} %get-tuple-element.222), channel_id=1, source_target_pairs={{0,8},{8,0},{16,24},{24,16},{1,9},{9,1},{17,25},{25,17},{2,10},{10... | collective-permute-start | bytes 1572872 | tf_op jit(solution)/shard_map/ppermute | solution.py:118
  57.3 8.6 %collective-permute-start.32 = (bf16[128,1024]{1,0:T(8,128)(2,1)S(1)}, bf16[128,1024]{1,0:T(8,128)(2,1)S(1)}, u32[]{:S(2)}, u32[]{:S(2)}) collective-permute-start(bf16[128,1024]{1,0:T(8,128)(2,1)S(1)} %get-tuple-element.223), channel_id=1, source_target_pairs={{0,8},{8,0},{16,24},{24,16},{1,9},{9,1},{17,25},{25,17},{2,10},{10... | collective-permute-start | bytes 786440 | tf_op jit(solution)/shard_map/ppermute | solution.py:118
  58.4 13.4 %collective-permute-start.34 = (bf16[128,1024]{1,0:T(8,128)(2,1)S(1)}, bf16[128,1024]{1,0:T(8,128)(2,1)S(1)}, u32[]{:S(2)}, u32[]{:S(2)}) collective-permute-start(bf16[128,1024]{1,0:T(8,128)(2,1)S(1)} %get-tuple-element.234), channel_id=1, source_target_pairs={{0,16},{8,24},{16,0},{24,8},{1,17},{9,25},{17,1},{25,9},{2,18},{10... | collective-permute-start | bytes 786440 | tf_op jit(solution)/shard_map/ppermute | solution.py:118
  65.9 11.2 %collective-permute-start.33 = (bf16[128,1024]{1,0:T(8,128)(2,1)S(1)}, bf16[128,1024]{1,0:T(8,128)(2,1)S(1)}, u32[]{:S(2)}, u32[]{:S(2)}) collective-permute-start(bf16[128,1024]{1,0:T(8,128)(2,1)S(1)} %get-tuple-element.225), channel_id=1, source_target_pairs={{0,16},{8,24},{16,0},{24,8},{1,17},{9,25},{17,1},{25,9},{2,18},{10... | collective-permute-start | bytes 786440 | tf_op jit(solution)/shard_map/ppermute | solution.py:118
  66.7 11.5 %collective-permute-start.28 = (bf16[64,1024]{1,0:T(8,128)(2,1)S(1)}, bf16[64,1024]{1,0:T(8,128)(2,1)S(1)}, u32[]{:S(2)}, u32[]{:S(2)}) collective-permute-start(bf16[64,1024]{1,0:T(8,128)(2,1)S(1)} %get-tuple-element.218), channel_id=1, source_target_pairs={{0,4},{1,5},{2,6},{3,7},{4,0},{5,1},{6,2},{7,3},{8,12},{9,13},{10,... | collective-permute-start | bytes 393224 | tf_op jit(solution)/shard_map/ppermute | solution.py:118
  69.8 8.4 %collective-permute-start.29 = (bf16[64,1024]{1,0:T(8,128)(2,1)S(1)}, bf16[64,1024]{1,0:T(8,128)(2,1)S(1)}, u32[]{:S(2)}, u32[]{:S(2)}) collective-permute-start(bf16[64,1024]{1,0:T(8,128)(2,1)S(1)} %get-tuple-element.219), channel_id=1, source_target_pairs={{0,2},{1,3},{2,0},{3,1},{4,6},{5,7},{6,4},{7,5},{8,10},{9,11},{10,... | collective-permute-start | bytes 393224 | tf_op jit(solution)/shard_map/ppermute | solution.py:118
  69.9 9.9 %collective-permute-start.30 = (bf16[64,1024]{1,0:T(8,128)(2,1)S(1)}, bf16[64,1024]{1,0:T(8,128)(2,1)S(1)}, u32[]{:S(2)}, u32[]{:S(2)}) collective-permute-start(bf16[64,1024]{1,0:T(8,128)(2,1)S(1)} %get-tuple-element.220), channel_id=1, source_target_pairs={{0,6},{1,7},{2,4},{3,5},{4,2},{5,3},{6,0},{7,1},{8,14},{9,15},{10,... | collective-permute-start | bytes 393224 | tf_op jit(solution)/shard_map/ppermute | solution.py:118
  71.9 8.0 %collective-permute-start.35 = (bf16[64,1024]{1,0:T(8,128)(2,1)S(1)}, bf16[64,1024]{1,0:T(8,128)(2,1)S(1)}, u32[]{:S(2)}, u32[]{:S(2)}) collective-permute-start(bf16[64,1024]{1,0:T(8,128)(2,1)S(1)} %get-tuple-element.241), channel_id=1, source_target_pairs={{0,1},{1,0},{2,3},{3,2},{4,5},{5,4},{6,7},{7,6},{8,9},{9,8},{10,11... | collective-permute-start | bytes 393224 | tf_op jit(solution)/shard_map/ppermute | solution.py:118
  79.9 9.5 %collective-permute-start.38 = (bf16[64,1024]{1,0:T(8,128)(2,1)S(1)}, bf16[64,1024]{1,0:T(8,128)(2,1)S(1)}, u32[]{:S(2)}, u32[]{:S(2)}) collective-permute-start(bf16[64,1024]{1,0:T(8,128)(2,1)S(1)} %get-tuple-element.247), channel_id=1, source_target_pairs={{0,4},{1,5},{2,6},{3,7},{4,0},{5,1},{6,2},{7,3},{8,12},{9,13},{10,... | collective-permute-start | bytes 393224 | tf_op jit(solution)/shard_map/ppermute | solution.py:118
  84.3 7.7 %collective-permute-start.41 = (bf16[64,1024]{1,0:T(8,128)(2,1)S(1)}, bf16[64,1024]{1,0:T(8,128)(2,1)S(1)}, u32[]{:S(2)}, u32[]{:S(2)}) collective-permute-start(bf16[64,1024]{1,0:T(8,128)(2,1)S(1)} %get-tuple-element.261), channel_id=1, source_target_pairs={{0,6},{1,7},{2,4},{3,5},{4,2},{5,3},{6,0},{7,1},{8,14},{9,15},{10,... | collective-permute-start | bytes 393224 | tf_op jit(solution)/shard_map/ppermute | solution.py:118
  96.0 8.6 %collective-permute-start.43 = (bf16[528,256]{1,0:T(8,128)(2,1)S(1)}, bf16[528,256]{1,0:T(8,128)(2,1)S(1)}, u32[]{:S(2)}, u32[]{:S(2)}) collective-permute-start(bf16[528,256]{1,0:T(8,128)(2,1)S(1)} %get-tuple-element.274), channel_id=1, source_target_pairs={{0,16},{8,24},{16,0},{24,8},{1,17},{9,25},{17,1},{25,9},{2,18},{10... | collective-permute-start | bytes 811016 | tf_op jit(solution)/shard_map/ppermute | solution.py:118
  97.5 8.9 %collective-permute-start.45 = (bf16[512,256]{1,0:T(8,128)(2,1)S(1)}, bf16[512,256]{1,0:T(8,128)(2,1)S(1)}, u32[]{:S(2)}, u32[]{:S(2)}) collective-permute-start(bf16[512,256]{1,0:T(8,128)(2,1)S(1)} %get-tuple-element.287), channel_id=1, source_target_pairs={{0,1},{1,0},{2,3},{3,2},{4,5},{5,4},{6,7},{7,6},{8,9},{9,8},{10,11... | collective-permute-start | bytes 786440 | tf_op jit(solution)/shard_map/ppermute | solution.py:118
  (39 other events, 228.3 us)

commit v8 on v7

--- a/solution.py
+++ b/solution.py
@@ -249,7 +249,7 @@
         def body(*refs):
             ins = refs[: len(parts)]
             router_ref, in_ref, down_ref, rows_hbm, act_hbm, der_ref, gate_ref = refs[len(parts) : len(parts) + 7]
-            sums, (rows_ref, act_ref, total, sems) = refs[len(parts) + 7 : -4], refs[-4:]
+            sums, (rows_ref, act_ref, sems) = refs[len(parts) + 7 : -3], refs[-3:]
             at = 0
             for ref in ins:
                 rows_ref[at : at + ref.shape[0], :] = ref[...]
@@ -263,7 +263,7 @@
                 act_ref[:, at] = act
                 der_ref[:, at] = derivative.astype(BF)
                 term = mm(act, down_ref[at, :])
-                total[...] = term if j == 0 else total[...] + term
+                total = term if j == 0 else total + term
             stores[1].start()
             for i in range(pieces):
                 sums[i][...] = total[i * piece : (i + 1) * piece, :].astype(BF)
@@ -280,7 +280,7 @@
             + [shape((piece, width))] * pieces,
             (*parts, router_t, weight_in, weight_down),
             out_specs=[HBM] * 2 + [VMEM] * (2 + pieces),
-            scratch=[pltpu.VMEM((rows, width), BF), pltpu.VMEM((rows, hidden), BF), pltpu.VMEM((rows, width), F32), DMA((2,))],
+            scratch=[pltpu.VMEM((rows, width), BF), pltpu.VMEM((rows, hidden), BF), DMA((2,))],
             vmem=20 * MIB, name="forward")
         return (*results[:4], results[4:])
 
@@ -291,7 +291,7 @@
         def body(*refs):
             ins, refs = refs[: len(parts)], refs[len(parts) :]
             gate_ref, der_ref, in_ref, down_ref, grads_hbm, pre_hbm = refs[:6]
-            sums, (grads_ref, pre_ref, total, sems) = refs[6 : 6 + pieces], refs[6 + pieces :]
+            sums, (grads_ref, pre_ref, sems) = refs[6 : 6 + pieces], refs[6 + pieces :]
             first = 0
             for ref in ins:
                 at = slice(first, first + ref.shape[0])
@@ -305,7 +305,7 @@
                 pre = (act_grad * der_ref[:, at].astype(F32)).astype(BF)
                 pre_ref[:, at] = pre
                 term = mm(pre, in_ref[:, at], NT)
-                total[...] = term if j == 0 else total[...] + term
+                total = term if j == 0 else total + term
             stores[1].start()
             for i in range(pieces):
                 sums[i][...] = total[i * piece : (i + 1) * piece, :].astype(BF)
@@ -317,7 +317,7 @@
             [shape((rows, width)), shape((rows, hidden))] + [shape((piece, width))] * pieces,
             (*parts, gate, der, weight_in, weight_down),
             out_specs=[HBM] * 2 + [VMEM] * pieces,
-            scratch=[pltpu.VMEM((rows, width), BF), pltpu.VMEM((rows, hidden), BF), pltpu.VMEM((rows, width), F32), DMA((2,))],
+            scratch=[pltpu.VMEM((rows, width), BF), pltpu.VMEM((rows, hidden), BF), DMA((2,))],
             vmem=20 * MIB, name="backward")
         return grads, pre, sums
 

time: 127 us -> 127 us (level)
  no operation moved by 1% of the time
where the time goes in v8:
time: 127 us
  starting transfers between devices  51.1 us (40%)
  waiting for transfers between devices  38.5 us (30%)
  Pallas kernels  34.1 us (27%)
  local copies, waits for them, and re-layouts  2.45 us (2%)
    ppermute x53, starting transfers between devices, swap(): lax.ppermute(x, axis, [(i, i ^ mask) for i in range(lax.axis_size(axis))])  51.1 us
    ppermute x53, waiting for transfers between devices, swap(): lax.ppermute(x, axis, [(i, i ^ mask) for i in range(lax.axis_size(axis))])  38.5 us
    pallas_call x39, Pallas kernels, call(): pl.pallas_call(kernel, out_shape=[*outs, shape((8, LANES), F32)], in_spec...  34.1 us
  transfers between devices with their start and end apart: 53, of which 19 were waited for; matrix products, arithmetic and copies ran while one was open for 0% of the time, Pallas kernels for 22%

profile of v8, /device:TPU:0, one launch (start us, length us, event | category | flops | bytes accessed | tf_op | source)
XLA Modules:
  0.0 127.2 jit_solution(14434061675870106146)
XLA Ops:
  1.5 3.4 %head.1 = (bf16[128,1024]{1,0:T(8,128)(2,1)S(1)}, bf16[128,1024]{1,0:T(8,128)(2,1)}, s32[2,128]{1,0:T(2,128)S(1)}, bf16[128,1024]{1,0:T(8,128)(2,1)}, f32[128,1]...) custom-call(s32[2,128]{1,0:T(2,128)S(1)} %bitcast.31, ...), custom_call_target="tpu_custom_call" | custom-call | tf_op jit(solution)/shard_map/head/pallas_call | solution.py:66
  4.8 3.0 %collective-permute-start.1 = (bf16[128,1024]{1,0:T(8,128)(2,1)}, bf16[128,1024]{1,0:T(8,128)(2,1)S(1)}, u32[]{:S(2)}, u32[]{:S(2)}) collective-permute-start(bf16[128,1024]{1,0:T(8,128)(2,1)} %get-tuple-element.158), channel_id=1, source_target_pairs={{0,1},{1,0},{2,3},{3,2},{4,5},{5,4},{6,7},{7,6},{8,9},{9,8},{10,11... | collective-permute-start | bytes 786440 | tf_op jit(solution)/shard_map/ppermute | solution.py:118
  7.9 3.0 %collective-permute-start.2 = (bf16[64,1024]{1,0:T(8,128)(2,1)S(1)}, bf16[64,1024]{1,0:T(8,128)(2,1)S(1)}, u32[]{:S(2)}, u32[]{:S(2)}) collective-permute-start(bf16[64,1024]{1,0:T(8,128)(2,1)S(1)} %get-tuple-element.162), channel_id=1, source_target_pairs={{0,4},{1,5},{2,6},{3,7},{4,0},{5,1},{6,2},{7,3},{8,12},{9,13},{10,... | collective-permute-start | bytes 393224 | tf_op jit(solution)/shard_map/ppermute | solution.py:118
  12.5 3.3 %collective-permute-done.refs_1_ = bf16[32,1024]{1,0:T(8,128)(2,1)S(1)} collective-permute-done((bf16[32,1024]{1,0:T(8,128)(2,1)S(1)}, bf16[32,1024]{1,0:T(8,128)(2,1)S(1)}, u32[]{:S(2)}, u32[]{:S(2)}) %collective-permute-start) | collective-permute-done | bytes 65568 | tf_op jit(solution)/shard_map/ppermute | solution.py:118
  25.1 2.6 %collective-permute-start.9 = (bf16[64,1024]{1,0:T(8,128)(2,1)S(1)}, bf16[64,1024]{1,0:T(8,128)(2,1)S(1)}, u32[]{:S(2)}, u32[]{:S(2)}) collective-permute-start(bf16[64,1024]{1,0:T(8,128)(2,1)S(1)} %get-tuple-element.172), channel_id=1, source_target_pairs={{0,4},{1,5},{2,6},{3,7},{4,0},{5,1},{6,2},{7,3},{8,12},{9,13},{10,... | collective-permute-start | bytes 393224 | tf_op jit(solution)/shard_map/ppermute | solution.py:118
  30.3 2.4 %forward.4 = (bf16[256,1024]{1,0:T(8,128)(2,1)S(1)}, bf16[256,1024]{1,0:T(8,128)(2,1)S(1)}, bf16[256,1024]{1,0:T(8,128)(2,1)S(1)}, f32[256,1]{1,0:T(8,128)S(1)},...) custom-call(bf16[256,1024]{1,0:T(8,128)(2,1)S(1)} %get-tuple-element.168.refs_0_, bf16[8,1024]{1,0:T(8,128)(2,1)S(1)} %bitcast.25, ...), custom_call_target="tpu_custom_call" | custom-call | tf_op jit(solution)/shard_map/forward/pallas_call | solution.py:66
  32.7 3.9 %collective-permute-done.9.refs_1_ = bf16[64,1024]{1,0:T(8,128)(2,1)S(1)} collective-permute-done((bf16[64,1024]{1,0:T(8,128)(2,1)S(1)}, bf16[64,1024]{1,0:T(8,128)(2,1)S(1)}, u32[]{:S(2)}, u32[]{:S(2)}) %collective-permute-start.9) | collective-permute-done | bytes 131104 | tf_op jit(solution)/shard_map/ppermute | solution.py:118
  38.1 2.4 %forward.5 = (bf16[256,1024]{1,0:T(8,128)(2,1)S(1)}, bf16[256,1024]{1,0:T(8,128)(2,1)S(1)}, bf16[256,1024]{1,0:T(8,128)(2,1)S(1)}, f32[256,1]{1,0:T(8,128)S(1)},...) custom-call(bf16[256,1024]{1,0:T(8,128)(2,1)S(1)} %collective-permute-done.8.refs_0_, bf16[8,1024]{1,0:T(8,128)(2,1)S(1)} %bitcast.26, ...), custom_call_target="tpu_custom_call" | custom-call | tf_op jit(solution)/shard_map/forward/pallas_call | solution.py:66
  41.6 2.4 %forward.6 = (bf16[256,1024]{1,0:T(8,128)(2,1)S(1)}, bf16[256,1024]{1,0:T(8,128)(2,1)S(1)}, bf16[256,1024]{1,0:T(8,128)(2,1)S(1)}, f32[256,1]{1,0:T(8,128)S(1)},...) custom-call(bf16[256,1024]{1,0:T(8,128)(2,1)S(1)} %get-tuple-element.181.refs_0_, bf16[8,1024]{1,0:T(8,128)(2,1)S(1)} %bitcast.27, ...), custom_call_target="tpu_custom_call" | custom-call | tf_op jit(solution)/shard_map/forward/pallas_call | solution.py:66
  44.1 2.4 %forward.7 = (bf16[256,1024]{1,0:T(8,128)(2,1)S(1)}, bf16[256,1024]{1,0:T(8,128)(2,1)S(1)}, bf16[256,1024]{1,0:T(8,128)(2,1)S(1)}, f32[256,1]{1,0:T(8,128)S(1)},...) custom-call(bf16[64,1024]{1,0:T(8,128)(2,1)S(1)} %collective-permute, ...), custom_call_target="tpu_custom_call" | custom-call | tf_op jit(solution)/shard_map/forward/pallas_call | solution.py:66
  59.8 5.8 %collective-permute-done.22.refs_2_ = bf16[256,1024]{1,0:T(8,128)(2,1)S(1)} collective-permute-done((bf16[256,1024]{1,0:T(8,128)(2,1)S(1)}, bf16[256,1024]{1,0:T(8,128)(2,1)S(1)}, u32[]{:S(2)}, u32[]{:S(2)}) %collective-permute-start.22) | collective-permute-done | bytes 524320 | tf_op jit(solution)/shard_map/ppermute | solution.py:118
  66.7 3.1 %collective-permute-start.28 = (bf16[64,1024]{1,0:T(8,128)(2,1)S(1)}, bf16[64,1024]{1,0:T(8,128)(2,1)S(1)}, u32[]{:S(2)}, u32[]{:S(2)}) collective-permute-start(bf16[64,1024]{1,0:T(8,128)(2,1)S(1)} %get-tuple-element.218), channel_id=1, source_target_pairs={{0,4},{1,5},{2,6},{3,7},{4,0},{5,1},{6,2},{7,3},{8,12},{9,13},{10,... | collective-permute-start | bytes 393224 | tf_op jit(solution)/shard_map/ppermute | solution.py:118
  69.9 1.9 %collective-permute-start.30 = (bf16[64,1024]{1,0:T(8,128)(2,1)S(1)}, bf16[64,1024]{1,0:T(8,128)(2,1)S(1)}, u32[]{:S(2)}, u32[]{:S(2)}) collective-permute-start(bf16[64,1024]{1,0:T(8,128)(2,1)S(1)} %get-tuple-element.220), channel_id=1, source_target_pairs={{0,6},{1,7},{2,4},{3,5},{4,2},{5,3},{6,0},{7,1},{8,14},{9,15},{10,... | collective-permute-start | bytes 393224 | tf_op jit(solution)/shard_map/ppermute | solution.py:118
  73.5 3.6 %weights.2 = (bf16[1024,1024]{1,0:T(8,128)(2,1)}, f32[8,128]{1,0:T(8,128)S(1)}) custom-call(bf16[256,1024]{1,0:T(8,128)(2,1)S(1)} %get-tuple-element.226.refs_0_, bf16[256,1024]{1,0:T(8,128)(2,1)S(1)} %get-tuple-element.227.refs_1_, bf16[256,1024]{1,0:T(8,128)(2,1)S(1)} %get-tuple-element.228.refs_2_, bf16[256,1024]{1,0:T(8,128)(2,1)S(1)} %get-tuple-element.229.refs_3_, ...), custom_call_target="tpu_custom_call" | custom-call | tf_op jit(solution)/shard_map/weights/pallas_call | solution.py:66
  79.9 2.1 %collective-permute-start.38 = (bf16[64,1024]{1,0:T(8,128)(2,1)S(1)}, bf16[64,1024]{1,0:T(8,128)(2,1)S(1)}, u32[]{:S(2)}, u32[]{:S(2)}) collective-permute-start(bf16[64,1024]{1,0:T(8,128)(2,1)S(1)} %get-tuple-element.247), channel_id=1, source_target_pairs={{0,4},{1,5},{2,6},{3,7},{4,0},{5,1},{6,2},{7,3},{8,12},{9,13},{10,... | collective-permute-start | bytes 393224 | tf_op jit(solution)/shard_map/ppermute | solution.py:118
  84.3 2.9 %collective-permute-start.41 = (bf16[64,1024]{1,0:T(8,128)(2,1)S(1)}, bf16[64,1024]{1,0:T(8,128)(2,1)S(1)}, u32[]{:S(2)}, u32[]{:S(2)}) collective-permute-start(bf16[64,1024]{1,0:T(8,128)(2,1)S(1)} %get-tuple-element.261), channel_id=1, source_target_pairs={{0,6},{1,7},{2,4},{3,5},{4,2},{5,3},{6,0},{7,1},{8,14},{9,15},{10,... | collective-permute-start | bytes 393224 | tf_op jit(solution)/shard_map/ppermute | solution.py:118
  87.3 2.2 %collective-permute-done.38.refs_1_ = bf16[64,1024]{1,0:T(8,128)(2,1)S(1)} collective-permute-done((bf16[64,1024]{1,0:T(8,128)(2,1)S(1)}, bf16[64,1024]{1,0:T(8,128)(2,1)S(1)}, u32[]{:S(2)}, u32[]{:S(2)}) %collective-permute-start.38) | collective-permute-done | bytes 131104 | tf_op jit(solution)/shard_map/ppermute | solution.py:118
  98.7 3.8 %weights.3 = (bf16[1024,1024]{1,0:T(8,128)(2,1)}, f32[8,128]{1,0:T(8,128)S(1)}) custom-call(bf16[256,1024]{1,0:T(8,128)(2,1)S(1)} %get-tuple-element.275.refs_0_, bf16[256,1024]{1,0:T(8,128)(2,1)S(1)} %get-tuple-element.276.refs_1_, bf16[256,1024]{1,0:T(8,128)(2,1)S(1)} %get-tuple-element.277.refs_2_, bf16[256,1024]{1,0:T(8,128)(2,1)S(1)} %get-tuple-element.278.refs_3_, ...), custom_call_target="tpu_custom_call" | custom-call | tf_op jit(solution)/shard_map/weights/pallas_call | solution.py:66
  102.5 2.1 %collective-permute-done.43.refs_2_ = bf16[528,256]{1,0:T(8,128)(2,1)S(1)} collective-permute-done((bf16[528,256]{1,0:T(8,128)(2,1)S(1)}, bf16[528,256]{1,0:T(8,128)(2,1)S(1)}, u32[]{:S(2)}, u32[]{:S(2)}) %collective-permute-start.43) | collective-permute-done | bytes 270368 | tf_op jit(solution)/shard_map/ppermute | solution.py:118
  107.5 4.0 %collective-permute-done.46.refs_3_ = bf16[256,256]{1,0:T(8,128)(2,1)S(1)} collective-permute-done((bf16[256,256]{1,0:T(8,128)(2,1)S(1)}, bf16[256,256]{1,0:T(8,128)(2,1)S(1)}, u32[]{:S(2)}, u32[]{:S(2)}) %collective-permute-start.46) | collective-permute-done | bytes 131104 | tf_op jit(solution)/shard_map/ppermute | solution.py:118
  111.6 1.9 %collective-permute-start.47 = (bf16[144,256]{1,0:T(8,128)(2,1)S(1)}, bf16[144,256]{1,0:T(8,128)(2,1)S(1)}, u32[]{:S(2)}, u32[]{:S(2)}) collective-permute-start(bf16[144,256]{1,0:T(8,128)(2,1)S(1)} %get-tuple-element.293), channel_id=1, source_target_pairs={{0,4},{1,5},{2,6},{3,7},{4,0},{5,1},{6,2},{7,3},{8,12},{9,13},{10,... | collective-permute-start | bytes 221192 | tf_op jit(solution)/shard_map/ppermute | solution.py:118
  113.9 2.2 %collective-permute-start.49 = (bf16[144,256]{1,0:T(8,128)(2,1)S(1)}, bf16[144,256]{1,0:T(8,128)(2,1)S(1)}, u32[]{:S(2)}, u32[]{:S(2)}) collective-permute-start(bf16[144,256]{1,0:T(8,128)(2,1)S(1)} %get-tuple-element.295), channel_id=1, source_target_pairs={{0,6},{1,7},{2,4},{3,5},{4,2},{5,3},{6,0},{7,1},{8,14},{9,15},{10,... | collective-permute-start | bytes 221192 | tf_op jit(solution)/shard_map/ppermute | solution.py:118
  116.1 2.3 %collective-permute-done.47.refs_1_ = bf16[144,256]{1,0:T(8,128)(2,1)S(1)} collective-permute-done((bf16[144,256]{1,0:T(8,128)(2,1)S(1)}, bf16[144,256]{1,0:T(8,128)(2,1)S(1)}, u32[]{:S(2)}, u32[]{:S(2)}) %collective-permute-start.47) | collective-permute-done | bytes 73760 | tf_op jit(solution)/shard_map/ppermute | solution.py:118
  122.1 2.5 %collective-permute-done.52.refs_3_ = bf16[144,256]{1,0:T(8,128)(2,1)S(1)} collective-permute-done((bf16[144,256]{1,0:T(8,128)(2,1)S(1)}, bf16[144,256]{1,0:T(8,128)(2,1)S(1)}, u32[]{:S(2)}, u32[]{:S(2)}) %collective-permute-start.52) | collective-permute-done | bytes 73760 | tf_op jit(solution)/shard_map/ppermute | solution.py:118
  (141 shorter events, 57.0 us)
Async XLA Ops:
  4.8 11.0 %collective-permute-start.1 = (bf16[128,1024]{1,0:T(8,128)(2,1)}, bf16[128,1024]{1,0:T(8,128)(2,1)S(1)}, u32[]{:S(2)}, u32[]{:S(2)}) collective-permute-start(bf16[128,1024]{1,0:T(8,128)(2,1)} %get-tuple-element.158), channel_id=1, source_target_pairs={{0,1},{1,0},{2,3},{3,2},{4,5},{5,4},{6,7},{7,6},{8,9},{9,8},{10,11... | collective-permute-start | bytes 786440 | tf_op jit(solution)/shard_map/ppermute | solution.py:118
  7.9 7.9 %collective-permute-start = (bf16[32,1024]{1,0:T(8,128)(2,1)S(1)}, bf16[32,1024]{1,0:T(8,128)(2,1)S(1)}, u32[]{:S(2)}, u32[]{:S(2)}) collective-permute-start(bf16[32,1024]{1,0:T(8,128)(2,1)S(1)} %get-tuple-element.156), channel_id=1, source_target_pairs={{0,1},{1,0},{2,3},{3,2},{4,5},{5,4},{6,7},{7,6},{8,9},{9,8},{10,11... | collective-permute-start | bytes 196616 | tf_op jit(solution)/shard_map/ppermute | solution.py:118
  7.9 12.8 %collective-permute-start.2 = (bf16[64,1024]{1,0:T(8,128)(2,1)S(1)}, bf16[64,1024]{1,0:T(8,128)(2,1)S(1)}, u32[]{:S(2)}, u32[]{:S(2)}) collective-permute-start(bf16[64,1024]{1,0:T(8,128)(2,1)S(1)} %get-tuple-element.162), channel_id=1, source_target_pairs={{0,4},{1,5},{2,6},{3,7},{4,0},{5,1},{6,2},{7,3},{8,12},{9,13},{10,... | collective-permute-start | bytes 393224 | tf_op jit(solution)/shard_map/ppermute | solution.py:118
  11.0 9.8 %collective-permute-start.5 = (bf16[64,1024]{1,0:T(8,128)(2,1)S(1)}, bf16[64,1024]{1,0:T(8,128)(2,1)S(1)}, u32[]{:S(2)}, u32[]{:S(2)}) collective-permute-start(bf16[64,1024]{1,0:T(8,128)(2,1)S(1)} %get-tuple-element.163), channel_id=1, source_target_pairs={{0,2},{1,3},{2,0},{3,1},{4,6},{5,7},{6,4},{7,5},{8,10},{9,11},{10,... | collective-permute-start | bytes 393224 | tf_op jit(solution)/shard_map/ppermute | solution.py:118
  12.5 8.2 %collective-permute-start.6 = (bf16[64,1024]{1,0:T(8,128)(2,1)S(1)}, bf16[64,1024]{1,0:T(8,128)(2,1)S(1)}, u32[]{:S(2)}, u32[]{:S(2)}) collective-permute-start(bf16[64,1024]{1,0:T(8,128)(2,1)S(1)} %get-tuple-element.164), channel_id=1, source_target_pairs={{0,6},{1,7},{2,4},{3,5},{4,2},{5,3},{6,0},{7,1},{8,14},{9,15},{10,... | collective-permute-start | bytes 393224 | tf_op jit(solution)/shard_map/ppermute | solution.py:118
  25.1 11.6 %collective-permute-start.9 = (bf16[64,1024]{1,0:T(8,128)(2,1)S(1)}, bf16[64,1024]{1,0:T(8,128)(2,1)S(1)}, u32[]{:S(2)}, u32[]{:S(2)}) collective-permute-start(bf16[64,1024]{1,0:T(8,128)(2,1)S(1)} %get-tuple-element.172), channel_id=1, source_target_pairs={{0,4},{1,5},{2,6},{3,7},{4,0},{5,1},{6,2},{7,3},{8,12},{9,13},{10,... | collective-permute-start | bytes 393224 | tf_op jit(solution)/shard_map/ppermute | solution.py:118
  27.7 9.0 %collective-permute-start.10 = (bf16[64,1024]{1,0:T(8,128)(2,1)S(1)}, bf16[64,1024]{1,0:T(8,128)(2,1)S(1)}, u32[]{:S(2)}, u32[]{:S(2)}) collective-permute-start(bf16[64,1024]{1,0:T(8,128)(2,1)S(1)} %get-tuple-element.173), channel_id=1, source_target_pairs={{0,2},{1,3},{2,0},{3,1},{4,6},{5,7},{6,4},{7,5},{8,10},{9,11},{10,... | collective-permute-start | bytes 393224 | tf_op jit(solution)/shard_map/ppermute | solution.py:118
  29.5 10.9 %collective-permute-start.13 = (bf16[192,1024]{1,0:T(8,128)(2,1)S(1)}, bf16[192,1024]{1,0:T(8,128)(2,1)S(1)}, u32[]{:S(2)}, u32[]{:S(2)}) collective-permute-start(bf16[192,1024]{1,0:T(8,128)(2,1)S(1)} %get-tuple-element.179), channel_id=1, source_target_pairs={{0,16},{8,24},{16,0},{24,8},{1,17},{9,25},{17,1},{25,9},{2,18},{10... | collective-permute-start | bytes 1179656 | tf_op jit(solution)/shard_map/ppermute | solution.py:118
  30.3 7.7 %collective-permute-start.8 = (bf16[256,1024]{1,0:T(8,128)(2,1)S(1)}, bf16[256,1024]{1,0:T(8,128)(2,1)S(1)}, u32[]{:S(2)}, u32[]{:S(2)}) collective-permute-start(bf16[256,1024]{1,0:T(8,128)(2,1)S(1)} %get-tuple-element.168.refs_0_), channel_id=1, source_target_pairs={{0,8},{8,0},{16,24},{24,16},{1,9},{9,1},{17,25},{25,17},{2,10},{10... | collective-permute-start | bytes 1572872 | tf_op jit(solution)/shard_map/ppermute | solution.py:118
  36.7 13.1 %collective-permute-start.23 = (bf16[256,1024]{1,0:T(8,128)(2,1)S(1)}, bf16[256,1024]{1,0:T(8,128)(2,1)S(1)}, u32[]{:S(2)}, u32[]{:S(2)}) collective-permute-start(bf16[256,1024]{1,0:T(8,128)(2,1)S(1)} %get-tuple-element.193.refs_0_), channel_id=1, source_target_pairs={{0,16},{8,24},{16,0},{24,8},{1,17},{9,25},{17,1},{25,9},{2,18},{10... | collective-permute-start | bytes 1572872 | tf_op jit(solution)/shard_map/ppermute | solution.py:118
  50.5 9.3 %collective-permute-start.12 = (bf16[256,1024]{1,0:T(8,128)(2,1)S(1)}, bf16[256,1024]{1,0:T(8,128)(2,1)S(1)}, u32[]{:S(2)}, u32[]{:S(2)}) collective-permute-start(bf16[256,1024]{1,0:T(8,128)(2,1)S(1)} %get-tuple-element.177), channel_id=1, source_target_pairs={{0,8},{8,0},{16,24},{24,16},{1,9},{9,1},{17,25},{25,17},{2,10},{10... | collective-permute-start | bytes 1572872 | tf_op jit(solution)/shard_map/ppermute | solution.py:118
  50.8 14.8 %collective-permute-start.22 = (bf16[256,1024]{1,0:T(8,128)(2,1)S(1)}, bf16[256,1024]{1,0:T(8,128)(2,1)S(1)}, u32[]{:S(2)}, u32[]{:S(2)}) collective-permute-start(bf16[256,1024]{1,0:T(8,128)(2,1)S(1)} %get-tuple-element.198), channel_id=1, source_target_pairs={{0,16},{8,24},{16,0},{24,8},{1,17},{9,25},{17,1},{25,9},{2,18},{10... | collective-permute-start | bytes 1572872 | tf_op jit(solution)/shard_map/ppermute | solution.py:118
  56.7 13.1 %collective-permute-start.31 = (bf16[256,1024]{1,0:T(8,128)(2,1)S(1)}, bf16[256,1024]{1,0:T(8,128)(2,1)S(1)}, u32[]{:S(2)}, u32[]{:S(2)}) collective-permute-start(bf16[256,1024]{1,0:T(8,128)(2,1)S(1)} %get-tuple-element.222), channel_id=1, source_target_pairs={{0,8},{8,0},{16,24},{24,16},{1,9},{9,1},{17,25},{25,17},{2,10},{10... | collective-permute-start | bytes 1572872 | tf_op jit(solution)/shard_map/ppermute | solution.py:118
  57.2 8.6 %collective-permute-start.32 = (bf16[128,1024]{1,0:T(8,128)(2,1)S(1)}, bf16[128,1024]{1,0:T(8,128)(2,1)S(1)}, u32[]{:S(2)}, u32[]{:S(2)}) collective-permute-start(bf16[128,1024]{1,0:T(8,128)(2,1)S(1)} %get-tuple-element.223), channel_id=1, source_target_pairs={{0,8},{8,0},{16,24},{24,16},{1,9},{9,1},{17,25},{25,17},{2,10},{10... | collective-permute-start | bytes 786440 | tf_op jit(solution)/shard_map/ppermute | solution.py:118
  58.3 13.5 %collective-permute-start.34 = (bf16[128,1024]{1,0:T(8,128)(2,1)S(1)}, bf16[128,1024]{1,0:T(8,128)(2,1)S(1)}, u32[]{:S(2)}, u32[]{:S(2)}) collective-permute-start(bf16[128,1024]{1,0:T(8,128)(2,1)S(1)} %get-tuple-element.234), channel_id=1, source_target_pairs={{0,16},{8,24},{16,0},{24,8},{1,17},{9,25},{17,1},{25,9},{2,18},{10... | collective-permute-start | bytes 786440 | tf_op jit(solution)/shard_map/ppermute | solution.py:118
  65.9 11.2 %collective-permute-start.33 = (bf16[128,1024]{1,0:T(8,128)(2,1)S(1)}, bf16[128,1024]{1,0:T(8,128)(2,1)S(1)}, u32[]{:S(2)}, u32[]{:S(2)}) collective-permute-start(bf16[128,1024]{1,0:T(8,128)(2,1)S(1)} %get-tuple-element.225), channel_id=1, source_target_pairs={{0,16},{8,24},{16,0},{24,8},{1,17},{9,25},{17,1},{25,9},{2,18},{10... | collective-permute-start | bytes 786440 | tf_op jit(solution)/shard_map/ppermute | solution.py:118
  66.7 11.5 %collective-permute-start.28 = (bf16[64,1024]{1,0:T(8,128)(2,1)S(1)}, bf16[64,1024]{1,0:T(8,128)(2,1)S(1)}, u32[]{:S(2)}, u32[]{:S(2)}) collective-permute-start(bf16[64,1024]{1,0:T(8,128)(2,1)S(1)} %get-tuple-element.218), channel_id=1, source_target_pairs={{0,4},{1,5},{2,6},{3,7},{4,0},{5,1},{6,2},{7,3},{8,12},{9,13},{10,... | collective-permute-start | bytes 393224 | tf_op jit(solution)/shard_map/ppermute | solution.py:118
  69.8 8.5 %collective-permute-start.29 = (bf16[64,1024]{1,0:T(8,128)(2,1)S(1)}, bf16[64,1024]{1,0:T(8,128)(2,1)S(1)}, u32[]{:S(2)}, u32[]{:S(2)}) collective-permute-start(bf16[64,1024]{1,0:T(8,128)(2,1)S(1)} %get-tuple-element.219), channel_id=1, source_target_pairs={{0,2},{1,3},{2,0},{3,1},{4,6},{5,7},{6,4},{7,5},{8,10},{9,11},{10,... | collective-permute-start | bytes 393224 | tf_op jit(solution)/shard_map/ppermute | solution.py:118
  69.9 10.0 %collective-permute-start.30 = (bf16[64,1024]{1,0:T(8,128)(2,1)S(1)}, bf16[64,1024]{1,0:T(8,128)(2,1)S(1)}, u32[]{:S(2)}, u32[]{:S(2)}) collective-permute-start(bf16[64,1024]{1,0:T(8,128)(2,1)S(1)} %get-tuple-element.220), channel_id=1, source_target_pairs={{0,6},{1,7},{2,4},{3,5},{4,2},{5,3},{6,0},{7,1},{8,14},{9,15},{10,... | collective-permute-start | bytes 393224 | tf_op jit(solution)/shard_map/ppermute | solution.py:118
  71.9 8.0 %collective-permute-start.35 = (bf16[64,1024]{1,0:T(8,128)(2,1)S(1)}, bf16[64,1024]{1,0:T(8,128)(2,1)S(1)}, u32[]{:S(2)}, u32[]{:S(2)}) collective-permute-start(bf16[64,1024]{1,0:T(8,128)(2,1)S(1)} %get-tuple-element.241), channel_id=1, source_target_pairs={{0,1},{1,0},{2,3},{3,2},{4,5},{5,4},{6,7},{7,6},{8,9},{9,8},{10,11... | collective-permute-start | bytes 393224 | tf_op jit(solution)/shard_map/ppermute | solution.py:118
  79.9 9.6 %collective-permute-start.38 = (bf16[64,1024]{1,0:T(8,128)(2,1)S(1)}, bf16[64,1024]{1,0:T(8,128)(2,1)S(1)}, u32[]{:S(2)}, u32[]{:S(2)}) collective-permute-start(bf16[64,1024]{1,0:T(8,128)(2,1)S(1)} %get-tuple-element.247), channel_id=1, source_target_pairs={{0,4},{1,5},{2,6},{3,7},{4,0},{5,1},{6,2},{7,3},{8,12},{9,13},{10,... | collective-permute-start | bytes 393224 | tf_op jit(solution)/shard_map/ppermute | solution.py:118
  84.3 7.6 %collective-permute-start.41 = (bf16[64,1024]{1,0:T(8,128)(2,1)S(1)}, bf16[64,1024]{1,0:T(8,128)(2,1)S(1)}, u32[]{:S(2)}, u32[]{:S(2)}) collective-permute-start(bf16[64,1024]{1,0:T(8,128)(2,1)S(1)} %get-tuple-element.261), channel_id=1, source_target_pairs={{0,6},{1,7},{2,4},{3,5},{4,2},{5,3},{6,0},{7,1},{8,14},{9,15},{10,... | collective-permute-start | bytes 393224 | tf_op jit(solution)/shard_map/ppermute | solution.py:118
  96.0 8.6 %collective-permute-start.43 = (bf16[528,256]{1,0:T(8,128)(2,1)S(1)}, bf16[528,256]{1,0:T(8,128)(2,1)S(1)}, u32[]{:S(2)}, u32[]{:S(2)}) collective-permute-start(bf16[528,256]{1,0:T(8,128)(2,1)S(1)} %get-tuple-element.274), channel_id=1, source_target_pairs={{0,16},{8,24},{16,0},{24,8},{1,17},{9,25},{17,1},{25,9},{2,18},{10... | collective-permute-start | bytes 811016 | tf_op jit(solution)/shard_map/ppermute | solution.py:118
  97.5 8.9 %collective-permute-start.45 = (bf16[512,256]{1,0:T(8,128)(2,1)S(1)}, bf16[512,256]{1,0:T(8,128)(2,1)S(1)}, u32[]{:S(2)}, u32[]{:S(2)}) collective-permute-start(bf16[512,256]{1,0:T(8,128)(2,1)S(1)} %get-tuple-element.287), channel_id=1, source_target_pairs={{0,1},{1,0},{2,3},{3,2},{4,5},{5,4},{6,7},{7,6},{8,9},{9,8},{10,11... | collective-permute-start | bytes 786440 | tf_op jit(solution)/shard_map/ppermute | solution.py:118
  (39 other events, 228.5 us)
